TPU v7x, 32 devices: a whole 2x2x4 slice. The times are simulated.
32 devices in a mesh: branch: 4 (over x, core), query: 8 (over z, y).
Axes of the slice: x: 2, y: 2, z: 4, core: 2. Of those that a mesh axis runs over, the one named last changes fastest.
Arguments:
- sensors: bfloat16 [3, 32, 2048], P(None, ('branch', 'query')), may hold values from -6 to 6
- branch_w: bfloat16 [3, 2048, 1024], replicated, may hold values from -0.125 to 0.125
- branch_b: float32 [3, 1024], replicated, may hold values from -3 to 3
- coords: bfloat16 [3, 16384], P(None, ('branch', 'query')), may hold values from -1 to 1
- func_index: int32 [16384], P(('branch', 'query')), may hold values from 0 to 7
- targets: float32 [16384], P(('branch', 'query')), may hold values from -6 to 6
- trunk_w1: bfloat16 [3, 1024], replicated, may hold values from -3.5 to 3.5
- trunk_b1: float32 [1024], replicated, may hold values from -3 to 3
- trunk_w2: bfloat16 [1024, 1024], replicated, may hold values from -0.1875 to 0.1875
- trunk_b2: float32 [1024], replicated, may hold values from -3 to 3
Outputs:
- grad_branch_w: float32 [3, 2048, 1024], P(None, 'query')
- grad_branch_b: float32 [3, 1024], replicated
- grad_trunk_w1: float32 [3, 1024], replicated
- grad_trunk_b1: float32 [1024], replicated
- grad_trunk_w2: float32 [1024, 1024], replicated
- grad_trunk_b2: float32 [1024], replicated
Inputs may be any that keep to these rules, and one draw needn't show every extreme that they name: func_index[i] names one of the 8 function samples whose rows of sensors stand in the same owner group (index of the mesh axis branch) as query point i.
All inputs are finite; a program needn't handle non-finite values.
Results may differ from a plain program's by a relative error of at most 0.018.
Values may be sent and summed in bfloat16 or wider, within the bound.
No kernel may reach another device: no remote copies, remote signals or barrier semaphores. Data moves between devices by JAX's collectives and lax.ppermute only.
A program may use at most 128 MiB of HBM per device.

v0:
```python
import jax
import jax.numpy as jnp
from jax import lax
from jax.sharding import PartitionSpec as P


def shards(
    sensors, branch_w, branch_b, coords, func_index, targets, trunk_w1, trunk_b1, trunk_w2, trunk_b2
):
    branches, func_dev, sensor_count = sensors.shape
    width = branch_w.shape[2]
    scale = width ** (-0.5)
    total_funcs = func_dev * lax.axis_size("branch") * lax.axis_size("query")
    pre = (
        jnp.einsum("kfs,ksl->kfl", sensors, branch_w, preferred_element_type=jnp.float32)
        + branch_b[:, None, :]
    )
    latent = jnp.tanh(pre).astype(jnp.bfloat16)
    lat_full = latent.astype(jnp.float32)
    every = lax.all_gather(latent, "query", axis=1, tiled=True).astype(jnp.float32)
    product = (every[0] * every[1] * every[2]).astype(jnp.bfloat16)
    group_funcs = product.shape[0]
    onehot = (func_index[:, None] == jnp.arange(group_funcs, dtype=jnp.int32)[None, :]).astype(
        jnp.bfloat16
    )
    first = lax.dot_general(
        coords, trunk_w1, (((0,), (0,)), ((), ())), preferred_element_type=jnp.float32
    )
    hidden = jnp.tanh(first + trunk_b1).astype(jnp.bfloat16)
    trunk_out = jnp.dot(hidden, trunk_w2, preferred_element_type=jnp.float32) + trunk_b2
    picked = jnp.dot(onehot, product, preferred_element_type=jnp.float32)
    pred = jnp.sum(picked * trunk_out, axis=1) * scale
    resid = (pred - targets) / total_funcs
    weighted = (resid[:, None] * trunk_out * scale).astype(jnp.bfloat16)
    dprod = lax.psum_scatter(
        lax.dot_general(
            onehot, weighted, (((0,), (0,)), ((), ())), preferred_element_type=jnp.float32
        ),
        "query",
        scatter_dimension=0,
        tiled=True,
    )
    grad_out = (resid[:, None] * picked * scale).astype(jnp.bfloat16)
    gw2 = lax.dot_general(
        hidden, grad_out, (((0,), (0,)), ((), ())), preferred_element_type=jnp.float32
    )
    gb2 = jnp.sum(grad_out.astype(jnp.float32), axis=0)
    grad_hidden = lax.dot_general(
        grad_out, trunk_w2, (((1,), (1,)), ((), ())), preferred_element_type=jnp.float32
    )
    hid_full = hidden.astype(jnp.float32)
    grad_pre = (grad_hidden * (1.0 - hid_full * hid_full)).astype(jnp.bfloat16)
    gw1 = lax.dot_general(
        coords, grad_pre, (((1,), (0,)), ((), ())), preferred_element_type=jnp.float32
    )
    gb1 = jnp.sum(grad_pre.astype(jnp.float32), axis=0)
    others = jnp.stack(
        [lat_full[1] * lat_full[2], lat_full[0] * lat_full[2], lat_full[0] * lat_full[1]]
    )
    delta = (dprod[None] * others * (1.0 - lat_full * lat_full)).astype(jnp.bfloat16)
    row_count = sensor_count // lax.axis_size("query")
    first_row = lax.axis_index("query") * row_count
    piece_sensors = lax.all_gather(sensors, ("branch", "query"), axis=1, tiled=True)
    piece_delta = lax.all_gather(delta, ("branch", "query"), axis=1, tiled=True)
    cut = lax.dynamic_slice_in_dim(piece_sensors, first_row, row_count, 2)
    grad_branch_w = jnp.einsum("kfs,kfl->ksl", cut, piece_delta, preferred_element_type=jnp.float32)
    gbb = jnp.sum(delta.astype(jnp.float32), axis=1)
    gbb, gw1, gb1, gw2, gb2 = lax.psum((gbb, gw1, gb1, gw2, gb2), ("branch", "query"))
    return (grad_branch_w, gbb, gw1, gb1, gw2, gb2)


def solution(mesh):
    placed = (
        P(None, ("branch", "query"), None),
        P(),
        P(),
        P(None, ("branch", "query")),
        P(("branch", "query")),
        P(("branch", "query")),
        P(),
        P(),
        P(),
        P(),
    )
    return jax.shard_map(
        shards,
        mesh=mesh,
        in_specs=placed,
        out_specs=(P(None, "query", None), P(), P(), P(), P(), P()),
        check_vma=False,
    )
```

profile of v0, /device:TPU:0, one launch (start us, length us, event | category | flops | bytes accessed | tf_op | source)
XLA Modules:
  0.0 283.9 jit_solution(10658825451934527237)
XLA Ops:
  7.2 0.0 copy-start
  7.2 0.0 all-reduce.4.cloned.1.call-start
  7.2 0.0 copy-start.4
  7.2 0.0 copy-start.7
  7.2 0.0 copy-start.9
  7.3 0.0 copy-start.10
  7.3 6.5 %fusion.10 = f32[3,1,1024]{2,1,0:T(1,128)S(1)} fusion(bf16[3,2048,1024]{2,1,0:T(8,128)(2,1)} %param.11, bf16[3,2048,1]{1,0,2:T(4,128)(2,1)} %bitcast.30), kind=kOutput, calls=%fused_computation.21 | convolution fusion | flops 12582912 | bytes 12607488 | tf_op jit(solution)/shard_map/kfs,ksl->kfl/dot_general | solution.py:15
  13.7 0.0 copy-done.4
  13.8 32.3 %all-gather = bf16[3,8192]{1,0:T(4,128)(2,1)S(1)} all-gather(bf16[3,1024]{1,0:T(4,128)(2,1)S(1)} %get-tuple-element.13), channel_id=2, replica_groups=mesh['branch'=4,'query'=8] {'query'}, dimensions={1}, use_global_device_ids=true | all-gather | bytes 55296 | tf_op jit(solution)/shard_map/all_gather | solution.py:20
  46.1 0.1 fusion.9
  46.2 0.0 copy-done.7
  46.2 0.0 copy-done.9
  46.2 0.0 copy-done.10
  46.2 0.5 tanh_convert_fusion
  46.8 0.0 copy-done
  46.8 0.0 copy-start.2
  46.8 0.0 copy-start.5
  46.8 0.0 copy-start.6
  46.8 1.3 fusion.19
  48.1 0.0 copy-done.5
  48.1 0.0 copy-done.6
  48.1 0.0 copy-start.1
  48.1 0.0 copy-start.8
  48.1 0.6 multiply_reduce_fusion
  48.7 0.7 copy-done.1
  49.4 0.0 copy-done.8
  49.4 0.3 convert_reduce_fusion
  49.7 0.0 copy-done.2
  49.7 3.3 %fusion.20 = f32[1024,1024]{1,0:T(8,128)} fusion(bf16[512,1024]{1,0:T(8,128)(2,1)S(1)} %tanh_convert_fusion, bf16[512,1024]{1,0:T(8,128)(2,1)S(1)} %get-tuple-element.11), kind=kOutput, calls=%fused_computation.38 | convolution fusion | flops 1073741824 | bytes 6291456 | tf_op jit(solution)/shard_map/dot_general | solution.py:44
  53.1 0.0 all-reduce.4.cloned.1.call-update
  53.1 0.0 copy-start.11
  53.1 2.1 fusion
  55.2 0.0 copy-done.11
  55.2 0.6 dynamic-slice
  55.8 37.6 %all-reduce = f32[8,1024]{1,0:T(8,128)S(1)} all-reduce(f32[8,1024]{1,0:T(8,128)S(1)} %fusion), channel_id=4, replica_groups=mesh['branch'=4,'query'=8] {'query'}, use_global_device_ids=true, to_apply=%region_1.0.clone | all-reduce | flops 8192 | bytes 65536
  93.4 0.7 constant_dynamic-slice_fusion
  94.1 0.0 copy-start.3
  94.1 2.6 convert_reduce_fusion.1
  96.7 0.2 convolution_bitcast_fusion
  97.0 38.1 %all-reduce.1 = (f32[3,1024]{1,0:T(4,128)}, f32[3,1024]{1,0:T(4,128)}, f32[1024]{0:T(1024)}, f32[1024]{0:T(1024)}) all-reduce(bf16[3,1024]{1,0:T(4,128)(2,1)S(1)} %fusion.13, f32[3,1024]{1,0:T(4,128)S(1)} %convolution_bitcast_fusion, f32[1024]{0:T(1024)S(1)} %get-tuple-element.19, ...), channel_id=1, replica_groups=mesh['branch'=4,'query'=8] {'branch','query'}, use_global_device_ids=true, to_apply=%region_2.0 | all-reduce | flops 8192 | bytes 59392 | tf_op jit(solution)/shard_map/psum | solution.py:68
  135.1 68.3 %all-gather.1 = bf16[3,32768]{1,0:T(4,128)(2,1)S(1)} all-gather(bf16[3,1024]{1,0:T(4,128)(2,1)S(1)} %fusion.13), channel_id=3, replica_groups=mesh['branch'=4,'query'=8] {'branch','query'}, dimensions={1}, use_global_device_ids=true | all-gather | bytes 202752 | tf_op jit(solution)/shard_map/all_gather | solution.py:64
  203.4 0.0 copy-done.3
  203.4 66.5 %all_gather.9 = bf16[3,32,2048]{2,0,1:T(4,128)(2,1)S(1)} all-gather(bf16[3,1,2048]{2,0,1:T(4,128)(2,1)S(1)} %copy-done.3), channel_id=1, replica_groups=mesh['branch'=4,'query'=8] {'branch','query'}, dimensions={1}, use_global_device_ids=true | all-gather | bytes 405504 | tf_op jit(solution)/shard_map/all_gather | solution.py:63
  270.0 2.3 fusion.2
  272.2 0.0 all-reduce.4.cloned.1.call-done
  272.2 4.8 %copy.33 = f32[1024,1024]{1,0:T(8,128)} copy(f32[1024,1024]{1,0:T(8,128)} %all-reduce.4.cloned.1.call-done) | data formatting | bytes 8388608
  (7 shorter events, 0.1 us)
Async XLA Ops:
  7.2 39.6 %copy-start = (bf16[1024,1024]{1,0:T(8,128)(2,1)S(1)}, bf16[1024,1024]{1,0:T(8,128)(2,1)}, u32[]{:S(2)}) copy-start(bf16[1024,1024]{1,0:T(8,128)(2,1)} %param.18) | copy-start | bytes 6291460
  7.2 265.1 %all-reduce.4.cloned.1.call-start = ((), (), s32[]{:S(2)}) async-start(), calls=%async_computation | async-start | bytes 8388608 | tf_op jit(solution)/shard_map/psum | solution.py:68
  7.2 6.5 %copy-start.4 = (f32[3,1024]{1,0:T(4,128)S(1)}, f32[3,1024]{1,0:T(4,128)}, u32[]{:S(2)}) copy-start(f32[3,1024]{1,0:T(4,128)} %param.12) | copy-start | bytes 36868
  7.2 39.0 %copy-start.7 = (bf16[3,512]{1,0:T(4,128)(2,1)S(1)}, bf16[3,512]{1,0:T(4,128)(2,1)}, u32[]{:S(2)}) copy-start(bf16[3,512]{1,0:T(4,128)(2,1)} %param.13) | copy-start | bytes 9220
  7.2 39.0 %copy-start.9 = (bf16[3,1024]{1,0:T(4,128)(2,1)S(1)}, bf16[3,1024]{1,0:T(4,128)(2,1)}, u32[]{:S(2)}) copy-start(bf16[3,1024]{1,0:T(4,128)(2,1)} %param.16) | copy-start | bytes 18436
  7.3 39.0 %copy-start.10 = (f32[1024]{0:T(1024)S(1)}, f32[1024]{0:T(1024)}, u32[]{:S(2)}) copy-start(f32[1024]{0:T(1024)} %param.17) | copy-start | bytes 12292
  46.8 3.0 %copy-start.2 = (bf16[512,1024]{1,0:T(8,128)(2,1)}, bf16[512,1024]{1,0:T(8,128)(2,1)S(1)}, u32[]{:S(2)}) copy-start(bf16[512,1024]{1,0:T(8,128)(2,1)S(1)} %tanh_convert_fusion) | copy-start | bytes 3145732
  46.8 1.3 copy-start.5
  46.8 1.3 copy-start.6
  48.1 1.3 copy-start.1
  48.1 1.3 copy-start.8
  53.1 2.1 copy-start.11
  94.1 109.3 %copy-start.3 = (bf16[3,1,2048]{2,0,1:T(4,128)(2,1)S(1)}, bf16[3,1,2048]{2,0,1:T(4,128)(2,1)}, u32[]{:S(2)}) copy-start(bf16[3,1,2048]{2,0,1:T(4,128)(2,1)} %param.10) | copy-start | bytes 36868
Sparse Core Ops, SparseCore 0:
  53.2 143.0 all-reduce.3
where the time goes:
time: 284 us
  blocking collectives  243 us (86%)
  matrix products  19.3 us (7%)
  between operations  14.3 us (5%)
  local copies, waits for them, and re-layouts  6.86 us (2%)
    all_gather x1, blocking collectives, shards(): piece_delta = lax.all_gather(delta, ('branch', 'query'), axis=1, tiled=True)  68.3 us
    all_gather x1, blocking collectives, shards(): lax.all_gather(sensors, ('branch', 'query'), axis=1, tiled=True)  66.5 us
    psum x1, blocking collectives, shards(): lax.psum((gbb, gw1, gb1, gw2, gb2), ('branch', 'query'))  38.1 us
    unnamed x1, blocking collectives  37.6 us
    all_gather x1, blocking collectives, shards(): lax.all_gather(latent, 'query', axis=1, tiled=True).astype(jnp.float32)  32.3 us
    unnamed x27, local copies, waits for them, and re-layouts  6.82 us
    dot_general x1, matrix products, shards(): jnp.einsum('kfs,ksl->kfl', sensors, branch_w, preferred_element_type=jnp....  6.45 us
  transfers between devices with their start and end apart: 1, of which 0 were waited for; matrix products, arithmetic and copies ran while one was open for 3% of the time, Pallas kernels for 0%

commit v1 on v0

v1 whole, which is shorter than its diff:
```python
import jax
import jax.numpy as jnp
from jax import lax
from jax.sharding import PartitionSpec as P

BF = jnp.bfloat16
F32 = jnp.float32


def pieces(value, count):
    out = []
    for _ in range(count):
        top = lax.reduce_precision(value, 8, 7)
        out.append(top.astype(BF))
        value = value - top
    return out


def dot(a, b, dims):
    return lax.dot_general(a, b, (dims, ((), ())), preferred_element_type=F32)


def shards(
    sensors, branch_w, branch_b, coords, func_index, targets, trunk_w1, trunk_b1, trunk_w2, trunk_b2
):
    branches, func_dev, sensor_count = sensors.shape
    dims, queries = coords.shape
    width = branch_w.shape[2]
    scale = width ** (-0.5)
    nb, nq = lax.axis_size("branch"), lax.axis_size("query")
    total_funcs = func_dev * nb * nq
    group_funcs = func_dev * nq

    parts = [sensors.reshape(-1, queries), coords, func_index.astype(BF)[None]]
    parts += [t[None] for t in pieces(targets, 3)]
    packed = jnp.concatenate(parts, axis=0)
    rows = packed.shape[0]
    packed = jnp.pad(packed, ((0, -rows % 8), (0, 0)))
    sent = jnp.broadcast_to(packed[None], (nq,) + packed.shape)
    got = lax.all_to_all(sent, "query", 0, 0, tiled=True)
    first = rows - dims - 4
    group_sensors = (
        got[:, :first]
        .reshape(nq, branches, func_dev, sensor_count)
        .transpose(1, 0, 2, 3)
        .reshape(branches, group_funcs, sensor_count)
    )
    tail = got[:, first:rows].transpose(1, 0, 2).reshape(dims + 4, nq * queries)
    q_coords = tail[:dims]
    q_index = tail[dims].astype(jnp.int32)
    q_target = tail[dims + 1].astype(F32) + tail[dims + 2].astype(F32) + tail[dims + 3].astype(F32)

    pre = (
        jnp.einsum("kfs,ksl->kfl", group_sensors, branch_w, preferred_element_type=F32)
        + branch_b[:, None, :]
    )
    latent = jnp.tanh(pre).astype(BF)
    lat = latent.astype(F32)
    product = (lat[0] * lat[1] * lat[2]).astype(BF)

    mixed = dot(product, trunk_w2, ((1,), (1,)))
    offset = jnp.sum(product.astype(F32) * trunk_b2, axis=1, keepdims=True)
    first = dot(trunk_w1, q_coords, ((0,), (0,)))
    hidden = jnp.tanh(first + trunk_b1[:, None]).astype(BF)
    hi, lo = pieces(mixed, 2)
    scores = dot(jnp.concatenate([hi, lo], 0), hidden, ((1,), (0,)))
    scores = scores[:group_funcs] + scores[group_funcs:] + offset
    owned = (q_index[None, :] == jnp.arange(group_funcs, dtype=jnp.int32)[:, None]).astype(F32)
    pred = jnp.sum(owned * scores, axis=0) * scale
    resid = (pred - q_target) / total_funcs
    coef = owned * (resid * scale)[None]
    weights = jnp.concatenate(pieces(coef, 2), 0)
    g = dot(weights, hidden, ((1,), (1,)))
    g = (g[:group_funcs] + g[group_funcs:]).astype(BF)
    r = jnp.sum(coef, axis=1)
    hid = hidden.astype(F32)
    slope = (1.0 - hid * hid).astype(BF)
    ones = jnp.concatenate([jnp.ones_like(q_coords[:1]), q_coords], 0).astype(F32)
    spread = (ones[:, None] * coef[None]).reshape((dims + 1) * group_funcs, -1)
    moments = dot(jnp.concatenate(pieces(spread, 2), 0), slope, ((1,), (1,)))
    moments = moments.reshape(2, dims + 1, group_funcs, -1).sum(0)
    first_grads = jnp.sum(moments * mixed[None], axis=1)

    begin = lax.axis_index("query") * (sensor_count // nq)
    cut = lax.dynamic_slice_in_dim(group_sensors, begin, sensor_count // nq, 2)

    def gather(x):
        index = [[(i, (i + k) % nb) for i in range(nb)] for k in range(1, nb)]
        return [x] + [lax.ppermute(x, "branch", pairs) for pairs in index]

    r_row = jnp.pad(jnp.concatenate(pieces(r, 2)), (0, width - 2 * group_funcs))
    late = jnp.concatenate([g, first_grads.astype(BF), r_row[None]], 0)
    early = jnp.concatenate([latent.reshape(-1, width), cut.reshape(-1, width)], 0)
    earlies, lates = gather(early), gather(late)
    lat_rows = branches * group_funcs
    latent = jnp.concatenate(
        [e[:lat_rows].reshape(branches, group_funcs, width) for e in earlies], 1
    )
    cut = jnp.concatenate([e[lat_rows:].reshape(cut.shape) for e in earlies], 1)
    g = jnp.concatenate([x[:group_funcs] for x in lates], 0)
    first_grads = sum(x[group_funcs : group_funcs + dims + 1].astype(F32) for x in lates)
    r_rows = jnp.stack([x[-1].astype(F32) for x in lates])
    r = (r_rows[:, :group_funcs] + r_rows[:, group_funcs : 2 * group_funcs]).reshape(-1)

    lat = latent.astype(F32)
    product = (lat[0] * lat[1] * lat[2]).astype(BF)
    gw2 = dot(g, product, ((0,), (0,)))
    gb2 = jnp.sum(r[:, None] * product.astype(F32), axis=0)
    dprod = dot(g, trunk_w2, ((1,), (0,))) + r[:, None] * trunk_b2
    others = jnp.stack([lat[1] * lat[2], lat[0] * lat[2], lat[0] * lat[1]])
    delta = (dprod[None] * others * (1.0 - lat * lat)).astype(BF)
    gbw = jnp.einsum("kfs,kfl->ksl", cut, delta, preferred_element_type=F32)
    gbb = jnp.sum(delta.astype(F32), axis=1)
    return (gbw, gbb, first_grads[1:], first_grads[0], gw2, gb2)


def solution(mesh):
    placed = (
        P(None, ("branch", "query"), None),
        P(),
        P(),
        P(None, ("branch", "query")),
        P(("branch", "query")),
        P(("branch", "query")),
        P(),
        P(),
        P(),
        P(),
    )
    return jax.shard_map(
        shards,
        mesh=mesh,
        in_specs=placed,
        out_specs=(P(None, "query", None), P(), P(), P(), P(), P()),
        check_vma=False,
    )
```

time: 284 us -> 48.8 us (0.17)
  blocking collectives: 243 us -> 0 us
  between operations: 14.3 us -> 0.89 us
  starting transfers between devices: 0.04 us -> 11.1 us
  waiting for transfers between devices: 0.02 us -> 10.5 us
  other arithmetic: 0.52 us -> 3.84 us
    all_gather x3 -> x0, blocking collectives: 167 us -> none  [the longest x1 68.3 us: shards(): piece_delta = lax.all_gather(delta, ('branch', 'query'), axis=1, tiled=True)]
    psum x1 -> x0, blocking collectives: 38.1 us -> none  [shards(): lax.psum((gbb, gw1, gb1, gw2, gb2), ('branch', 'query'))]
    unnamed x1 -> x0, blocking collectives: 37.6 us -> none
    all_to_all x0 -> x1, waiting for transfers between devices: none -> 7.95 us  [shards(): got = lax.all_to_all(sent, 'query', 0, 0, tiled=True)]
    all_to_all x0 -> x1, starting transfers between devices: none -> 7.28 us  [shards(): got = lax.all_to_all(sent, 'query', 0, 0, tiled=True)]
    unnamed x27 -> x8, local copies, waits for them, and re-layouts: 6.82 us -> 1.11 us
    ppermute x0 -> x6, starting transfers between devices: none -> 3.81 us  [gather(): return [x] + [lax.ppermute(x, 'branch', pairs) for pairs in index]]
  transfers between devices with their start and end apart: 1 -> 7, of which waited for: 0 -> 5; matrix products, arithmetic and copies ran while one was open for 3% -> 4% of each run, Pallas kernels for 0% -> 0%
where the time goes in v1:
time: 48.8 us; the launch traced here: 48.5 us
  matrix products  17.2 us (35%)
  starting transfers between devices  11.1 us (23%)
  waiting for transfers between devices  10.5 us (22%)
  local copies, waits for them, and re-layouts  4.95 us (10%)
  other arithmetic  3.84 us (8%)
  between operations  0.89 us (2%)
    dot_general x7, matrix products, dot(): return lax.dot_general(a, b, (dims, ((), ())), preferred_element_type=F32)  13.2 us
    all_to_all x1, waiting for transfers between devices, shards(): got = lax.all_to_all(sent, 'query', 0, 0, tiled=True)  7.95 us
    all_to_all x1, starting transfers between devices, shards(): got = lax.all_to_all(sent, 'query', 0, 0, tiled=True)  7.28 us
    ppermute x6, starting transfers between devices, gather(): return [x] + [lax.ppermute(x, 'branch', pairs) for pairs in index]  3.81 us
    ppermute x6, waiting for transfers between devices, gather(): return [x] + [lax.ppermute(x, 'branch', pairs) for pairs in index]  2.55 us
    dot_general x1, matrix products, shards(): gbw = jnp.einsum('kfs,kfl->ksl', cut, delta, preferred_element_type=F32)  2.27 us
    dot_general x1, matrix products, shards(): jnp.einsum('kfs,ksl->kfl', group_sensors, branch_w, preferred_element_typ...  1.74 us
    slice x2, local copies, waits for them, and re-layouts, shards(): return (gbw, gbb, first_grads[1:], first_grads[0], gw2, gb2)  1.21 us
  transfers between devices with their start and end apart: 7, of which 5 were waited for; matrix products, arithmetic and copies ran while one was open for 4% of the time, Pallas kernels for 0%

profile of v1, /device:TPU:0, one launch (start us, length us, event | category | flops | bytes accessed | tf_op | source)
XLA Modules:
  0.0 48.5 jit_solution(16996562746087755834)
XLA Ops:
  0.6 0.0 copy-start
  0.6 0.8 %fusion.47 = (bf16[512]{0:T(512)(128)(2,1)S(1)}, bf16[512]{0:T(512)(128)(2,1)S(1)}, bf16[512]{0:T(512)(128)(2,1)S(1)}) fusion(f32[512]{0:T(512)} %param.15), kind=kLoop, calls=%fused_computation.93 | loop fusion | flops 4096 | bytes 5120 | tf_op jit(solution)/shard_map/convert_element_type | solution.py:14
  1.5 0.7 %reshape.148 = bf16[12,512]{1,0:T(8,128)(2,1)S(1)} reshape(bf16[3,1,2048]{2,0,1:T(4,128)(2,1)} %param.10) | data formatting | bytes 24576 | tf_op jit(solution)/shard_map/reshape | solution.py:34
  2.3 0.7 %convert_element_type.149 = bf16[512]{0:T(512)(128)(2,1)S(1)} convert(s32[512]{0:T(512)} %param.14) | non-fusion elementwise | flops 512 | bytes 3072 | tf_op jit(solution)/shard_map/convert_element_type | solution.py:34
  2.9 0.7 %concatenate.33 = bf16[19,512]{1,0:T(8,128)(2,1)S(1)} concatenate(bf16[12,512]{1,0:T(8,128)(2,1)S(1)} %reshape.148, bf16[3,512]{1,0:T(4,128)(2,1)} %param.13, bf16[1,512]{1,0:T(2,128)(2,1)S(1)} %broadcast_in_dim.12, bf16[1,512]{1,0:T(2,128)(2,1)S(1)} %broadcast_in_dim.13, bf16[1,512]{1,0:T(2,128)(2,1)S(1)} %broadcast_in_dim.14, bf16[1,512]{1,0:T(2,128)(2,1)S(1)} %broadcast_in_dim.15), dimensions={0} | concatenate | bytes 38912 | tf_op jit(solution)/shard_map/concatenate | solution.py:36
  3.7 0.7 %broadcast_in_dim.16 = bf16[8,24,512]{2,1,0:T(8,128)(2,1)} broadcast(bf16[24,512]{1,0:T(8,128)(2,1)S(1)} %pad.9), dimensions={1,2} | broadcast | bytes 221184 | tf_op jit(solution)/shard_map/broadcast_in_dim | solution.py:39
  4.4 7.3 %all-to-all-start = ((bf16[8,24,512]{2,1,0:T(8,128)(2,1)}), bf16[8,24,512]{2,1,0:T(8,128)(2,1)S(1)}, u32[]{:S(2)}, u32[]{:S(2)}) async-start(bf16[8,24,512]{2,1,0:T(8,128)(2,1)} %broadcast_in_dim.16), calls=%async_computation | async-start | bytes 393216 | tf_op jit(solution)/shard_map/all_to_all | solution.py:40
  11.7 8.0 %all-to-all-done = bf16[8,24,512]{2,1,0:T(8,128)(2,1)S(1)} async-done(((bf16[8,24,512]{2,1,0:T(8,128)(2,1)}), bf16[8,24,512]{2,1,0:T(8,128)(2,1)S(1)}, u32[]{:S(2)}, u32[]{:S(2)}) %all-to-all-start) | async-done | bytes 196640 | tf_op jit(solution)/shard_map/all_to_all | solution.py:40
  19.8 0.1 reshape.149
  19.9 0.1 copy.18
  20.0 0.0 copy-start.1
  20.0 0.0 copy-start.2
  20.0 3.5 %tanh_convert_fusion = bf16[4096,1024]{1,0:T(8,128)(2,1)S(1)} fusion(bf16[3,4096]{1,0:T(4,128)(2,1)S(1)} %bitcast.56, bf16[3,1024]{1,0:T(4,128)(2,1)} %param.16, f32[1024]{0:T(1024)} %param.17), kind=kOutput, calls=%fused_computation.1 | convolution fusion | flops 33554432 | bytes 8423424 | tf_op jit(solution)/shard_map/dot_general | solution.py:20
  23.5 1.1 %copy-done.1 = bf16[3,2048,1024]{2,1,0:T(8,128)(2,1)S(1)} copy-done((bf16[3,2048,1024]{2,1,0:T(8,128)(2,1)S(1)}, bf16[3,2048,1024]{2,1,0:T(8,128)(2,1)}, u32[]{:S(2)}) %copy-start.1) | copy-done | bytes 12582936
  24.6 0.0 copy-done.2
  24.6 0.0 copy-start.3
  24.6 1.7 %fusion.61 = (f32[3,8,1024]{2,1,0:T(8,128)S(1)}, bf16[3,8,1024]{2,1,0:T(8,128)(2,1)S(1)}) fusion(f32[3,1024]{1,0:T(4,128)S(1)} %copy-done.2, bf16[3,2048,1024]{2,1,0:T(8,128)(2,1)S(1)} %copy-done.1, bf16[8,3,1,2048]{3,0,1,2:T(8,128)(2,1)S(1)} %copy.18), kind=kOutput, calls=%fused_computation.110 | convolution fusion | flops 100737024 | bytes 12840960 | tf_op jit(solution)/shard_map/kfs,ksl->kfl/dot_general | solution.py:54
  26.3 0.0 copy-done.3
  26.3 0.1 multiply_reduce_fusion.2
  26.5 0.0 copy-done
  26.5 0.6 %reduce-precision_convert_fusion.2 = (bf16[8,1024]{1,0:T(8,128)(2,1)S(1)}, bf16[8,1024]{1,0:T(8,128)(2,1)S(1)}, f32[8,1024]{1,0:T(8,128)S(1)}) fusion(bf16[8,1024]{1,0:T(8,128)(2,1)S(1)} %get-tuple-element.12, bf16[1024,1024]{1,0:T(8,128)(2,1)S(1)} %copy-done), kind=kOutput, calls=%fused_computation.58 | convolution fusion | flops 16818176 | bytes 2179072 | tf_op jit(solution)/shard_map/dot_general | solution.py:20
  27.1 2.3 %fusion.36 = f32[16,4096]{1,0:T(8,128)S(1)} fusion(bf16[4096,1024]{1,0:T(8,128)(2,1)S(1)} %tanh_convert_fusion, bf16[8,1024]{1,0:T(8,128)(2,1)S(1)} %get-tuple-element.24, bf16[8,1024]{1,0:T(8,128)(2,1)S(1)} %get-tuple-element.23), kind=kOutput, calls=%fused_computation.66 | convolution fusion | flops 134283264 | bytes 8683520 | tf_op jit(solution)/shard_map/dot_general | solution.py:20
  29.4 0.1 fusion.15
  29.5 0.1 reduce-precision_convert_fusion.1
  29.7 1.2 %fusion.16 = f32[16,1024]{1,0:T(8,128)S(1)} fusion(bf16[4096,1024]{1,0:T(8,128)(2,1)S(1)} %tanh_convert_fusion, bf16[8,4096]{1,0:T(8,128)(2,1)S(1)} %get-tuple-element.21, bf16[8,4096]{1,0:T(8,128)(2,1)S(1)} %get-tuple-element.19), kind=kOutput, calls=%fused_computation.28 | convolution fusion | flops 134479872 | bytes 8585216 | tf_op jit(solution)/shard_map/dot_general | solution.py:20
  30.9 0.1 fusion.48
  31.0 0.1 reduce-precision_convert_fusion
  31.1 2.4 %fusion = f32[64,1024]{1,0:T(8,128)S(1)} fusion(bf16[4096,1024]{1,0:T(8,128)(2,1)S(1)} %tanh_convert_fusion, bf16[32,4096]{1,0:T(8,128)(2,1)S(1)} %get-tuple-element.16, bf16[32,4096]{1,0:T(8,128)(2,1)S(1)} %get-tuple-element.15), kind=kOutput, calls=%fused_computation.2 | convolution fusion | flops 554696704 | bytes 9175040 | tf_op jit(solution)/shard_map/dot_general | solution.py:20
  33.6 0.1 collective-permute-start.3
  33.6 1.6 %collective-permute-start.4 = (bf16[13,1024]{1,0:T(8,128)(2,1)S(1)}, bf16[13,1024]{1,0:T(8,128)(2,1)S(1)}, u32[]{:S(2)}, u32[]{:S(2)}) collective-permute-start(bf16[13,1024]{1,0:T(8,128)(2,1)S(1)} %pad_maximum_fusion.2), channel_id=1, source_target_pairs={{0,16},{8,24},{16,0},{24,8},{1,17},{9,25},{17,1},{25,9},{2,18},{10... | collective-permute-start | bytes 79880 | tf_op jit(solution)/shard_map/ppermute | solution.py:89
  35.2 1.4 %collective-permute-start.5 = (bf16[13,1024]{1,0:T(8,128)(2,1)S(1)}, bf16[13,1024]{1,0:T(8,128)(2,1)S(1)}, u32[]{:S(2)}, u32[]{:S(2)}) collective-permute-start(bf16[13,1024]{1,0:T(8,128)(2,1)S(1)} %pad_maximum_fusion.2), channel_id=1, source_target_pairs={{0,24},{8,0},{16,8},{24,16},{1,25},{9,1},{17,9},{25,17},{2,26},{10... | collective-permute-start | bytes 79880 | tf_op jit(solution)/shard_map/ppermute | solution.py:89
  36.6 0.1 collective-permute-start.2
  36.7 0.7 %collective-permute-start.1 = (bf16[30,1024]{1,0:T(8,128)(2,1)S(1)}, bf16[30,1024]{1,0:T(8,128)(2,1)S(1)}, u32[]{:S(2)}, u32[]{:S(2)}) collective-permute-start(bf16[30,1024]{1,0:T(8,128)(2,1)S(1)} %pad_maximum_fusion), channel_id=1, source_target_pairs={{0,16},{8,24},{16,0},{24,8},{1,17},{9,25},{17,1},{25,9},{2,18},{10... | collective-permute-start | bytes 184328 | tf_op jit(solution)/shard_map/ppermute | solution.py:89
  37.4 0.0 collective-permute-done.3
  37.4 0.0 collective-permute-start
  37.4 0.2 collective-permute-done.4
  37.6 0.6 %collective-permute-done.5 = bf16[13,1024]{1,0:T(8,128)(2,1)S(1)} collective-permute-done((bf16[13,1024]{1,0:T(8,128)(2,1)S(1)}, bf16[13,1024]{1,0:T(8,128)(2,1)S(1)}, u32[]{:S(2)}, u32[]{:S(2)}) %collective-permute-start.5) | collective-permute-done | bytes 26656 | tf_op jit(solution)/shard_map/ppermute | solution.py:89
  38.2 0.1 convert_add_fusion.1
  38.3 0.1 mul.145
  38.4 0.5 convolution_add_fusion
  38.9 0.6 %slice.190 = f32[3,1024]{1,0:T(4,128)} slice(f32[4,1024]{1,0:T(4,128)S(1)} %convert_add_fusion), slice={[1:4], [0:1024]} | slice | bytes 24576 | tf_op jit(solution)/shard_map/slice | solution.py:114
  39.5 0.6 %slice.191 = f32[1,1024]{1,0:T(1,128)} slice(f32[4,1024]{1,0:T(4,128)S(1)} %convert_add_fusion), slice={[0:1], [0:1024]} | slice | bytes 8192 | tf_op jit(solution)/shard_map/slice | solution.py:114
  40.1 0.0 collective-permute-done.2
  40.1 1.6 %collective-permute-done.1 = bf16[30,1024]{1,0:T(8,128)(2,1)S(1)} collective-permute-done((bf16[30,1024]{1,0:T(8,128)(2,1)S(1)}, bf16[30,1024]{1,0:T(8,128)(2,1)S(1)}, u32[]{:S(2)}, u32[]{:S(2)}) %collective-permute-start.1) | collective-permute-done | bytes 61472 | tf_op jit(solution)/shard_map/ppermute | solution.py:89
  41.6 0.2 collective-permute-done
  41.9 0.7 %multiply_reduce_fusion = (f32[1024]{0:T(1024)}, bf16[32,1024]{1,0:T(8,128)(2,1)S(1)}, f32[1,32,1024]{2,1,0:T(8,128)S(1)}) fusion(f32[32]{0:T(128)S(1)} %mul.145, f32[3,32,1024]{2,1,0:T(8,128)S(1)} %maximum_convert_fusion), kind=kLoop, calls=%fused_computation.32 | loop fusion | flops 195584 | bytes 594048 | tf_op jit(solution)/shard_map/reduce_sum | solution.py:108
  42.6 2.7 %fusion.43 = f32[1024,1024]{1,0:T(8,128)} fusion(bf16[32,1024]{1,0:T(8,128)(2,1)S(1)} %get-tuple-element.7, bf16[8,1024]{1,0:T(8,128)(2,1)S(1)} %slice.177, bf16[8,1024]{1,0:T(8,128)(2,1)S(1)} %slice.176, bf16[8,1024]{1,0:T(8,128)(2,1)S(1)} %slice.175, bf16[8,1024]{1,0:T(8,128)(2,1)S(1)} %fusion.34), kind=kOutput, calls=%fused_computation.82 | convolution fusion | flops 67371008 | bytes 4325376 | tf_op jit(solution)/shard_map/dot_general | solution.py:20
  45.5 0.7 %convert_reduce_fusion = (f32[3,1024]{1,0:T(4,128)}, bf16[3,32,1024]{2,1,0:T(8,128)(2,1)S(1)}) fusion(bf16[3,8,1024]{2,1,0:T(8,128)(2,1)S(1)} %slice_bitcast_fusion.1, bf16[3,8,1024]{2,1,0:T(8,128)(2,1)S(1)} %slice_bitcast_fusion.2, bf16[3,8,1024]{2,1,0:T(8,128)(2,1)S(1)} %slice_bitcast_fusion.3, bf16[3,8,1024]{2,1,0:T(8,128)(2,1)S(1)} %get-tuple-element.31, ...), kind=kLoop, calls=%fused_computation.18 | loop fusion | flops 1668096 | bytes 929792 | tf_op jit(solution)/shard_map/reduce_sum | solution.py:113
  46.2 2.3 %fusion.24 = f32[3,256,1024]{2,1,0:T(8,128)} fusion(bf16[3,32,1024]{2,1,0:T(8,128)(2,1)S(1)} %get-tuple-element.10, bf16[3,8,256]{2,1,0:T(8,128)(2,1)S(1)} %reshape.155, bf16[3,8,256]{2,1,0:T(8,128)(2,1)S(1)} %reshape.154, bf16[3,8,256]{2,1,0:T(8,128)(2,1)S(1)} %reshape.153, bf16[3,8,256]{2,1,0:T(8,128)(2,1)S(1)} %get-tuple-element.17), kind=kOutput, calls=%fused_computation.49 | convolution fusion | flops 50528256 | bytes 3391488 | tf_op jit(solution)/shard_map/kfs,kfl->ksl/dot_general | solution.py:112
  (39 shorter events, 0.5 us)
Async XLA Ops:
  0.6 25.8 %copy-start = (bf16[1024,1024]{1,0:T(8,128)(2,1)S(1)}, bf16[1024,1024]{1,0:T(8,128)(2,1)}, u32[]{:S(2)}) copy-start(bf16[1024,1024]{1,0:T(8,128)(2,1)} %param.18) | copy-start | bytes 6291460
  4.4 15.2 %all-to-all-start = ((bf16[8,24,512]{2,1,0:T(8,128)(2,1)}), bf16[8,24,512]{2,1,0:T(8,128)(2,1)S(1)}, u32[]{:S(2)}, u32[]{:S(2)}) async-start(bf16[8,24,512]{2,1,0:T(8,128)(2,1)} %broadcast_in_dim.16), calls=%async_computation | async-start | bytes 393216 | tf_op jit(solution)/shard_map/all_to_all | solution.py:40
  20.0 4.6 %copy-start.1 = (bf16[3,2048,1024]{2,1,0:T(8,128)(2,1)S(1)}, bf16[3,2048,1024]{2,1,0:T(8,128)(2,1)}, u32[]{:S(2)}) copy-start(bf16[3,2048,1024]{2,1,0:T(8,128)(2,1)} %param.11) | copy-start | bytes 37748740
  20.0 4.6 %copy-start.2 = (f32[3,1024]{1,0:T(4,128)S(1)}, f32[3,1024]{1,0:T(4,128)}, u32[]{:S(2)}) copy-start(f32[3,1024]{1,0:T(4,128)} %param.12) | copy-start | bytes 36868
  24.6 1.7 %copy-start.3 = (f32[1024]{0:T(1024)S(1)}, f32[1024]{0:T(1024)}, u32[]{:S(2)}) copy-start(f32[1024]{0:T(1024)} %param.19) | copy-start | bytes 12292
  33.6 3.9 %collective-permute-start.3 = (bf16[13,1024]{1,0:T(8,128)(2,1)S(1)}, bf16[13,1024]{1,0:T(8,128)(2,1)S(1)}, u32[]{:S(2)}, u32[]{:S(2)}) collective-permute-start(bf16[13,1024]{1,0:T(8,128)(2,1)S(1)} %pad_maximum_fusion.2), channel_id=1, source_target_pairs={{0,8},{8,16},{16,24},{24,0},{1,9},{9,17},{17,25},{25,1},{2,10},{10... | collective-permute-start | bytes 79880 | tf_op jit(solution)/shard_map/ppermute | solution.py:89
  33.6 4.0 %collective-permute-start.4 = (bf16[13,1024]{1,0:T(8,128)(2,1)S(1)}, bf16[13,1024]{1,0:T(8,128)(2,1)S(1)}, u32[]{:S(2)}, u32[]{:S(2)}) collective-permute-start(bf16[13,1024]{1,0:T(8,128)(2,1)S(1)} %pad_maximum_fusion.2), channel_id=1, source_target_pairs={{0,16},{8,24},{16,0},{24,8},{1,17},{9,25},{17,1},{25,9},{2,18},{10... | collective-permute-start | bytes 79880 | tf_op jit(solution)/shard_map/ppermute | solution.py:89
  35.2 3.0 %collective-permute-start.5 = (bf16[13,1024]{1,0:T(8,128)(2,1)S(1)}, bf16[13,1024]{1,0:T(8,128)(2,1)S(1)}, u32[]{:S(2)}, u32[]{:S(2)}) collective-permute-start(bf16[13,1024]{1,0:T(8,128)(2,1)S(1)} %pad_maximum_fusion.2), channel_id=1, source_target_pairs={{0,24},{8,0},{16,8},{24,16},{1,25},{9,1},{17,9},{25,17},{2,26},{10... | collective-permute-start | bytes 79880 | tf_op jit(solution)/shard_map/ppermute | solution.py:89
  36.6 3.5 %collective-permute-start.2 = (bf16[30,1024]{1,0:T(8,128)(2,1)S(1)}, bf16[30,1024]{1,0:T(8,128)(2,1)S(1)}, u32[]{:S(2)}, u32[]{:S(2)}) collective-permute-start(bf16[30,1024]{1,0:T(8,128)(2,1)S(1)} %pad_maximum_fusion), channel_id=1, source_target_pairs={{0,24},{8,0},{16,8},{24,16},{1,25},{9,1},{17,9},{25,17},{2,26},{10... | collective-permute-start | bytes 184328 | tf_op jit(solution)/shard_map/ppermute | solution.py:89
  36.7 5.0 %collective-permute-start.1 = (bf16[30,1024]{1,0:T(8,128)(2,1)S(1)}, bf16[30,1024]{1,0:T(8,128)(2,1)S(1)}, u32[]{:S(2)}, u32[]{:S(2)}) collective-permute-start(bf16[30,1024]{1,0:T(8,128)(2,1)S(1)} %pad_maximum_fusion), channel_id=1, source_target_pairs={{0,16},{8,24},{16,0},{24,8},{1,17},{9,25},{17,1},{25,9},{2,18},{10... | collective-permute-start | bytes 184328 | tf_op jit(solution)/shard_map/ppermute | solution.py:89
  37.4 4.5 %collective-permute-start = (bf16[30,1024]{1,0:T(8,128)(2,1)S(1)}, bf16[30,1024]{1,0:T(8,128)(2,1)S(1)}, u32[]{:S(2)}, u32[]{:S(2)}) collective-permute-start(bf16[30,1024]{1,0:T(8,128)(2,1)S(1)} %pad_maximum_fusion), channel_id=1, source_target_pairs={{0,8},{8,16},{16,24},{24,0},{1,9},{9,17},{17,25},{25,1},{2,10},{10... | collective-permute-start | bytes 184328 | tf_op jit(solution)/shard_map/ppermute | solution.py:89

commit v2 on v0

v2 whole, which is shorter than its diff:
```python
import functools

import jax
import jax.numpy as jnp
from jax import lax
from jax.experimental import pallas as pl
from jax.experimental.pallas import tpu as pltpu
from jax.sharding import PartitionSpec as P

BF = jnp.bfloat16
F32 = jnp.float32
MIB = 1 << 20
VMEM = pl.BlockSpec(memory_space=pltpu.VMEM)
ANY = pl.BlockSpec(memory_space=pl.ANY)


def up(value, step):
    return -(-value // step) * step


def pieces(value, count):
    out = []
    for _ in range(count):
        top = value.astype(BF)
        out.append(top)
        value = value - top.astype(F32)
    return out


def dot(a, b, dims=((1,), (0,))):
    return lax.dot_general(a, b, (dims, ((), ())), preferred_element_type=F32)


def stack(rows, count):
    have = sum(r.shape[0] for r in rows)
    if have < count:
        rows = rows + [jnp.zeros((count - have, rows[0].shape[1]), rows[0].dtype)]
    return jnp.concatenate(rows, axis=0)


def pack_kernel(sensors_ref, coords_ref, index_ref, targets_ref, out_ref):
    peers, rows, q = out_ref.shape
    branches, sensor_count = sensors_ref.shape
    cut = sensor_count // peers
    s = sensors_ref[...].astype(F32)
    base = [s[k : k + 1, c : c + q] for k in range(branches) for c in range(0, sensor_count, q)]
    base += [coords_ref[...].astype(F32), index_ref[...].astype(F32)]
    base += [t.astype(F32) for t in pieces(targets_ref[...], 3)]
    have = sum(r.shape[0] for r in base)
    whole = have // 8 * 8
    both = jnp.concatenate(base, axis=0)
    top, rest = both[:whole], both[whole:]
    flat = up(branches * cut, q)
    for j in range(peers):
        line = [s[k : k + 1, j * cut : (j + 1) * cut] for k in range(branches)]
        if flat > branches * cut:
            line.append(jnp.zeros((1, flat - branches * cut), F32))
        line = jnp.concatenate(line, axis=1)
        tail = [rest] + [line[:, c : c + q] for c in range(0, flat, q)]
        out_ref[j] = jnp.concatenate([top, stack(tail, rows - whole)], axis=0).astype(BF)


def latent_kernel(cut_row, got_ref, w_ref, bias_ref, w2_ref, b2_ref, early_ref, mixed_ref, offset_ref):
    _, funcs, q = got_ref.shape
    branches, sensor_count, width = w_ref.shape
    per = sensor_count // q
    lats = []
    for k in range(branches):
        x = jnp.concatenate([got_ref[k * per + c] for c in range(per)], axis=1)
        pre = dot(x, w_ref[k]) + bias_ref[k : k + 1, :]
        lats.append(jnp.tanh(pre).astype(BF).astype(F32))
    product = (lats[0] * lats[1] * lats[2]).astype(BF)
    lines = [got_ref[cut_row + c].astype(F32) for c in range(up(branches * sensor_count // funcs, q) // q)]
    if len(lines) * q < width:
        lines.append(jnp.zeros((funcs, width - len(lines) * q), F32))
    early_ref[...] = jnp.concatenate(lats + [jnp.concatenate(lines, axis=1)], axis=0).astype(BF)
    mixed_ref[...] = dot(product, w2_ref[...], ((1,), (1,)))
    offset = jnp.sum(product.astype(F32) * b2_ref[...], axis=1, keepdims=True)
    offset_ref[...] = jnp.broadcast_to(offset, offset_ref.shape)


def trunk_kernel(
    row, dims, total_funcs, unroll,
    got_ref, mixed_ref, offset_ref, w1_ref, b1_ref, late_ref, h_ref, s_ref, g_ref, m_ref, r_ref,
):
    chunks, _, q = got_ref.shape
    funcs, width = mixed_ref.shape
    scale = width ** (-0.5)
    known = up(dims + 3, 8)
    first = stack([w1_ref[...].astype(F32)] + [b.astype(F32) for b in pieces(b1_ref[...], 3)], known)
    first = first.astype(BF)
    mixed = jnp.concatenate(pieces(mixed_ref[...], 2), axis=0)
    offset = offset_ref[:, 0:1]
    lane_of = lax.broadcasted_iota(jnp.int32, (funcs, q), 0).astype(F32)
    g_ref[...] = jnp.zeros_like(g_ref)
    m_ref[...] = jnp.zeros_like(m_ref)
    r_ref[...] = jnp.zeros_like(r_ref)

    def visit(j, slot):
        block = got_ref[j].astype(F32)
        xyz = block[row : row + dims]
        owner = block[row + dims : row + dims + 1]
        target = block[row + dims + 1 : row + dims + 2]
        target = target + block[row + dims + 2 : row + dims + 3]
        target = target + block[row + dims + 3 : row + dims + 4]
        a = stack([xyz, jnp.ones((3, q), F32)], known).T.astype(BF)
        h = jnp.tanh(dot(a, first)).astype(BF)
        h_ref[slot] = h
        hf = h.astype(F32)
        s_ref[slot] = (1.0 - hf * hf).astype(BF)
        scores = dot(mixed, h_ref[slot], ((1,), (1,)))
        scores = scores[:funcs] + scores[funcs:] + offset
        owned = (owner == lane_of).astype(F32)
        pred = jnp.sum(owned * scores, axis=0, keepdims=True) * scale
        resid = (pred - target) / total_funcs
        coef = owned * (resid * scale)
        g_ref[...] += dot(jnp.concatenate(pieces(coef, 2), axis=0), h_ref[slot])
        spread = jnp.concatenate([coef] + [coef * xyz[d : d + 1] for d in range(dims)], axis=0)
        m_ref[...] += dot(jnp.concatenate(pieces(spread, 2), axis=0), s_ref[slot])
        r_ref[...] += coef

    if chunks == unroll:
        for j in range(chunks):
            visit(j, j)
    else:
        def several(i, carry):
            for u in range(unroll):
                visit(i * unroll + u, u)
            return carry
        lax.fori_loop(0, chunks // unroll, several, 0)

    g = g_ref[:funcs] + g_ref[funcs:]
    r = jnp.broadcast_to(jnp.sum(r_ref[...], axis=1, keepdims=True), (funcs, late_ref.shape[1] - width))
    high, low = pieces(r, 2)
    lane = lax.broadcasted_iota(jnp.int32, r.shape, 1)
    r = jnp.where(lane < r.shape[1] // 2, high.astype(F32), low.astype(F32))
    half = (dims + 1) * funcs
    moments = m_ref[:half] + m_ref[half:]
    grads = [
        jnp.sum(moments[d * funcs : (d + 1) * funcs] * mixed_ref[...], axis=0, keepdims=True)
        for d in range(dims + 1)
    ]
    grads = jnp.concatenate(grads, axis=0)
    grads = jnp.concatenate([grads, jnp.zeros((dims + 1, r.shape[1]), F32)], axis=1)
    late_ref[...] = stack([jnp.concatenate([g, r], axis=1), grads], late_ref.shape[0]).astype(BF)


def tail_kernel(
    groups, funcs, dims, cut,
    *refs,
):
    earlies, lates = refs[:groups], refs[groups : 2 * groups]
    w2_ref, b2_ref, gbw_ref, gbb_ref, gw1_ref, gb1_ref, gw2_ref, gb2_ref, gbw_buf, gw2_buf, sems = refs[2 * groups :]
    width = w2_ref.shape[1]
    branches = gbw_ref.shape[0]
    early = [e[...].astype(F32) for e in earlies]
    late = [x[...].astype(F32) for x in lates]

    def rows(parts, first):
        return jnp.concatenate([p[first : first + funcs] for p in parts], axis=0)

    lat = [rows(early, k * funcs) for k in range(branches)]
    lines = rows(early, branches * funcs)
    product = (lat[0] * lat[1] * lat[2]).astype(BF)
    ends = rows(late, 0)
    g, r = ends[:, :width], ends[:, width:]
    r = r[:, :1] + r[:, r.shape[1] // 2 : r.shape[1] // 2 + 1]
    copies = []

    def send(buf, out, index):
        copy = pltpu.make_async_copy(buf, out, sems.at[index])
        copy.start()
        copies.append(copy)

    height = gw2_buf.shape[1]
    for c in range(gw2_buf.shape[0]):
        gw2_buf[c] = dot(g[:, c * height : (c + 1) * height].T.astype(BF), product)
        send(gw2_buf.at[c], gw2_ref.at[pl.ds(c * height, height)], c)
    dprod = dot(g.astype(BF), w2_ref[...]) + r * b2_ref[...]
    gbb = []
    for k in range(branches):
        others = [lat[j] for j in range(branches) if j != k]
        delta = (dprod * (others[0] * others[1]) * (1.0 - lat[k] * lat[k])).astype(BF)
        gbw_buf[k] = dot(lines[:, k * cut : (k + 1) * cut].T.astype(BF), delta)
        send(gbw_buf.at[k], gbw_ref.at[k], gw2_buf.shape[0] + k)
        gbb.append(jnp.sum(delta.astype(F32), axis=0, keepdims=True))
    gbb_ref[...] = jnp.concatenate(gbb, axis=0)
    grads = late[0][funcs : funcs + dims + 1, :width]
    for x in late[1:]:
        grads = grads + x[funcs : funcs + dims + 1, :width]
    gb1_ref[...] = grads[:1]
    gw1_ref[...] = grads[1:]
    gb2_ref[...] = jnp.sum(r * product.astype(F32), axis=0, keepdims=True)
    for copy in copies:
        copy.wait()


def shards(
    sensors, branch_w, branch_b, coords, func_index, targets, trunk_w1, trunk_b1, trunk_w2, trunk_b2
):
    branches, func_dev, sensor_count = sensors.shape
    dims, queries = coords.shape
    hidden, width = trunk_w2.shape
    nb, nq = lax.axis_size("branch"), lax.axis_size("query")
    assert func_dev == 1 and sensor_count % queries == 0 and hidden == width
    funcs = nq
    cut = sensor_count // nq
    row = branches * sensor_count // queries
    cut_row = row + dims + 4
    rows = up(cut_row + up(branches * cut, queries) // queries, 8)

    packed = pl.pallas_call(
        pack_kernel,
        out_shape=jax.ShapeDtypeStruct((nq, rows, queries), BF),
        in_specs=[VMEM] * 4,
        out_specs=VMEM,
        compiler_params=pltpu.CompilerParams(vmem_limit_bytes=8 * MIB),
        name="pack",
    )(sensors.reshape(branches, sensor_count), coords, func_index[None], targets[None])
    got = lax.all_to_all(packed, "query", 0, 0, tiled=True)

    early, mixed, offset = pl.pallas_call(
        functools.partial(latent_kernel, cut_row),
        out_shape=(
            jax.ShapeDtypeStruct(((branches + 1) * funcs, width), BF),
            jax.ShapeDtypeStruct((funcs, hidden), F32),
            jax.ShapeDtypeStruct((funcs, 128), F32),
        ),
        in_specs=[VMEM] * 5,
        out_specs=(VMEM,) * 3,
        compiler_params=pltpu.CompilerParams(vmem_limit_bytes=24 * MIB),
        cost_estimate=pl.CostEstimate(
            flops=2 * funcs * branch_w.size, bytes_accessed=2 * branch_w.size, transcendentals=0
        ),
        name="latents",
    )(got.transpose(1, 0, 2), branch_w, branch_b, trunk_w2, trunk_b2[None])

    unroll = min(nq, 8)
    late_rows = up(funcs + dims + 1, 16)
    late = pl.pallas_call(
        functools.partial(trunk_kernel, row, dims, nb * nq, unroll),
        out_shape=jax.ShapeDtypeStruct((late_rows, width + 128), BF),
        in_specs=[VMEM] * 5,
        out_specs=VMEM,
        scratch_shapes=[
            pltpu.VMEM((unroll, queries, hidden), BF),
            pltpu.VMEM((unroll, queries, hidden), BF),
            pltpu.VMEM((2 * funcs, hidden), F32),
            pltpu.VMEM((2 * (dims + 1) * funcs, hidden), F32),
            pltpu.VMEM((funcs, queries), F32),
        ],
        compiler_params=pltpu.CompilerParams(vmem_limit_bytes=32 * MIB),
        cost_estimate=pl.CostEstimate(
            flops=2 * 1024 * nq * queries * hidden, bytes_accessed=2 * MIB, transcendentals=nq * queries * hidden
        ),
        name="trunk",
    )(got, mixed, offset, trunk_w1, trunk_b1[None])

    def gather(x):
        shifts = [[(i, (i + k) % nb) for i in range(nb)] for k in range(1, nb)]
        return [x] + [lax.ppermute(x, "branch", pairs) for pairs in shifts]

    earlies, lates = gather(early), gather(late)
    blocks = 4
    gbw, gbb, gw1, gb1, gw2, gb2 = pl.pallas_call(
        functools.partial(tail_kernel, nb, funcs, dims, cut),
        out_shape=(
            jax.ShapeDtypeStruct((branches, cut, width), F32),
            jax.ShapeDtypeStruct((branches, width), F32),
            jax.ShapeDtypeStruct((dims, hidden), F32),
            jax.ShapeDtypeStruct((1, hidden), F32),
            jax.ShapeDtypeStruct((hidden, width), F32),
            jax.ShapeDtypeStruct((1, width), F32),
        ),
        in_specs=[VMEM] * (2 * nb + 2),
        out_specs=(ANY, VMEM, VMEM, VMEM, ANY, VMEM),
        scratch_shapes=[
            pltpu.VMEM((branches, cut, width), F32),
            pltpu.VMEM((blocks, hidden // blocks, width), F32),
            pltpu.SemaphoreType.DMA((blocks + branches,)),
        ],
        compiler_params=pltpu.CompilerParams(vmem_limit_bytes=24 * MIB),
        name="tail",
    )(*earlies, *lates, trunk_w2, trunk_b2[None])
    return (gbw, gbb, gw1, gb1[0], gw2, gb2[0])


def solution(mesh):
    placed = (
        P(None, ("branch", "query"), None),
        P(),
        P(),
        P(None, ("branch", "query")),
        P(("branch", "query")),
        P(("branch", "query")),
        P(),
        P(),
        P(),
        P(),
    )
    return jax.shard_map(
        shards,
        mesh=mesh,
        in_specs=placed,
        out_specs=(P(None, "query", None), P(), P(), P(), P(), P()),
        check_vma=False,
    )
```

time: 284 us -> 48.3 us (0.17)
  blocking collectives: 243 us -> 15 us
  matrix products: 19.3 us -> 0 us
  Pallas kernels: 0 us -> 13.9 us
  between operations: 14.3 us -> 0.69 us
  starting transfers between devices: 0.04 us -> 4.05 us
  waiting for transfers between devices: 0.02 us -> 3.72 us
  local copies, waits for them, and re-layouts: 6.86 us -> 10.4 us
    all_gather x3 -> x0, blocking collectives: 167 us -> none  [the longest x1 68.3 us: shards(): piece_delta = lax.all_gather(delta, ('branch', 'query'), axis=1, tiled=True)]
    psum x1 -> x0, blocking collectives: 38.1 us -> none  [shards(): lax.psum((gbb, gw1, gb1, gw2, gb2), ('branch', 'query'))]
    unnamed x1 -> x0, blocking collectives: 37.6 us -> none
    dot_general x9 -> x0, matrix products: 19.3 us -> none  [the longest x1 6.45 us: shards(): jnp.einsum('kfs,ksl->kfl', sensors, branch_w, preferred_element_type=jnp....]
    all_to_all x0 -> x1, blocking collectives: none -> 15 us  [shards(): got = lax.all_to_all(packed, 'query', 0, 0, tiled=True)]
    pallas_call x0 -> x4, Pallas kernels: none -> 13.9 us  [the longest x1 7.61 us: shards(): pl.pallas_call(functools.partial(trunk_kernel, row, dims, nb * nq, unroll...]
    ppermute x0 -> x6, starting transfers between devices: none -> 4.05 us  [gather(): return [x] + [lax.ppermute(x, 'branch', pairs) for pairs in shifts]]
    ppermute x0 -> x6, waiting for transfers between devices: none -> 3.72 us  [gather(): return [x] + [lax.ppermute(x, 'branch', pairs) for pairs in shifts]]
  transfers between devices with their start and end apart: 1 -> 6, of which waited for: 0 -> 2; matrix products, arithmetic and copies ran while one was open for 3% -> 0% of each run, Pallas kernels for 0% -> 0%
where the time goes in v2:
time: 48.3 us; the launch traced here: 47.8 us
  blocking collectives  15 us (31%)
  Pallas kernels  13.9 us (29%)
  local copies, waits for them, and re-layouts  10.4 us (22%)
  starting transfers between devices  4.05 us (8%)
  waiting for transfers between devices  3.72 us (8%)
  between operations  0.69 us (1%)
    all_to_all x1, blocking collectives, shards(): got = lax.all_to_all(packed, 'query', 0, 0, tiled=True)  15 us
    unnamed x20, local copies, waits for them, and re-layouts  10.3 us
    pallas_call x1, Pallas kernels, shards(): pl.pallas_call(functools.partial(trunk_kernel, row, dims, nb * nq, unroll...  7.61 us
    ppermute x6, starting transfers between devices, gather(): return [x] + [lax.ppermute(x, 'branch', pairs) for pairs in shifts]  4.05 us
    pallas_call x1, Pallas kernels, shards(): pl.pallas_call(functools.partial(tail_kernel, nb, funcs, dims, cut), out_...  4 us
    ppermute x6, waiting for transfers between devices, gather(): return [x] + [lax.ppermute(x, 'branch', pairs) for pairs in shifts]  3.72 us
    pallas_call x1, Pallas kernels, shards(): pl.pallas_call(functools.partial(latent_kernel, cut_row), out_shape=(jax....  2.27 us
  transfers between devices with their start and end apart: 6, of which 2 were waited for; matrix products, arithmetic and copies ran while one was open for 0% of the time, Pallas kernels for 0%

profile of v2, /device:TPU:0, one launch (start us, length us, event | category | flops | bytes accessed | tf_op | source)
XLA Modules:
  0.0 47.8 jit_solution(6674807144184989303)
XLA Ops:
  0.6 0.0 copy-start.4
  0.6 0.7 %copy-done.4 = bf16[3,1,2048]{2,0,1:T(4,128)(2,1)S(1)} copy-done((bf16[3,1,2048]{2,0,1:T(4,128)(2,1)S(1)}, bf16[3,1,2048]{2,0,1:T(4,128)(2,1)}, u32[]{:S(2)}) %copy-start.4) | copy-done | bytes 12312
  1.4 0.0 copy-start.5
  1.4 0.7 %copy-done.5 = bf16[3,512]{1,0:T(4,128)(2,1)S(1)} copy-done((bf16[3,512]{1,0:T(4,128)(2,1)S(1)}, bf16[3,512]{1,0:T(4,128)(2,1)}, u32[]{:S(2)}) %copy-start.5) | copy-done | bytes 3096
  2.0 0.0 copy-start.6
  2.0 0.7 %copy-done.6 = s32[512]{0:T(512)S(1)} copy-done((s32[512]{0:T(512)S(1)}, s32[512]{0:T(512)}, u32[]{:S(2)}) %copy-start.6) | copy-done | bytes 2072
  2.7 0.0 copy-start.7
  2.7 0.7 %copy-done.7 = f32[512]{0:T(512)S(1)} copy-done((f32[512]{0:T(512)S(1)}, f32[512]{0:T(512)}, u32[]{:S(2)}) %copy-start.7) | copy-done | bytes 2072
  3.4 0.1 pack.1
  3.5 15.0 %all_to_all.5.got_ref = bf16[8,24,512]{2,1,0:T(8,128)(2,1)S(1)} all-to-all(bf16[8,24,512]{2,1,0:T(8,128)(2,1)S(1)} %pack.1), channel_id=1, replica_groups=mesh['branch'=4,'query'=8] {'query'}, dimensions={0} | all-to-all | bytes 393216 | tf_op jit(solution)/shard_map/all_to_all | solution.py:220
  18.5 0.1 copy.16.got_ref
  18.6 0.0 copy-start
  18.6 4.6 %copy-done = bf16[3,2048,1024]{2,1,0:T(8,128)(2,1)S(1)} copy-done((bf16[3,2048,1024]{2,1,0:T(8,128)(2,1)S(1)}, bf16[3,2048,1024]{2,1,0:T(8,128)(2,1)}, u32[]{:S(2)}) %copy-start) | copy-done | bytes 12582936
  23.1 0.0 copy-start.1
  23.1 1.6 %copy-done.1 = bf16[1024,1024]{1,0:T(8,128)(2,1)S(1)} copy-done((bf16[1024,1024]{1,0:T(8,128)(2,1)S(1)}, bf16[1024,1024]{1,0:T(8,128)(2,1)}, u32[]{:S(2)}) %copy-start.1) | copy-done | bytes 2097176
  24.7 0.0 copy-start.2
  24.7 0.7 %copy-done.2 = f32[3,1024]{1,0:T(4,128)S(1)} copy-done((f32[3,1024]{1,0:T(4,128)S(1)}, f32[3,1024]{1,0:T(4,128)}, u32[]{:S(2)}) %copy-start.2) | copy-done | bytes 12312
  25.4 0.0 copy-start.3
  25.4 0.7 %copy-done.3 = f32[1024]{0:T(1024)S(1)} copy-done((f32[1024]{0:T(1024)S(1)}, f32[1024]{0:T(1024)}, u32[]{:S(2)}) %copy-start.3) | copy-done | bytes 4120
  26.1 0.0 copy-start.8
  26.1 0.0 copy-start.9
  26.1 2.3 %latents.1 = (bf16[32,1024]{1,0:T(8,128)(2,1)S(1)}, f32[8,1024]{1,0:T(8,128)S(1)}, f32[8,128]{1,0:T(8,128)S(1)}) custom-call(bf16[24,8,512]{2,1,0:T(8,128)(2,1)S(1)} %copy.16.got_ref, bf16[3,2048,1024]{2,1,0:T(8,128)(2,1)S(1)} %copy-done, f32[3,1024]{1,0:T(4,128)S(1)} %copy-done.2, bf16[1024,1024]{1,0:T(8,128)(2,1)S(1)} %copy-done.1, f32[1,1024]{1,0:T(1,128)S(1)} %bitcast.9), custom_call_target="tpu_custom_call" | custom-call | flops 100663296 | bytes 12582912 | tf_op jit(solution)/shard_map/latents/pallas_call | solution.py:222
  28.4 0.0 copy-done.8
  28.4 0.0 copy-done.9
  28.4 7.6 %trunk.1.refs_4_ = bf16[16,1152]{1,0:T(8,128)(2,1)S(1)} custom-call(bf16[8,24,512]{2,1,0:T(8,128)(2,1)S(1)} %all_to_all.5.got_ref, f32[8,1024]{1,0:T(8,128)S(1)} %get-tuple-element.16.mixed_ref, f32[8,128]{1,0:T(8,128)S(1)} %get-tuple-element.17.offset_ref, bf16[3,1024]{1,0:T(4,128)(2,1)S(1)} %copy-done.8, f32[1,1024]{1,0:T(1,128)S(1)} %bitcast.14), custom_call_target="tpu_custom_call" | custom-call | flops 8589934592 | bytes 2097152 | tf_op jit(solution)/shard_map/trunk/pallas_call | solution.py:240
  36.0 0.1 collective-permute-start.5
  36.1 1.6 %collective-permute-start.2 = (bf16[32,1024]{1,0:T(8,128)(2,1)S(1)}, bf16[32,1024]{1,0:T(8,128)(2,1)S(1)}, u32[]{:S(2)}, u32[]{:S(2)}) collective-permute-start(bf16[32,1024]{1,0:T(8,128)(2,1)S(1)} %get-tuple-element.15.refs_0_), channel_id=1, source_target_pairs={{0,24},{8,0},{16,8},{24,16},{1,25},{9,1},{17,9},{25,17},{2,26},{10... | collective-permute-start | bytes 196616 | tf_op jit(solution)/shard_map/ppermute | solution.py:261
  37.7 0.5 %collective-permute-start.1 = (bf16[32,1024]{1,0:T(8,128)(2,1)S(1)}, bf16[32,1024]{1,0:T(8,128)(2,1)S(1)}, u32[]{:S(2)}, u32[]{:S(2)}) collective-permute-start(bf16[32,1024]{1,0:T(8,128)(2,1)S(1)} %get-tuple-element.15.refs_0_), channel_id=1, source_target_pairs={{0,16},{8,24},{16,0},{24,8},{1,17},{9,25},{17,1},{25,9},{2,18},{10... | collective-permute-start | bytes 196616 | tf_op jit(solution)/shard_map/ppermute | solution.py:261
  38.2 0.0 collective-permute-start
  38.2 1.5 %collective-permute-start.4 = (bf16[16,1152]{1,0:T(8,128)(2,1)S(1)}, bf16[16,1152]{1,0:T(8,128)(2,1)S(1)}, u32[]{:S(2)}, u32[]{:S(2)}) collective-permute-start(bf16[16,1152]{1,0:T(8,128)(2,1)S(1)} %trunk.1.refs_4_), channel_id=1, source_target_pairs={{0,16},{8,24},{16,0},{24,8},{1,17},{9,25},{17,1},{25,9},{2,18},{10... | collective-permute-start | bytes 110600 | tf_op jit(solution)/shard_map/ppermute | solution.py:261
  39.7 0.0 collective-permute-done.5.refs_7_
  39.8 0.3 collective-permute-start.3
  40.1 3.4 %collective-permute-done.4.refs_6_ = bf16[16,1152]{1,0:T(8,128)(2,1)S(1)} collective-permute-done((bf16[16,1152]{1,0:T(8,128)(2,1)S(1)}, bf16[16,1152]{1,0:T(8,128)(2,1)S(1)}, u32[]{:S(2)}, u32[]{:S(2)}) %collective-permute-start.4) | collective-permute-done | bytes 36896 | tf_op jit(solution)/shard_map/ppermute | solution.py:261
  43.4 0.4 collective-permute-done.3.refs_5_
  43.8 0.0 collective-permute-done.2.refs_3_
  43.8 0.0 collective-permute-done.1.refs_2_
  43.8 0.0 collective-permute-done.refs_1_
  43.8 4.0 %tail.1 = (f32[3,256,1024]{2,1,0:T(8,128)}, f32[3,1024]{1,0:T(4,128)}, f32[3,1024]{1,0:T(4,128)}, f32[1,1024]{1,0:T(1,128)}, f32[1024,1024]{1,0:T(8,128)}, /*index=5*/f32[1,1024]{1,0:T(1,128)}) custom-call(bf16[32,1024]{1,0:T(8,128)(2,1)S(1)} %get-tuple-element.15.refs_0_, bf16[32,1024]{1,0:T(8,128)(2,1)S(1)} %collective-permute-done.refs_1_, ...), custom_call_target="tpu_custom_call" | custom-call | tf_op jit(solution)/shard_map/tail/pallas_call | solution.py:265
Async XLA Ops:
  0.6 0.7 %copy-start.4 = (bf16[3,1,2048]{2,0,1:T(4,128)(2,1)S(1)}, bf16[3,1,2048]{2,0,1:T(4,128)(2,1)}, u32[]{:S(2)}) copy-start(bf16[3,1,2048]{2,0,1:T(4,128)(2,1)} %param.10) | copy-start | bytes 36868
  1.4 0.7 %copy-start.5 = (bf16[3,512]{1,0:T(4,128)(2,1)S(1)}, bf16[3,512]{1,0:T(4,128)(2,1)}, u32[]{:S(2)}) copy-start(bf16[3,512]{1,0:T(4,128)(2,1)} %coords_ref.1) | copy-start | bytes 9220
  2.0 0.7 %copy-start.6 = (s32[512]{0:T(512)S(1)}, s32[512]{0:T(512)}, u32[]{:S(2)}) copy-start(s32[512]{0:T(512)} %param.14) | copy-start | bytes 6148
  2.7 0.7 %copy-start.7 = (f32[512]{0:T(512)S(1)}, f32[512]{0:T(512)}, u32[]{:S(2)}) copy-start(f32[512]{0:T(512)} %param.15) | copy-start | bytes 6148
  18.6 4.6 %copy-start = (bf16[3,2048,1024]{2,1,0:T(8,128)(2,1)S(1)}, bf16[3,2048,1024]{2,1,0:T(8,128)(2,1)}, u32[]{:S(2)}) copy-start(bf16[3,2048,1024]{2,1,0:T(8,128)(2,1)} %w_ref.1) | copy-start | bytes 37748740
  23.1 1.6 %copy-start.1 = (bf16[1024,1024]{1,0:T(8,128)(2,1)S(1)}, bf16[1024,1024]{1,0:T(8,128)(2,1)}, u32[]{:S(2)}) copy-start(bf16[1024,1024]{1,0:T(8,128)(2,1)} %refs_8_.1) | copy-start | bytes 6291460
  24.7 0.7 %copy-start.2 = (f32[3,1024]{1,0:T(4,128)S(1)}, f32[3,1024]{1,0:T(4,128)}, u32[]{:S(2)}) copy-start(f32[3,1024]{1,0:T(4,128)} %bias_ref.1) | copy-start | bytes 36868
  25.4 0.7 %copy-start.3 = (f32[1024]{0:T(1024)S(1)}, f32[1024]{0:T(1024)}, u32[]{:S(2)}) copy-start(f32[1024]{0:T(1024)} %param.19) | copy-start | bytes 12292
  26.1 2.3 %copy-start.8 = (bf16[3,1024]{1,0:T(4,128)(2,1)S(1)}, bf16[3,1024]{1,0:T(4,128)(2,1)}, u32[]{:S(2)}) copy-start(bf16[3,1024]{1,0:T(4,128)(2,1)} %w1_ref.1) | copy-start | bytes 18436
  26.1 2.3 %copy-start.9 = (f32[1024]{0:T(1024)S(1)}, f32[1024]{0:T(1024)}, u32[]{:S(2)}) copy-start(f32[1024]{0:T(1024)} %param.17) | copy-start | bytes 12292
  36.0 3.7 %collective-permute-start.5 = (bf16[16,1152]{1,0:T(8,128)(2,1)S(1)}, bf16[16,1152]{1,0:T(8,128)(2,1)S(1)}, u32[]{:S(2)}, u32[]{:S(2)}) collective-permute-start(bf16[16,1152]{1,0:T(8,128)(2,1)S(1)} %trunk.1.refs_4_), channel_id=1, source_target_pairs={{0,24},{8,0},{16,8},{24,16},{1,25},{9,1},{17,9},{25,17},{2,26},{10... | collective-permute-start | bytes 110600 | tf_op jit(solution)/shard_map/ppermute | solution.py:261
  36.1 7.7 %collective-permute-start.2 = (bf16[32,1024]{1,0:T(8,128)(2,1)S(1)}, bf16[32,1024]{1,0:T(8,128)(2,1)S(1)}, u32[]{:S(2)}, u32[]{:S(2)}) collective-permute-start(bf16[32,1024]{1,0:T(8,128)(2,1)S(1)} %get-tuple-element.15.refs_0_), channel_id=1, source_target_pairs={{0,24},{8,0},{16,8},{24,16},{1,25},{9,1},{17,9},{25,17},{2,26},{10... | collective-permute-start | bytes 196616 | tf_op jit(solution)/shard_map/ppermute | solution.py:261
  37.7 6.1 %collective-permute-start.1 = (bf16[32,1024]{1,0:T(8,128)(2,1)S(1)}, bf16[32,1024]{1,0:T(8,128)(2,1)S(1)}, u32[]{:S(2)}, u32[]{:S(2)}) collective-permute-start(bf16[32,1024]{1,0:T(8,128)(2,1)S(1)} %get-tuple-element.15.refs_0_), channel_id=1, source_target_pairs={{0,16},{8,24},{16,0},{24,8},{1,17},{9,25},{17,1},{25,9},{2,18},{10... | collective-permute-start | bytes 196616 | tf_op jit(solution)/shard_map/ppermute | solution.py:261
  38.2 5.6 %collective-permute-start = (bf16[32,1024]{1,0:T(8,128)(2,1)S(1)}, bf16[32,1024]{1,0:T(8,128)(2,1)S(1)}, u32[]{:S(2)}, u32[]{:S(2)}) collective-permute-start(bf16[32,1024]{1,0:T(8,128)(2,1)S(1)} %get-tuple-element.15.refs_0_), channel_id=1, source_target_pairs={{0,8},{8,16},{16,24},{24,0},{1,9},{9,17},{17,25},{25,1},{2,10},{10... | collective-permute-start | bytes 196616 | tf_op jit(solution)/shard_map/ppermute | solution.py:261
  38.2 5.2 %collective-permute-start.4 = (bf16[16,1152]{1,0:T(8,128)(2,1)S(1)}, bf16[16,1152]{1,0:T(8,128)(2,1)S(1)}, u32[]{:S(2)}, u32[]{:S(2)}) collective-permute-start(bf16[16,1152]{1,0:T(8,128)(2,1)S(1)} %trunk.1.refs_4_), channel_id=1, source_target_pairs={{0,16},{8,24},{16,0},{24,8},{1,17},{9,25},{17,1},{25,9},{2,18},{10... | collective-permute-start | bytes 110600 | tf_op jit(solution)/shard_map/ppermute | solution.py:261
  39.8 4.0 %collective-permute-start.3 = (bf16[16,1152]{1,0:T(8,128)(2,1)S(1)}, bf16[16,1152]{1,0:T(8,128)(2,1)S(1)}, u32[]{:S(2)}, u32[]{:S(2)}) collective-permute-start(bf16[16,1152]{1,0:T(8,128)(2,1)S(1)} %trunk.1.refs_4_), channel_id=1, source_target_pairs={{0,8},{8,16},{16,24},{24,0},{1,9},{9,17},{17,25},{25,1},{2,10},{10... | collective-permute-start | bytes 110600 | tf_op jit(solution)/shard_map/ppermute | solution.py:261

commit v3 on v2

v3 whole, which is shorter than its diff:
```python
import functools

import jax
import jax.numpy as jnp
from jax import lax
from jax.experimental import pallas as pl
from jax.experimental.pallas import tpu as pltpu
from jax.sharding import PartitionSpec as P

BF = jnp.bfloat16
F32 = jnp.float32
MIB = 1 << 20
VMEM = pl.BlockSpec(memory_space=pltpu.VMEM)
HBM = pl.BlockSpec(memory_space=pltpu.HBM)


def up(value, step):
    return -(-value // step) * step


def pieces(value, count):
    out = []
    for _ in range(count):
        top = value.astype(BF)
        out.append(top)
        value = value - top.astype(F32)
    return out


def dot(a, b, dims=((1,), (0,))):
    return lax.dot_general(a, b, (dims, ((), ())), preferred_element_type=F32)


def stack(rows, count):
    have = sum(r.shape[0] for r in rows)
    if have < count:
        rows = rows + [jnp.zeros((count - have, rows[0].shape[1]), rows[0].dtype)]
    return jnp.concatenate(rows, axis=0)


def in_hbm(*arrays):
    return [pltpu.with_memory_space_constraint(a, pltpu.HBM) for a in arrays]


def first_layer(w1_ref, b1_ref):
    rows = [w1_ref[...].astype(F32)] + [b.astype(F32) for b in pieces(b1_ref[...], 3)]
    return stack(rows, up(w1_ref.shape[0] + 3, 8)).astype(BF)


def hidden_units(xyz, first):
    a = stack([xyz, jnp.ones((3, xyz.shape[1]), F32)], first.shape[0]).T.astype(BF)
    return jnp.tanh(dot(a, first)).astype(BF)


def for_chunks(chunks, unroll, visit):
    if chunks == unroll:
        for j in range(chunks):
            visit(j, j)
    else:
        def several(i, carry):
            for u in range(unroll):
                visit(i * unroll + u, u)
            return carry
        lax.fori_loop(0, chunks // unroll, several, 0)


def fetch(sems, first, *pairs):
    copies = [pltpu.make_async_copy(src, dst, sems.at[first + i]) for i, (src, dst) in enumerate(pairs)]
    for copy in copies:
        copy.start()
    return copies


def wait(copies):
    for copy in copies:
        copy.wait()


def pack_kernel(sensors_hbm, coords_hbm, index_hbm, targets_hbm, out_ref, sensors_ref, coords_ref, index_ref, targets_ref, sems):
    wait(fetch(
        sems, 0, (sensors_hbm, sensors_ref), (coords_hbm, coords_ref), (index_hbm, index_ref), (targets_hbm, targets_ref)
    ))
    peers, rows, q = out_ref.shape
    branches, sensor_count = sensors_ref.shape
    cut = sensor_count // peers
    s = sensors_ref[...].astype(F32)
    base = [s[k : k + 1, c : c + q] for k in range(branches) for c in range(0, sensor_count, q)]
    base += [coords_ref[...].astype(F32), index_ref[...].astype(F32)]
    base += [t.astype(F32) for t in pieces(targets_ref[...], 3)]
    have = sum(r.shape[0] for r in base)
    whole = have // 8 * 8
    both = jnp.concatenate(base, axis=0)
    top, rest = both[:whole], both[whole:]
    flat = up(branches * cut, q)
    for j in range(peers):
        line = [s[k : k + 1, j * cut : (j + 1) * cut] for k in range(branches)]
        if flat > branches * cut:
            line.append(jnp.zeros((1, flat - branches * cut), F32))
        line = jnp.concatenate(line, axis=1)
        tail = [rest] + [line[:, c : c + q] for c in range(0, flat, q)]
        out_ref[j] = jnp.concatenate([top, stack(tail, rows - whole)], axis=0).astype(BF)


def latent_kernel(
    row, cut_row, ahead,
    got_ref, turned_ref, w_hbm, bias_hbm, w2_hbm, b2_hbm, w1_hbm, b1_hbm,
    early_ref, mixed_ref, offset_ref, *refs,
):
    h_ref = refs[0] if ahead else None
    w_ref, bias_ref, w2_ref, b2_ref, w1_ref, b1_ref, sems = refs[-7:]
    chunks, _, q = got_ref.shape
    funcs = turned_ref.shape[1]
    branches, sensor_count, width = w_ref.shape
    dims = w1_ref.shape[0]
    per = sensor_count // q
    small = fetch(sems, 0, (w1_hbm, w1_ref), (b1_hbm, b1_ref), (bias_hbm, bias_ref), (b2_hbm, b2_ref))
    parts = [(k, pl.ds(c * q, q)) for k in range(branches) for c in range(per)]
    large = fetch(sems, 4, *[(w_hbm.at[p], w_ref.at[p]) for p in parts], (w2_hbm, w2_ref))
    wait(small)

    if ahead:
        first = first_layer(w1_ref, b1_ref)
        for j in range(chunks):
            h_ref[j] = hidden_units(got_ref[j].astype(F32)[row : row + dims], first)

    lats = []
    for k in range(branches):
        pre = bias_ref[k : k + 1, :]
        for c in range(per):
            large[k * per + c].wait()
            pre = pre + dot(turned_ref[k * per + c], w_ref[k, c * q : (c + 1) * q])
        lats.append(jnp.tanh(pre).astype(BF).astype(F32))
    product = (lats[0] * lats[1] * lats[2]).astype(BF)
    lines = [turned_ref[cut_row + c].astype(F32) for c in range(up(branches * sensor_count // funcs, q) // q)]
    if len(lines) * q < width:
        lines.append(jnp.zeros((funcs, width - len(lines) * q), F32))
    early_ref[...] = jnp.concatenate(lats + [jnp.concatenate(lines, axis=1)], axis=0).astype(BF)
    offset = jnp.sum(product.astype(F32) * b2_ref[...], axis=1, keepdims=True)
    offset_ref[...] = jnp.broadcast_to(offset, offset_ref.shape)
    large[-1].wait()
    mixed_ref[...] = dot(product, w2_ref[...], ((1,), (1,)))


def trunk_kernel(
    row, dims, total_funcs, ahead,
    got_ref, mixed_ref, offset_ref, *refs,
):
    if ahead:
        h_ref, late_ref, g_ref, m_ref, r_ref = refs
        unroll = h_ref.shape[0]
    else:
        w1_ref, b1_ref, late_ref, g_ref, m_ref, r_ref, h_ref = refs
        first = first_layer(w1_ref, b1_ref)
        unroll = h_ref.shape[0]
    chunks, _, q = got_ref.shape
    funcs, width = mixed_ref.shape
    scale = width ** (-0.5)
    mixed = jnp.concatenate(pieces(mixed_ref[...], 2), axis=0)
    offset = offset_ref[:, 0:1]
    place = lax.broadcasted_iota(jnp.int32, (funcs, q), 0).astype(F32)
    g_ref[...] = jnp.zeros_like(g_ref)
    m_ref[...] = jnp.zeros_like(m_ref)
    r_ref[...] = jnp.zeros_like(r_ref)

    def visit(j, slot):
        block = got_ref[j].astype(F32)
        xyz = block[row : row + dims]
        owner = block[row + dims : row + dims + 1]
        target = block[row + dims + 1 : row + dims + 2]
        target = target + block[row + dims + 2 : row + dims + 3]
        target = target + block[row + dims + 3 : row + dims + 4]
        if not ahead:
            h_ref[slot] = hidden_units(xyz, first)
        h = h_ref[slot]
        scores = dot(mixed, h, ((1,), (1,)))
        scores = scores[:funcs] + scores[funcs:] + offset
        owned = (owner == place).astype(F32)
        pred = jnp.sum(owned * scores, axis=0, keepdims=True) * scale
        resid = (pred - target) / total_funcs
        coef = owned * (resid * scale)
        g_ref[...] += dot(jnp.concatenate(pieces(coef, 2), axis=0), h)
        hf = h.astype(F32)
        slope = (1.0 - hf * hf).astype(BF)
        spread = jnp.concatenate([coef] + [coef * xyz[d : d + 1] for d in range(dims)], axis=0)
        m_ref[...] += dot(jnp.concatenate(pieces(spread, 2), axis=0), slope)
        r_ref[...] += coef

    for_chunks(chunks, unroll, visit)

    g = g_ref[:funcs] + g_ref[funcs:]
    r = jnp.broadcast_to(jnp.sum(r_ref[...], axis=1, keepdims=True), (funcs, late_ref.shape[1] - width))
    high, low = pieces(r, 2)
    lane = lax.broadcasted_iota(jnp.int32, r.shape, 1)
    r = jnp.where(lane < r.shape[1] // 2, high.astype(F32), low.astype(F32))
    half = (dims + 1) * funcs
    moments = m_ref[:half] + m_ref[half:]
    grads = [
        jnp.sum(moments[d * funcs : (d + 1) * funcs] * mixed_ref[...], axis=0, keepdims=True)
        for d in range(dims + 1)
    ]
    grads = jnp.concatenate(grads, axis=0)
    grads = jnp.concatenate([grads, jnp.zeros((dims + 1, r.shape[1]), F32)], axis=1)
    late_ref[...] = stack([jnp.concatenate([g, r], axis=1), grads], late_ref.shape[0]).astype(BF)


def factor_kernel(groups, funcs, *refs):
    earlies = refs[:groups]
    w2_hbm, b2_hbm, product_ref, factor_ref, turned_ref, w2_ref, b2_ref, sems = refs[groups:]
    copies = fetch(sems, 0, (w2_hbm, w2_ref), (b2_hbm, b2_ref))
    branches, cut, _ = turned_ref.shape
    early = [e[...].astype(F32) for e in earlies]

    def rows(first):
        return jnp.concatenate([p[first : first + funcs] for p in early], axis=0)

    lat = [rows(k * funcs) for k in range(branches)]
    product_ref[...] = (lat[0] * lat[1] * lat[2]).astype(BF)
    lines = rows(branches * funcs)
    for k in range(branches):
        others = [lat[j] for j in range(branches) if j != k]
        factor_ref[k] = others[0] * others[1] * (1.0 - lat[k] * lat[k])
        turned_ref[k] = lines[:, k * cut : (k + 1) * cut].T.astype(BF)
    wait(copies)


def tail_kernel(groups, funcs, dims, *refs):
    lates = refs[:groups]
    (
        product_ref, factor_ref, turned_ref, w2_ref, b2_ref,
        gbw_ref, gbb_ref, gw1_ref, gb1_ref, gw2_ref, gb2_ref, gbw_buf, gw2_buf, sems,
    ) = refs[groups:]
    width = w2_ref.shape[1]
    branches = gbw_ref.shape[0]
    late = [x[...].astype(F32) for x in lates]
    product = product_ref[...]
    ends = jnp.concatenate([x[:funcs] for x in late], axis=0)
    g, r = ends[:, :width], ends[:, width:]
    r = r[:, :1] + r[:, r.shape[1] // 2 : r.shape[1] // 2 + 1]
    copies = []
    blocks, height, _ = gw2_buf.shape
    for c in range(blocks):
        gw2_buf[c] = dot(g[:, c * height : (c + 1) * height].T.astype(BF), product)
        copies += fetch(sems, c, (gw2_buf.at[c], gw2_ref.at[pl.ds(c * height, height)]))
    dprod = dot(g.astype(BF), w2_ref[...]) + r * b2_ref[...]
    gbb = []
    for k in range(branches):
        delta = (dprod * factor_ref[k]).astype(BF)
        gbw_buf[k] = dot(turned_ref[k], delta)
        copies += fetch(sems, blocks + k, (gbw_buf.at[k], gbw_ref.at[k]))
        gbb.append(jnp.sum(delta.astype(F32), axis=0, keepdims=True))
    gbb_ref[...] = jnp.concatenate(gbb, axis=0)
    grads = late[0][funcs : funcs + dims + 1, :width]
    for x in late[1:]:
        grads = grads + x[funcs : funcs + dims + 1, :width]
    gb1_ref[...] = grads[:1]
    gw1_ref[...] = grads[1:]
    gb2_ref[...] = jnp.sum(r * product.astype(F32), axis=0, keepdims=True)
    wait(copies)


def shards(
    sensors, branch_w, branch_b, coords, func_index, targets, trunk_w1, trunk_b1, trunk_w2, trunk_b2
):
    branches, func_dev, sensor_count = sensors.shape
    dims, queries = coords.shape
    hidden, width = trunk_w2.shape
    nb, nq = lax.axis_size("branch"), lax.axis_size("query")
    assert func_dev == 1 and sensor_count % queries == 0 and hidden == width
    funcs = nq
    cut = sensor_count // nq
    per = sensor_count // queries
    row = branches * per
    cut_row = row + dims + 4
    rows = up(cut_row + up(branches * cut, queries) // queries, 8)
    ahead = nq * queries * hidden * 2 <= 16 * MIB
    units_shape = (nq if ahead else min(nq, 8), queries, hidden)

    packed = pl.pallas_call(
        pack_kernel,
        out_shape=jax.ShapeDtypeStruct((nq, rows, queries), BF),
        in_specs=[HBM] * 4,
        out_specs=VMEM,
        scratch_shapes=[
            pltpu.VMEM((branches, sensor_count), BF),
            pltpu.VMEM((dims, queries), BF),
            pltpu.VMEM((1, queries), jnp.int32),
            pltpu.VMEM((1, queries), F32),
            pltpu.SemaphoreType.DMA((4,)),
        ],
        compiler_params=pltpu.CompilerParams(vmem_limit_bytes=8 * MIB),
        name="pack",
    )(*in_hbm(sensors.reshape(branches, sensor_count), coords, func_index[None], targets[None]))
    got = lax.all_to_all(packed, "query", 0, 0, tiled=True)

    early, mixed, offset, *units = pl.pallas_call(
        functools.partial(latent_kernel, row, cut_row, ahead),
        out_shape=(
            jax.ShapeDtypeStruct(((branches + 1) * funcs, width), BF),
            jax.ShapeDtypeStruct((funcs, hidden), F32),
            jax.ShapeDtypeStruct((funcs, 128), F32),
        ) + (jax.ShapeDtypeStruct(units_shape, BF),) * ahead,
        in_specs=[VMEM] * 2 + [HBM] * 6,
        out_specs=(VMEM,) * (3 + ahead),
        scratch_shapes=[
            pltpu.VMEM((branches, sensor_count, width), BF),
            pltpu.VMEM((branches, width), F32),
            pltpu.VMEM((hidden, width), BF),
            pltpu.VMEM((1, width), F32),
            pltpu.VMEM((dims, hidden), BF),
            pltpu.VMEM((1, hidden), F32),
            pltpu.SemaphoreType.DMA((4 + branches * per + 1,)),
        ],
        compiler_params=pltpu.CompilerParams(vmem_limit_bytes=28 * MIB),
        cost_estimate=pl.CostEstimate(
            flops=2 * (256 * nq * queries * hidden + 256 * branch_w.size),
            bytes_accessed=2 * branch_w.size,
            transcendentals=nq * queries * hidden,
        ),
        name="latents",
    )(
        got,
        got.transpose(1, 0, 2),
        *in_hbm(branch_w, branch_b, trunk_w2, trunk_b2[None], trunk_w1, trunk_b1[None]),
    )

    needs = units if ahead else [trunk_w1, trunk_b1[None]]
    late_rows = up(funcs + dims + 1, 16)
    late = pl.pallas_call(
        functools.partial(trunk_kernel, row, dims, nb * nq, ahead),
        out_shape=jax.ShapeDtypeStruct((late_rows, width + 128), BF),
        in_specs=[VMEM] * (3 + len(needs)),
        out_specs=VMEM,
        scratch_shapes=[
            pltpu.VMEM((2 * funcs, hidden), F32),
            pltpu.VMEM((2 * (dims + 1) * funcs, hidden), F32),
            pltpu.VMEM((funcs, queries), F32),
        ] + [pltpu.VMEM(units_shape, BF)] * (not ahead),
        compiler_params=pltpu.CompilerParams(vmem_limit_bytes=24 * MIB),
        cost_estimate=pl.CostEstimate(
            flops=2 * 768 * nq * queries * hidden, bytes_accessed=2 * MIB, transcendentals=0
        ),
        name="trunk",
    )(got, mixed, offset, *needs)

    def gather(x):
        shifts = [[(i, (i + k) % nb) for i in range(nb)] for k in range(1, nb)]
        return [x] + [lax.ppermute(x, "branch", pairs) for pairs in shifts]

    earlies, lates = gather(early), gather(late)
    every = nb * funcs
    prepared = pl.pallas_call(
        functools.partial(factor_kernel, nb, funcs),
        out_shape=(
            jax.ShapeDtypeStruct((every, width), BF),
            jax.ShapeDtypeStruct((branches, every, width), F32),
            jax.ShapeDtypeStruct((branches, cut, every), BF),
            jax.ShapeDtypeStruct((hidden, width), BF),
            jax.ShapeDtypeStruct((1, width), F32),
        ),
        in_specs=[VMEM] * nb + [HBM] * 2,
        out_specs=(VMEM,) * 5,
        scratch_shapes=[pltpu.SemaphoreType.DMA((2,))],
        compiler_params=pltpu.CompilerParams(vmem_limit_bytes=16 * MIB),
        cost_estimate=pl.CostEstimate(flops=MIB, bytes_accessed=4 * MIB, transcendentals=0),
        name="factors",
    )(*earlies, *in_hbm(trunk_w2, trunk_b2[None]))
    blocks = 4
    gbw, gbb, gw1, gb1, gw2, gb2 = pl.pallas_call(
        functools.partial(tail_kernel, nb, funcs, dims),
        out_shape=(
            jax.ShapeDtypeStruct((branches, cut, width), F32),
            jax.ShapeDtypeStruct((branches, width), F32),
            jax.ShapeDtypeStruct((dims, hidden), F32),
            jax.ShapeDtypeStruct((1, hidden), F32),
            jax.ShapeDtypeStruct((hidden, width), F32),
            jax.ShapeDtypeStruct((1, width), F32),
        ),
        in_specs=[VMEM] * (nb + 5),
        out_specs=(HBM, VMEM, VMEM, VMEM, HBM, VMEM),
        scratch_shapes=[
            pltpu.VMEM((branches, cut, width), F32),
            pltpu.VMEM((blocks, hidden // blocks, width), F32),
            pltpu.SemaphoreType.DMA((blocks + branches,)),
        ],
        compiler_params=pltpu.CompilerParams(vmem_limit_bytes=24 * MIB),
        name="tail",
    )(*lates, *prepared)
    return (gbw, gbb, gw1, gb1[0], gw2, gb2[0])


def solution(mesh):
    placed = (
        P(None, ("branch", "query"), None),
        P(),
        P(),
        P(None, ("branch", "query")),
        P(("branch", "query")),
        P(("branch", "query")),
        P(),
        P(),
        P(),
        P(),
    )
    return jax.shard_map(
        shards,
        mesh=mesh,
        in_specs=placed,
        out_specs=(P(None, "query", None), P(), P(), P(), P(), P()),
        check_vma=False,
    )
```

time: 48.3 us -> 40.9 us (0.85)
  local copies, waits for them, and re-layouts: 10.4 us -> 0.06 us
  Pallas kernels: 13.9 us -> 18.8 us
  waiting for transfers between devices: 3.72 us -> 2.07 us
    unnamed x20 -> x0, local copies, waits for them, and re-layouts: 10.3 us -> none
    pallas_call x3 -> x4, Pallas kernels: 13.9 us -> 17.9 us  [the longest x1 6.22 us: shards(): pl.pallas_call(functools.partial(latent_kernel, row, cut_row, ahead), out...]
    ppermute x6, waiting for transfers between devices: 3.72 us -> 2.07 us  [gather(): return [x] + [lax.ppermute(x, 'branch', pairs) for pairs in shifts]]
    pallas_call x1, Pallas kernels: 0.06 us -> 0.82 us  [shards(): pl.pallas_call(pack_kernel, out_shape=jax.ShapeDtypeStruct((nq, rows, que...]
  transfers between devices with their start and end apart: 6 -> 6, of which waited for: 2 -> 1; matrix products, arithmetic and copies ran while one was open for 0% -> 0% of each run, Pallas kernels for 0% -> 19%
where the time goes in v3:
time: 40.9 us; the launch traced here: 40.6 us
  Pallas kernels  18.8 us (46%)
  blocking collectives  15 us (37%)
  starting transfers between devices  3.95 us (10%)
  waiting for transfers between devices  2.07 us (5%)
  between operations  0.7 us (2%)
    all_to_all x1, blocking collectives, shards(): got = lax.all_to_all(packed, 'query', 0, 0, tiled=True)  15 us
    pallas_call x1, Pallas kernels, shards(): pl.pallas_call(functools.partial(latent_kernel, row, cut_row, ahead), out...  6.22 us
    pallas_call x1, Pallas kernels, shards(): pl.pallas_call(functools.partial(trunk_kernel, row, dims, nb * nq, ahead)...  6.03 us
    pallas_call x1, Pallas kernels, shards(): pl.pallas_call(functools.partial(tail_kernel, nb, funcs, dims), out_shape...  3.99 us
    ppermute x6, starting transfers between devices, gather(): return [x] + [lax.ppermute(x, 'branch', pairs) for pairs in shifts]  3.95 us
    ppermute x6, waiting for transfers between devices, gather(): return [x] + [lax.ppermute(x, 'branch', pairs) for pairs in shifts]  2.07 us
    pallas_call x1, Pallas kernels, shards(): pl.pallas_call(functools.partial(factor_kernel, nb, funcs), out_shape=(ja...  1.69 us
    pallas_call x1, Pallas kernels, shards(): pl.pallas_call(pack_kernel, out_shape=jax.ShapeDtypeStruct((nq, rows, que...  0.82 us
  transfers between devices with their start and end apart: 6, of which 1 were waited for; matrix products, arithmetic and copies ran while one was open for 0% of the time, Pallas kernels for 19%

profile of v3, /device:TPU:0, one launch (start us, length us, event | category | flops | bytes accessed | tf_op | source)
XLA Modules:
  0.0 40.6 jit_solution(16607175908588593168)
XLA Ops:
  0.6 0.8 %pack.1 = bf16[8,24,512]{2,1,0:T(8,128)(2,1)S(1)} custom-call(bf16[3,2048]{1,0:T(4,128)(2,1)} %bitcast.9, bf16[3,512]{1,0:T(4,128)(2,1)} %coords_hbm.1, s32[1,512]{1,0:T(1,128)} %bitcast.12, f32[1,512]{1,0:T(1,128)} %bitcast.13), custom_call_target="tpu_custom_call" | custom-call | tf_op jit(solution)/shard_map/pack/pallas_call | solution.py:278
  1.5 15.0 %all_to_all.5.got_ref = bf16[8,24,512]{2,1,0:T(8,128)(2,1)S(1)} all-to-all(bf16[8,24,512]{2,1,0:T(8,128)(2,1)S(1)} %pack.1), channel_id=1, replica_groups=mesh['branch'=4,'query'=8] {'query'}, dimensions={0} | all-to-all | bytes 393216 | tf_op jit(solution)/shard_map/all_to_all | solution.py:293
  16.5 0.1 copy.16.turned_ref
  16.6 6.2 %latents.1 = (bf16[32,1024]{1,0:T(8,128)(2,1)S(1)}, f32[8,1024]{1,0:T(8,128)S(1)}, f32[8,128]{1,0:T(8,128)S(1)}, bf16[8,512,1024]{2,1,0:T(8,128)(2,1)S(1)}) custom-call(bf16[8,24,512]{2,1,0:T(8,128)(2,1)S(1)} %all_to_all.5.got_ref, bf16[24,8,512]{2,1,0:T(8,128)(2,1)S(1)} %copy.16.turned_ref, bf16[3,2048,1024]{2,1,0:T(8,128)(2,1)} %w_hbm.1, ...), custom_call_target="tpu_custom_call" | custom-call | flops 5368709120 | bytes 12582912 | tf_op jit(solution)/shard_map/latents/pallas_call | solution.py:295
  22.8 0.1 collective-permute-start.5
  22.9 1.6 %collective-permute-start.4 = (bf16[32,1024]{1,0:T(8,128)(2,1)S(1)}, bf16[32,1024]{1,0:T(8,128)(2,1)S(1)}, u32[]{:S(2)}, u32[]{:S(2)}) collective-permute-start(bf16[32,1024]{1,0:T(8,128)(2,1)S(1)} %get-tuple-element.24.refs_0_), channel_id=1, source_target_pairs={{0,16},{8,24},{16,0},{24,8},{1,17},{9,25},{17,1},{25,9},{2,18},{10... | collective-permute-start | bytes 196616 | tf_op jit(solution)/shard_map/ppermute | solution.py:347
  24.4 0.2 collective-permute-start.3
  24.6 6.0 %trunk.1.refs_0_ = bf16[16,1152]{1,0:T(8,128)(2,1)S(1)} custom-call(bf16[8,24,512]{2,1,0:T(8,128)(2,1)S(1)} %all_to_all.5.got_ref, f32[8,1024]{1,0:T(8,128)S(1)} %get-tuple-element.21.mixed_ref, f32[8,128]{1,0:T(8,128)S(1)} %get-tuple-element.22.offset_ref, bf16[8,512,1024]{2,1,0:T(8,128)(2,1)S(1)} %get-tuple-element.23.refs_0_), custom_call_target="tpu_custom_call" | custom-call | flops 6442450944 | bytes 2097152 | tf_op jit(solution)/shard_map/trunk/pallas_call | solution.py:328
  30.6 1.6 %collective-permute-start.2 = (bf16[16,1152]{1,0:T(8,128)(2,1)S(1)}, bf16[16,1152]{1,0:T(8,128)(2,1)S(1)}, u32[]{:S(2)}, u32[]{:S(2)}) collective-permute-start(bf16[16,1152]{1,0:T(8,128)(2,1)S(1)} %trunk.1.refs_0_), channel_id=1, source_target_pairs={{0,24},{8,0},{16,8},{24,16},{1,25},{9,1},{17,9},{25,17},{2,26},{10... | collective-permute-start | bytes 110600 | tf_op jit(solution)/shard_map/ppermute | solution.py:347
  32.2 0.5 %collective-permute-start.1 = (bf16[16,1152]{1,0:T(8,128)(2,1)S(1)}, bf16[16,1152]{1,0:T(8,128)(2,1)S(1)}, u32[]{:S(2)}, u32[]{:S(2)}) collective-permute-start(bf16[16,1152]{1,0:T(8,128)(2,1)S(1)} %trunk.1.refs_0_), channel_id=1, source_target_pairs={{0,16},{8,24},{16,0},{24,8},{1,17},{9,25},{17,1},{25,9},{2,18},{10... | collective-permute-start | bytes 110600 | tf_op jit(solution)/shard_map/ppermute | solution.py:347
  32.8 0.0 collective-permute-done.5.refs_3_
  32.8 0.0 collective-permute-start
  32.8 0.0 collective-permute-done.4.refs_2_
  32.8 0.0 collective-permute-done.3.refs_1_
  32.8 1.7 %factors.1 = (bf16[32,1024]{1,0:T(8,128)(2,1)S(1)}, f32[3,32,1024]{2,1,0:T(8,128)S(1)}, bf16[3,256,32]{2,1,0:T(8,128)(2,1)S(1)}, bf16[1024,1024]{1,0:T(8,128)(2,1)S(1)}, f32[1,1024]{1,0:T(1,128)S(1)}) custom-call(bf16[32,1024]{1,0:T(8,128)(2,1)S(1)} %get-tuple-element.24.refs_0_, bf16[32,1024]{1,0:T(8,128)(2,1)S(1)} %collective-permute-done.3.refs_1_, ...), custom_call_target="tpu_custom_call" | custom-call | flops 1048576 | bytes 4194304 | tf_op jit(solution)/shard_map/factors/pallas_call | solution.py:351
  34.5 0.0 collective-permute-done.2.refs_3_
  34.5 2.1 %collective-permute-done.1.refs_2_ = bf16[16,1152]{1,0:T(8,128)(2,1)S(1)} collective-permute-done((bf16[16,1152]{1,0:T(8,128)(2,1)S(1)}, bf16[16,1152]{1,0:T(8,128)(2,1)S(1)}, u32[]{:S(2)}, u32[]{:S(2)}) %collective-permute-start.1) | collective-permute-done | bytes 36896 | tf_op jit(solution)/shard_map/ppermute | solution.py:347
  36.6 0.0 collective-permute-done.refs_1_
  36.6 4.0 %tail.1 = (f32[3,256,1024]{2,1,0:T(8,128)}, f32[3,1024]{1,0:T(4,128)}, f32[3,1024]{1,0:T(4,128)}, f32[1,1024]{1,0:T(1,128)}, f32[1024,1024]{1,0:T(8,128)}, /*index=5*/f32[1,1024]{1,0:T(1,128)}) custom-call(bf16[16,1152]{1,0:T(8,128)(2,1)S(1)} %trunk.1.refs_0_, bf16[16,1152]{1,0:T(8,128)(2,1)S(1)} %collective-permute-done.refs_1_, ...), custom_call_target="tpu_custom_call" | custom-call | tf_op jit(solution)/shard_map/tail/pallas_call | solution.py:368
Async XLA Ops:
  22.8 10.0 %collective-permute-start.5 = (bf16[32,1024]{1,0:T(8,128)(2,1)S(1)}, bf16[32,1024]{1,0:T(8,128)(2,1)S(1)}, u32[]{:S(2)}, u32[]{:S(2)}) collective-permute-start(bf16[32,1024]{1,0:T(8,128)(2,1)S(1)} %get-tuple-element.24.refs_0_), channel_id=1, source_target_pairs={{0,24},{8,0},{16,8},{24,16},{1,25},{9,1},{17,9},{25,17},{2,26},{10... | collective-permute-start | bytes 196616 | tf_op jit(solution)/shard_map/ppermute | solution.py:347
  22.9 9.9 %collective-permute-start.4 = (bf16[32,1024]{1,0:T(8,128)(2,1)S(1)}, bf16[32,1024]{1,0:T(8,128)(2,1)S(1)}, u32[]{:S(2)}, u32[]{:S(2)}) collective-permute-start(bf16[32,1024]{1,0:T(8,128)(2,1)S(1)} %get-tuple-element.24.refs_0_), channel_id=1, source_target_pairs={{0,16},{8,24},{16,0},{24,8},{1,17},{9,25},{17,1},{25,9},{2,18},{10... | collective-permute-start | bytes 196616 | tf_op jit(solution)/shard_map/ppermute | solution.py:347
  24.4 8.4 %collective-permute-start.3 = (bf16[32,1024]{1,0:T(8,128)(2,1)S(1)}, bf16[32,1024]{1,0:T(8,128)(2,1)S(1)}, u32[]{:S(2)}, u32[]{:S(2)}) collective-permute-start(bf16[32,1024]{1,0:T(8,128)(2,1)S(1)} %get-tuple-element.24.refs_0_), channel_id=1, source_target_pairs={{0,8},{8,16},{16,24},{24,0},{1,9},{9,17},{17,25},{25,1},{2,10},{10... | collective-permute-start | bytes 196616 | tf_op jit(solution)/shard_map/ppermute | solution.py:347
  30.6 3.9 %collective-permute-start.2 = (bf16[16,1152]{1,0:T(8,128)(2,1)S(1)}, bf16[16,1152]{1,0:T(8,128)(2,1)S(1)}, u32[]{:S(2)}, u32[]{:S(2)}) collective-permute-start(bf16[16,1152]{1,0:T(8,128)(2,1)S(1)} %trunk.1.refs_0_), channel_id=1, source_target_pairs={{0,24},{8,0},{16,8},{24,16},{1,25},{9,1},{17,9},{25,17},{2,26},{10... | collective-permute-start | bytes 110600 | tf_op jit(solution)/shard_map/ppermute | solution.py:347
  32.2 4.3 %collective-permute-start.1 = (bf16[16,1152]{1,0:T(8,128)(2,1)S(1)}, bf16[16,1152]{1,0:T(8,128)(2,1)S(1)}, u32[]{:S(2)}, u32[]{:S(2)}) collective-permute-start(bf16[16,1152]{1,0:T(8,128)(2,1)S(1)} %trunk.1.refs_0_), channel_id=1, source_target_pairs={{0,16},{8,24},{16,0},{24,8},{1,17},{9,25},{17,1},{25,9},{2,18},{10... | collective-permute-start | bytes 110600 | tf_op jit(solution)/shard_map/ppermute | solution.py:347
  32.8 3.8 %collective-permute-start = (bf16[16,1152]{1,0:T(8,128)(2,1)S(1)}, bf16[16,1152]{1,0:T(8,128)(2,1)S(1)}, u32[]{:S(2)}, u32[]{:S(2)}) collective-permute-start(bf16[16,1152]{1,0:T(8,128)(2,1)S(1)} %trunk.1.refs_0_), channel_id=1, source_target_pairs={{0,8},{8,16},{16,24},{24,0},{1,9},{9,17},{17,25},{25,1},{2,10},{10... | collective-permute-start | bytes 110600 | tf_op jit(solution)/shard_map/ppermute | solution.py:347

commit v4 on v3

v4 whole, which is shorter than its diff:
```python
import functools

import jax
import jax.numpy as jnp
from jax import lax
from jax.experimental import pallas as pl
from jax.experimental.pallas import tpu as pltpu
from jax.sharding import PartitionSpec as P

BF = jnp.bfloat16
F32 = jnp.float32
MIB = 1 << 20
VMEM = pl.BlockSpec(memory_space=pltpu.VMEM)
HBM = pl.BlockSpec(memory_space=pltpu.HBM)


def up(value, step):
    return -(-value // step) * step


def pieces(value, count):
    out = []
    for _ in range(count):
        top = value.astype(BF)
        out.append(top)
        value = value - top.astype(F32)
    return out


def dot(a, b, dims=((1,), (0,))):
    return lax.dot_general(a, b, (dims, ((), ())), preferred_element_type=F32)


def stack(rows, count):
    have = sum(r.shape[0] for r in rows)
    if have < count:
        rows = rows + [jnp.zeros((count - have, rows[0].shape[1]), rows[0].dtype)]
    return jnp.concatenate(rows, axis=0)


def in_hbm(*arrays):
    return [pltpu.with_memory_space_constraint(a, pltpu.HBM) for a in arrays]


def first_layer(w1_ref, b1_ref):
    rows = [w1_ref[...].astype(F32)] + [b.astype(F32) for b in pieces(b1_ref[...], 3)]
    return stack(rows, up(w1_ref.shape[0] + 3, 8)).astype(BF)


def hidden_units(xyz, first):
    a = stack([xyz, jnp.ones((3, xyz.shape[1]), F32)], first.shape[0]).T.astype(BF)
    return jnp.tanh(dot(a, first)).astype(BF)


def fetch(sems, first, *pairs):
    copies = [pltpu.make_async_copy(src, dst, sems.at[first + i]) for i, (src, dst) in enumerate(pairs)]
    for copy in copies:
        copy.start()
    return copies


def wait(copies):
    for copy in copies:
        copy.wait()


LANES = 128


def plan(branches, sensor_count, dims, q, peers):
    row = branches * sensor_count // q
    cut = branches * (sensor_count // peers)
    side = 2 * q // LANES + up(cut, LANES) // LANES
    return row, up(max(row + dims + 1, side), 8)


def pack_kernel(
    row, sensors_hbm, coords_hbm, index_hbm, targets_hbm, out_ref, sensors_ref, coords_ref, index_ref, targets_ref, sems
):
    wait(fetch(
        sems, 0, (sensors_hbm, sensors_ref), (coords_hbm, coords_ref), (index_hbm, index_ref), (targets_hbm, targets_ref)
    ))
    peers, rows, _ = out_ref.shape
    q = coords_ref.shape[1]
    branches, sensor_count = sensors_ref.shape
    cut = sensor_count // peers
    s = sensors_ref[...].astype(F32)
    base = [s[k : k + 1, c : c + q] for k in range(branches) for c in range(0, sensor_count, q)]
    base += [coords_ref[...].astype(F32), index_ref[...].astype(F32)]
    base = stack(base, rows)
    targets = jnp.concatenate([t.astype(F32) for t in pieces(targets_ref[...], 2)], axis=1)
    targets = [targets[:, c : c + LANES] for c in range(0, 2 * q, LANES)]
    flat = up(branches * cut, LANES)
    for j in range(peers):
        line = [s[k : k + 1, j * cut : (j + 1) * cut] for k in range(branches)]
        if flat > branches * cut:
            line.append(jnp.zeros((1, flat - branches * cut), F32))
        line = jnp.concatenate(line, axis=1)
        side = stack(targets + [line[:, c : c + LANES] for c in range(0, flat, LANES)], rows)
        out_ref[j] = jnp.concatenate([base, side], axis=1).astype(BF)


def load_kernel(*refs):
    count = len(refs) // 2
    wait(fetch(refs[-1], 0, *zip(refs[:count], refs[count:-1])))


def latent_kernel(
    row, ahead,
    got_ref, turned_ref, bias_ref, w2_ref, b2_ref, w1_ref, b1_ref, w_hbm,
    early_ref, mixed_ref, offset_ref, *refs,
):
    w_ref, sems = refs[-2:]
    chunks = got_ref.shape[0]
    q = got_ref.shape[2] - LANES
    funcs = turned_ref.shape[1]
    branches, sensor_count, width = w_ref.shape
    dims = w1_ref.shape[0]
    parts = [(k, c) for k in range(branches) for c in range(0, sensor_count, q)]
    copies = fetch(sems, 0, *[(w_hbm.at[k, pl.ds(c, q)], w_ref.at[k, pl.ds(c, q)]) for k, c in parts])
    pre = [bias_ref[k : k + 1, :] for k in range(branches)]

    def multiply(i):
        k, c = parts[i]
        copies[i].wait()
        pre[k] = pre[k] + dot(turned_ref[i, :, :q], w_ref[k, c : c + q])

    done = 0
    if ahead:
        first = first_layer(w1_ref, b1_ref)
        for j in range(chunks):
            refs[0][j] = hidden_units(got_ref[j].astype(F32)[row : row + dims, :q], first)
            while done < len(parts) * max(j - 1, 0) // chunks:
                multiply(done)
                done += 1
    for i in range(done, len(parts)):
        multiply(i)
    lats = [jnp.tanh(p).astype(BF).astype(F32) for p in pre]
    product = (lats[0] * lats[1] * lats[2]).astype(BF)
    start = 2 * q // LANES
    flat = up(branches * sensor_count // chunks, LANES)
    lines = [turned_ref[start + c].astype(F32)[:, q:] for c in range(flat // LANES)]
    if flat < width:
        lines.append(jnp.zeros((funcs, width - flat), F32))
    early_ref[...] = jnp.concatenate(lats + [jnp.concatenate(lines, axis=1)], axis=0).astype(BF)
    offset = jnp.sum(product.astype(F32) * b2_ref[...], axis=1, keepdims=True)
    offset_ref[...] = jnp.broadcast_to(offset, offset_ref.shape)
    mixed_ref[...] = dot(product, w2_ref[...], ((1,), (1,)))


def trunk_kernel(
    row, dims, total_funcs, ahead,
    got_ref, mixed_ref, offset_ref, *refs,
):
    if ahead:
        h_ref, late_ref, g_ref, m_ref, r_ref, coef_ref = refs
    else:
        w1_ref, b1_ref, late_ref, g_ref, m_ref, r_ref, coef_ref, h_ref = refs
        first = first_layer(w1_ref, b1_ref)
    chunks = got_ref.shape[0]
    q = got_ref.shape[2] - LANES
    at_once = h_ref.shape[0]
    funcs, width = mixed_ref.shape
    scale = width ** (-0.5)
    mixed = jnp.concatenate(pieces(mixed_ref[...], 2), axis=0)
    offset = offset_ref[:, 0:1]
    place = lax.broadcasted_iota(jnp.int32, (funcs, q), 0).astype(F32)
    one = jnp.ones((), BF)
    g_ref[...] = jnp.zeros_like(g_ref)
    m_ref[...] = jnp.zeros_like(m_ref)
    r_ref[...] = jnp.zeros_like(r_ref)

    def residuals(j, slot):
        block = got_ref[j].astype(F32)
        xyz = block[row : row + dims, :q]
        owner = block[row + dims : row + dims + 1, :q]
        target = jnp.concatenate([block[c : c + 1, q:] for c in range(2 * q // LANES)], axis=1)
        target = target[:, :q] + target[:, q:]
        if not ahead:
            h_ref[slot] = hidden_units(xyz, first)
        scores = dot(mixed, h_ref[slot], ((1,), (1,)))
        scores = scores[:funcs] + scores[funcs:] + offset
        owned = (owner == place).astype(F32)
        pred = jnp.sum(owned * scores, axis=0, keepdims=True) * scale
        resid = (pred - target) / total_funcs
        coef = owned * (resid * scale)
        spread = jnp.concatenate([coef] + [coef * xyz[d : d + 1] for d in range(dims)], axis=0)
        coef_ref[slot] = jnp.concatenate(pieces(coef, 2) + pieces(spread, 2), axis=0)
        return coef

    def batch(start):
        r = r_ref[...]
        for slot in range(at_once):
            r = r + residuals(start + slot, slot)
        r_ref[...] = r
        g, m = g_ref[...], m_ref[...]
        for slot in range(at_once):
            h = h_ref[slot]
            g = g + dot(coef_ref[slot, : 2 * funcs], h)
            m = m + dot(coef_ref[slot, 2 * funcs :], (one - h) * (one + h))
        g_ref[...] = g
        m_ref[...] = m

    if chunks == at_once:
        batch(0)
    else:
        lax.fori_loop(0, chunks // at_once, lambda i, carry: (batch(i * at_once), carry)[1], 0)

    r = jnp.broadcast_to(jnp.sum(r_ref[...], axis=1, keepdims=True), (funcs, LANES))
    high, low = pieces(r, 2)
    lane = lax.broadcasted_iota(jnp.int32, r.shape, 1)
    r = jnp.where(lane < LANES // 2, high.astype(F32), low.astype(F32))
    half = (dims + 1) * funcs
    moments = m_ref[:half] + m_ref[half:]
    extra = late_ref.shape[1] - width - LANES
    grads = []
    for d in range(dims + 1):
        grad = jnp.sum(moments[d * funcs : (d + 1) * funcs] * mixed_ref[...], axis=0, keepdims=True)
        grads += [grad[:, c : c + extra] for c in range(0, grad.shape[1], extra)]
    late_ref[...] = jnp.concatenate([g_ref[:funcs] + g_ref[funcs:], r, stack(grads, funcs)], axis=1).astype(BF)


def factor_kernel(groups, funcs, *refs):
    earlies = refs[:groups]
    product_ref, factor_ref, turned_ref = refs[groups:]
    branches, cut, _ = turned_ref.shape
    early = [e[...].astype(F32) for e in earlies]

    def rows(first):
        return jnp.concatenate([p[first : first + funcs] for p in early], axis=0)

    lat = [rows(k * funcs) for k in range(branches)]
    product_ref[...] = (lat[0] * lat[1] * lat[2]).astype(BF)
    lines = rows(branches * funcs)
    for k in range(branches):
        others = [lat[j] for j in range(branches) if j != k]
        factor_ref[k] = others[0] * others[1] * (1.0 - lat[k] * lat[k])
        turned_ref[k] = lines[:, k * cut : (k + 1) * cut].T.astype(BF)


def tail_kernel(groups, funcs, dims, *refs):
    lates = refs[:groups]
    (
        product_ref, factor_ref, turned_ref, w2_ref, b2_ref,
        gbw_ref, gbb_ref, gw1_ref, gb1_ref, gw2_ref, gb2_ref, gbw_buf, gw2_buf, sems,
    ) = refs[groups:]
    width = w2_ref.shape[1]
    branches = gbw_ref.shape[0]
    late = [x[...].astype(F32) for x in lates]
    product = product_ref[...]
    g = jnp.concatenate([x[:, :width] for x in late], axis=0)
    r = jnp.concatenate([x[:, width : width + LANES] for x in late], axis=0)
    r = r[:, :1] + r[:, LANES // 2 : LANES // 2 + 1]
    copies = []
    blocks, height, _ = gw2_buf.shape
    for c in range(blocks):
        gw2_buf[c] = dot(g[:, c * height : (c + 1) * height].T.astype(BF), product)
        copies += fetch(sems, c, (gw2_buf.at[c], gw2_ref.at[pl.ds(c * height, height)]))
    dprod = dot(g.astype(BF), w2_ref[...]) + r * b2_ref[...]
    gbb = []
    for k in range(branches):
        delta = (dprod * factor_ref[k]).astype(BF)
        gbw_buf[k] = dot(turned_ref[k], delta)
        copies += fetch(sems, blocks + k, (gbw_buf.at[k], gbw_ref.at[k]))
        gbb.append(jnp.sum(delta.astype(F32), axis=0, keepdims=True))
    gbb_ref[...] = jnp.concatenate(gbb, axis=0)
    parts = late[0][:, width + LANES :]
    for x in late[1:]:
        parts = parts + x[:, width + LANES :]
    each = gw1_ref.shape[1] // parts.shape[1]
    grads = [
        jnp.concatenate([parts[d * each + c : d * each + c + 1] for c in range(each)], axis=1) for d in range(dims + 1)
    ]
    grads = jnp.concatenate(grads, axis=0)
    gb1_ref[...] = grads[:1]
    gw1_ref[...] = grads[1:]
    gb2_ref[...] = jnp.sum(r * product.astype(F32), axis=0, keepdims=True)
    wait(copies)


def shards(
    sensors, branch_w, branch_b, coords, func_index, targets, trunk_w1, trunk_b1, trunk_w2, trunk_b2
):
    branches, func_dev, sensor_count = sensors.shape
    dims, queries = coords.shape
    hidden, width = trunk_w2.shape
    nb, nq = lax.axis_size("branch"), lax.axis_size("query")
    assert func_dev == 1 and sensor_count % queries == 0 and hidden == width
    funcs = nq
    cut = sensor_count // nq
    row, rows = plan(branches, sensor_count, dims, queries, nq)
    ahead = nq * queries * hidden * 2 <= 16 * MIB
    units_shape = (nq if ahead else min(nq, 8), queries, hidden)

    packed = pl.pallas_call(
        functools.partial(pack_kernel, row),
        out_shape=jax.ShapeDtypeStruct((nq, rows, queries + LANES), BF),
        in_specs=[HBM] * 4,
        out_specs=VMEM,
        scratch_shapes=[
            pltpu.VMEM((branches, sensor_count), BF),
            pltpu.VMEM((dims, queries), BF),
            pltpu.VMEM((1, queries), jnp.int32),
            pltpu.VMEM((1, queries), F32),
            pltpu.SemaphoreType.DMA((4,)),
        ],
        compiler_params=pltpu.CompilerParams(vmem_limit_bytes=8 * MIB),
        name="pack",
    )(*in_hbm(sensors.reshape(branches, sensor_count), coords, func_index[None], targets[None]))
    got = lax.all_to_all(packed, "query", 0, 0, tiled=True)

    small = (branch_b, trunk_w2, trunk_b2[None], trunk_w1, trunk_b1[None])
    small = pl.pallas_call(
        load_kernel,
        out_shape=tuple(jax.ShapeDtypeStruct(x.shape, x.dtype) for x in small),
        in_specs=[HBM] * len(small),
        out_specs=(VMEM,) * len(small),
        scratch_shapes=[pltpu.SemaphoreType.DMA((len(small),))],
        compiler_params=pltpu.CompilerParams(vmem_limit_bytes=8 * MIB),
        cost_estimate=pl.CostEstimate(flops=0, bytes_accessed=4 * trunk_w2.size, transcendentals=0),
        name="load",
    )(*in_hbm(*small))
    early, mixed, offset, *units = pl.pallas_call(
        functools.partial(latent_kernel, row, ahead),
        out_shape=(
            jax.ShapeDtypeStruct(((branches + 1) * funcs, width), BF),
            jax.ShapeDtypeStruct((funcs, hidden), F32),
            jax.ShapeDtypeStruct((funcs, LANES), F32),
        ) + (jax.ShapeDtypeStruct(units_shape, BF),) * ahead,
        in_specs=[VMEM] * 7 + [HBM],
        out_specs=(VMEM,) * (3 + ahead),
        scratch_shapes=[
            pltpu.VMEM(branch_w.shape, BF),
            pltpu.SemaphoreType.DMA((row,)),
        ],
        compiler_params=pltpu.CompilerParams(vmem_limit_bytes=24 * MIB),
        cost_estimate=pl.CostEstimate(
            flops=2 * 256 * (nq * queries * hidden + branch_w.size), bytes_accessed=2 * branch_w.size, transcendentals=0
        ),
        name="latents",
    )(got, got.transpose(1, 0, 2), *small, *in_hbm(branch_w))

    needs = units if ahead else [trunk_w1, trunk_b1[None]]
    late_width = width + LANES + up(-(-(dims + 1) * hidden // funcs), LANES)
    late = pl.pallas_call(
        functools.partial(trunk_kernel, row, dims, nb * nq, ahead),
        out_shape=jax.ShapeDtypeStruct((funcs, late_width), BF),
        in_specs=[VMEM] * (3 + len(needs)),
        out_specs=VMEM,
        scratch_shapes=[
            pltpu.VMEM((2 * funcs, hidden), F32),
            pltpu.VMEM((2 * (dims + 1) * funcs, hidden), F32),
            pltpu.VMEM((funcs, queries), F32),
            pltpu.VMEM((units_shape[0], 2 * (dims + 2) * funcs, queries), BF),
        ] + [pltpu.VMEM(units_shape, BF)] * (not ahead),
        compiler_params=pltpu.CompilerParams(vmem_limit_bytes=24 * MIB),
        cost_estimate=pl.CostEstimate(
            flops=2 * 768 * nq * queries * hidden, bytes_accessed=2 * MIB, transcendentals=0
        ),
        name="trunk",
    )(got, mixed, offset, *needs)

    def gather(x):
        shifts = [[(i, (i + k) % nb) for i in range(nb)] for k in range(1, nb)]
        return [x] + [lax.ppermute(x, "branch", pairs) for pairs in shifts]

    earlies, lates = gather(early), gather(late)
    every = nb * funcs
    prepared = pl.pallas_call(
        functools.partial(factor_kernel, nb, funcs),
        out_shape=(
            jax.ShapeDtypeStruct((every, width), BF),
            jax.ShapeDtypeStruct((branches, every, width), F32),
            jax.ShapeDtypeStruct((branches, cut, every), BF),
        ),
        in_specs=[VMEM] * nb,
        out_specs=(VMEM,) * 3,
        compiler_params=pltpu.CompilerParams(vmem_limit_bytes=16 * MIB),
        cost_estimate=pl.CostEstimate(flops=MIB, bytes_accessed=4 * MIB, transcendentals=0),
        name="factors",
    )(*earlies)
    blocks = 4
    gbw, gbb, gw1, gb1, gw2, gb2 = pl.pallas_call(
        functools.partial(tail_kernel, nb, funcs, dims),
        out_shape=(
            jax.ShapeDtypeStruct((branches, cut, width), F32),
            jax.ShapeDtypeStruct((branches, width), F32),
            jax.ShapeDtypeStruct((dims, hidden), F32),
            jax.ShapeDtypeStruct((1, hidden), F32),
            jax.ShapeDtypeStruct((hidden, width), F32),
            jax.ShapeDtypeStruct((1, width), F32),
        ),
        in_specs=[VMEM] * (nb + 5),
        out_specs=(HBM, VMEM, VMEM, VMEM, HBM, VMEM),
        scratch_shapes=[
            pltpu.VMEM((branches, cut, width), F32),
            pltpu.VMEM((blocks, hidden // blocks, width), F32),
            pltpu.SemaphoreType.DMA((blocks + branches,)),
        ],
        compiler_params=pltpu.CompilerParams(vmem_limit_bytes=24 * MIB),
        name="tail",
    )(*lates, *prepared, small[1], small[2])
    return (gbw, gbb, gw1, gb1[0], gw2, gb2[0])


def solution(mesh):
    placed = (
        P(None, ("branch", "query"), None),
        P(),
        P(),
        P(None, ("branch", "query")),
        P(("branch", "query")),
        P(("branch", "query")),
        P(),
        P(),
        P(),
        P(),
    )
    return jax.shard_map(
        shards,
        mesh=mesh,
        in_specs=placed,
        out_specs=(P(None, "query", None), P(), P(), P(), P(), P()),
        check_vma=False,
    )
```

time: 40.9 us -> 39.6 us (0.968)
  blocking collectives: 15 us -> 0 us
  starting transfers between devices: 3.95 us -> 11.2 us
  waiting for transfers between devices: 2.07 us -> 9.26 us
  Pallas kernels: 18.8 us -> 18 us
    all_to_all x1 -> x0, blocking collectives: 15 us -> none  [shards(): got = lax.all_to_all(packed, 'query', 0, 0, tiled=True)]
    all_to_all x0 -> x1, starting transfers between devices: none -> 7.29 us  [shards(): got = lax.all_to_all(packed, 'query', 0, 0, tiled=True)]
    all_to_all x0 -> x1, waiting for transfers between devices: none -> 5.9 us  [shards(): got = lax.all_to_all(packed, 'query', 0, 0, tiled=True)]
    pallas_call x2 -> x3, Pallas kernels: 7.05 us -> 8.97 us  [the longest x1 5.85 us: shards(): pl.pallas_call(functools.partial(latent_kernel, row, ahead), out_shape=(j...]
    pallas_call x1, Pallas kernels: 1.69 us -> 0.19 us  [shards(): pl.pallas_call(functools.partial(factor_kernel, nb, funcs), out_shape=(ja...]
    ppermute x6, waiting for transfers between devices: 2.07 us -> 3.36 us  [gather(): return [x] + [lax.ppermute(x, 'branch', pairs) for pairs in shifts]]
    pallas_call x1, Pallas kernels: 6.03 us -> 4.85 us  [shards(): pl.pallas_call(functools.partial(trunk_kernel, row, dims, nb * nq, ahead)...]
  transfers between devices with their start and end apart: 6 -> 7, of which waited for: 1 -> 3; matrix products, arithmetic and copies ran while one was open for 0% -> 0% of each run, Pallas kernels for 19% -> 17%
where the time goes in v4:
time: 39.6 us; the launch traced here: 39.2 us
  Pallas kernels  18 us (45%)
  starting transfers between devices  11.2 us (28%)
  waiting for transfers between devices  9.26 us (23%)
  between operations  0.7 us (2%)
    all_to_all x1, starting transfers between devices, shards(): got = lax.all_to_all(packed, 'query', 0, 0, tiled=True)  7.29 us
    all_to_all x1, waiting for transfers between devices, shards(): got = lax.all_to_all(packed, 'query', 0, 0, tiled=True)  5.9 us
    pallas_call x1, Pallas kernels, shards(): pl.pallas_call(functools.partial(latent_kernel, row, ahead), out_shape=(j...  5.85 us
    pallas_call x1, Pallas kernels, shards(): pl.pallas_call(functools.partial(trunk_kernel, row, dims, nb * nq, ahead)...  4.85 us
    pallas_call x1, Pallas kernels, shards(): pl.pallas_call(functools.partial(tail_kernel, nb, funcs, dims), out_shape...  3.99 us
    ppermute x6, starting transfers between devices, gather(): return [x] + [lax.ppermute(x, 'branch', pairs) for pairs in shifts]  3.94 us
    ppermute x6, waiting for transfers between devices, gather(): return [x] + [lax.ppermute(x, 'branch', pairs) for pairs in shifts]  3.36 us
    pallas_call x1, Pallas kernels, shards(): pl.pallas_call(load_kernel, out_shape=tuple((jax.ShapeDtypeStruct(x.shape...  1.66 us
  transfers between devices with their start and end apart: 7, of which 3 were waited for; matrix products, arithmetic and copies ran while one was open for 0% of the time, Pallas kernels for 17%

profile of v4, /device:TPU:0, one launch (start us, length us, event | category | flops | bytes accessed | tf_op | source)
XLA Modules:
  0.0 39.2 jit_solution(17268727030137405846)
XLA Ops:
  0.6 1.5 %pack.1 = bf16[8,16,640]{2,1,0:T(8,128)(2,1)} custom-call(bf16[3,2048]{1,0:T(4,128)(2,1)} %bitcast.9, bf16[3,512]{1,0:T(4,128)(2,1)} %coords_hbm.1, s32[1,512]{1,0:T(1,128)} %bitcast.12, f32[1,512]{1,0:T(1,128)} %bitcast.13), custom_call_target="tpu_custom_call" | custom-call | tf_op jit(solution)/shard_map/pack/pallas_call | solution.py:295
  2.1 7.3 %all-to-all-start = ((bf16[8,16,640]{2,1,0:T(8,128)(2,1)}), bf16[8,16,640]{2,1,0:T(8,128)(2,1)S(1)}, u32[]{:S(2)}, u32[]{:S(2)}) async-start(bf16[8,16,640]{2,1,0:T(8,128)(2,1)} %pack.1), calls=%async_computation | async-start | bytes 327680 | tf_op jit(solution)/shard_map/all_to_all | solution.py:310
  9.4 1.7 %load.1 = (f32[3,1024]{1,0:T(4,128)S(1)}, bf16[1024,1024]{1,0:T(8,128)(2,1)S(1)}, f32[1,1024]{1,0:T(1,128)S(1)}, bf16[3,1024]{1,0:T(4,128)(2,1)S(1)}, f32[1,1024]{1,0:T(1,128)S(1)}) custom-call(f32[3,1024]{1,0:T(4,128)} %refs_0_.1, bf16[1024,1024]{1,0:T(8,128)(2,1)} %refs_1_.1, f32[1,1024]{1,0:T(1,128)} %bitcast.10, bf16[3,1024]{1,0:T(4,128)(2,1)} %refs_3_.1, ...), custom_call_target="tpu_custom_call" | custom-call | bytes 4194304 | tf_op jit(solution)/shard_map/load/pallas_call | solution.py:313
  11.1 5.9 %all-to-all-done.got_ref = bf16[8,16,640]{2,1,0:T(8,128)(2,1)S(1)} async-done(((bf16[8,16,640]{2,1,0:T(8,128)(2,1)}), bf16[8,16,640]{2,1,0:T(8,128)(2,1)S(1)}, u32[]{:S(2)}, u32[]{:S(2)}) %all-to-all-start) | async-done | bytes 163872 | tf_op jit(solution)/shard_map/all_to_all | solution.py:310
  17.0 5.8 %latents.1 = (bf16[32,1024]{1,0:T(8,128)(2,1)S(1)}, f32[8,1024]{1,0:T(8,128)S(1)}, f32[8,128]{1,0:T(8,128)S(1)}, bf16[8,512,1024]{2,1,0:T(8,128)(2,1)S(1)}) custom-call(bf16[8,16,640]{2,1,0:T(8,128)(2,1)S(1)} %all-to-all-done.got_ref, bf16[16,8,640]{2,1,0:T(8,128)(2,1)S(1)} %copy.16.turned_ref, f32[3,1024]{1,0:T(4,128)S(1)} %get-tuple-element.24.bias_ref, ...), custom_call_target="tpu_custom_call" | custom-call | flops 5368709120 | bytes 12582912 | tf_op jit(solution)/shard_map/latents/pallas_call | solution.py:323
  22.9 0.1 collective-permute-start.5
  22.9 1.6 %collective-permute-start.4 = (bf16[32,1024]{1,0:T(8,128)(2,1)S(1)}, bf16[32,1024]{1,0:T(8,128)(2,1)S(1)}, u32[]{:S(2)}, u32[]{:S(2)}) collective-permute-start(bf16[32,1024]{1,0:T(8,128)(2,1)S(1)} %get-tuple-element.32.refs_0_), channel_id=1, source_target_pairs={{0,16},{8,24},{16,0},{24,8},{1,17},{9,25},{17,1},{25,9},{2,18},{10... | collective-permute-start | bytes 196616 | tf_op jit(solution)/shard_map/ppermute | solution.py:365
  24.5 0.2 collective-permute-start.3
  24.6 4.9 %trunk.1.refs_0_ = bf16[8,1664]{1,0:T(8,128)(2,1)S(1)} custom-call(bf16[8,16,640]{2,1,0:T(8,128)(2,1)S(1)} %all-to-all-done.got_ref, f32[8,1024]{1,0:T(8,128)S(1)} %get-tuple-element.29.mixed_ref, f32[8,128]{1,0:T(8,128)S(1)} %get-tuple-element.30.offset_ref, bf16[8,512,1024]{2,1,0:T(8,128)(2,1)S(1)} %get-tuple-element.31.refs_0_), custom_call_target="tpu_custom_call" | custom-call | flops 6442450944 | bytes 2097152 | tf_op jit(solution)/shard_map/trunk/pallas_call | solution.py:345
  29.5 1.6 %collective-permute-start.2 = (bf16[8,1664]{1,0:T(8,128)(2,1)S(1)}, bf16[8,1664]{1,0:T(8,128)(2,1)S(1)}, u32[]{:S(2)}, u32[]{:S(2)}) collective-permute-start(bf16[8,1664]{1,0:T(8,128)(2,1)S(1)} %trunk.1.refs_0_), channel_id=1, source_target_pairs={{0,24},{8,0},{16,8},{24,16},{1,25},{9,1},{17,9},{25,17},{2,26},{10... | collective-permute-start | bytes 79880 | tf_op jit(solution)/shard_map/ppermute | solution.py:365
  31.1 0.5 %collective-permute-start.1 = (bf16[8,1664]{1,0:T(8,128)(2,1)S(1)}, bf16[8,1664]{1,0:T(8,128)(2,1)S(1)}, u32[]{:S(2)}, u32[]{:S(2)}) collective-permute-start(bf16[8,1664]{1,0:T(8,128)(2,1)S(1)} %trunk.1.refs_0_), channel_id=1, source_target_pairs={{0,16},{8,24},{16,0},{24,8},{1,17},{9,25},{17,1},{25,9},{2,18},{10... | collective-permute-start | bytes 79880 | tf_op jit(solution)/shard_map/ppermute | solution.py:365
  31.7 0.0 collective-permute-done.5.refs_3_
  31.7 0.0 collective-permute-start
  31.7 0.0 collective-permute-done.4.refs_2_
  31.7 0.0 collective-permute-done.3.refs_1_
  31.7 0.2 factors.1
  31.9 0.8 %collective-permute-done.2.refs_3_ = bf16[8,1664]{1,0:T(8,128)(2,1)S(1)} collective-permute-done((bf16[8,1664]{1,0:T(8,128)(2,1)S(1)}, bf16[8,1664]{1,0:T(8,128)(2,1)S(1)}, u32[]{:S(2)}, u32[]{:S(2)}) %collective-permute-start.2) | collective-permute-done | bytes 26656 | tf_op jit(solution)/shard_map/ppermute | solution.py:365
  32.7 2.6 %collective-permute-done.1.refs_2_ = bf16[8,1664]{1,0:T(8,128)(2,1)S(1)} collective-permute-done((bf16[8,1664]{1,0:T(8,128)(2,1)S(1)}, bf16[8,1664]{1,0:T(8,128)(2,1)S(1)}, u32[]{:S(2)}, u32[]{:S(2)}) %collective-permute-start.1) | collective-permute-done | bytes 26656 | tf_op jit(solution)/shard_map/ppermute | solution.py:365
  35.2 0.0 collective-permute-done.refs_1_
  35.2 4.0 %tail.1 = (f32[3,256,1024]{2,1,0:T(8,128)}, f32[3,1024]{1,0:T(4,128)}, f32[3,1024]{1,0:T(4,128)}, f32[1,1024]{1,0:T(1,128)}, f32[1024,1024]{1,0:T(8,128)}, /*index=5*/f32[1,1024]{1,0:T(1,128)}) custom-call(bf16[8,1664]{1,0:T(8,128)(2,1)S(1)} %trunk.1.refs_0_, bf16[8,1664]{1,0:T(8,128)(2,1)S(1)} %collective-permute-done.refs_1_, ...), custom_call_target="tpu_custom_call" | custom-call | tf_op jit(solution)/shard_map/tail/pallas_call | solution.py:383
  (1 shorter events, 0.0 us)
Async XLA Ops:
  2.1 14.9 %all-to-all-start = ((bf16[8,16,640]{2,1,0:T(8,128)(2,1)}), bf16[8,16,640]{2,1,0:T(8,128)(2,1)S(1)}, u32[]{:S(2)}, u32[]{:S(2)}) async-start(bf16[8,16,640]{2,1,0:T(8,128)(2,1)} %pack.1), calls=%async_computation | async-start | bytes 327680 | tf_op jit(solution)/shard_map/all_to_all | solution.py:310
  22.9 8.8 %collective-permute-start.5 = (bf16[32,1024]{1,0:T(8,128)(2,1)S(1)}, bf16[32,1024]{1,0:T(8,128)(2,1)S(1)}, u32[]{:S(2)}, u32[]{:S(2)}) collective-permute-start(bf16[32,1024]{1,0:T(8,128)(2,1)S(1)} %get-tuple-element.32.refs_0_), channel_id=1, source_target_pairs={{0,24},{8,0},{16,8},{24,16},{1,25},{9,1},{17,9},{25,17},{2,26},{10... | collective-permute-start | bytes 196616 | tf_op jit(solution)/shard_map/ppermute | solution.py:365
  22.9 8.8 %collective-permute-start.4 = (bf16[32,1024]{1,0:T(8,128)(2,1)S(1)}, bf16[32,1024]{1,0:T(8,128)(2,1)S(1)}, u32[]{:S(2)}, u32[]{:S(2)}) collective-permute-start(bf16[32,1024]{1,0:T(8,128)(2,1)S(1)} %get-tuple-element.32.refs_0_), channel_id=1, source_target_pairs={{0,16},{8,24},{16,0},{24,8},{1,17},{9,25},{17,1},{25,9},{2,18},{10... | collective-permute-start | bytes 196616 | tf_op jit(solution)/shard_map/ppermute | solution.py:365
  24.5 7.2 %collective-permute-start.3 = (bf16[32,1024]{1,0:T(8,128)(2,1)S(1)}, bf16[32,1024]{1,0:T(8,128)(2,1)S(1)}, u32[]{:S(2)}, u32[]{:S(2)}) collective-permute-start(bf16[32,1024]{1,0:T(8,128)(2,1)S(1)} %get-tuple-element.32.refs_0_), channel_id=1, source_target_pairs={{0,8},{8,16},{16,24},{24,0},{1,9},{9,17},{17,25},{25,1},{2,10},{10... | collective-permute-start | bytes 196616 | tf_op jit(solution)/shard_map/ppermute | solution.py:365
  29.5 3.2 %collective-permute-start.2 = (bf16[8,1664]{1,0:T(8,128)(2,1)S(1)}, bf16[8,1664]{1,0:T(8,128)(2,1)S(1)}, u32[]{:S(2)}, u32[]{:S(2)}) collective-permute-start(bf16[8,1664]{1,0:T(8,128)(2,1)S(1)} %trunk.1.refs_0_), channel_id=1, source_target_pairs={{0,24},{8,0},{16,8},{24,16},{1,25},{9,1},{17,9},{25,17},{2,26},{10... | collective-permute-start | bytes 79880 | tf_op jit(solution)/shard_map/ppermute | solution.py:365
  31.1 4.1 %collective-permute-start.1 = (bf16[8,1664]{1,0:T(8,128)(2,1)S(1)}, bf16[8,1664]{1,0:T(8,128)(2,1)S(1)}, u32[]{:S(2)}, u32[]{:S(2)}) collective-permute-start(bf16[8,1664]{1,0:T(8,128)(2,1)S(1)} %trunk.1.refs_0_), channel_id=1, source_target_pairs={{0,16},{8,24},{16,0},{24,8},{1,17},{9,25},{17,1},{25,9},{2,18},{10... | collective-permute-start | bytes 79880 | tf_op jit(solution)/shard_map/ppermute | solution.py:365
  31.7 3.6 %collective-permute-start = (bf16[8,1664]{1,0:T(8,128)(2,1)S(1)}, bf16[8,1664]{1,0:T(8,128)(2,1)S(1)}, u32[]{:S(2)}, u32[]{:S(2)}) collective-permute-start(bf16[8,1664]{1,0:T(8,128)(2,1)S(1)} %trunk.1.refs_0_), channel_id=1, source_target_pairs={{0,8},{8,16},{16,24},{24,0},{1,9},{9,17},{17,25},{25,1},{2,10},{10... | collective-permute-start | bytes 79880 | tf_op jit(solution)/shard_map/ppermute | solution.py:365

commit v5 on v4

--- a/solution.py
+++ b/solution.py
@@ -65,6 +65,7 @@
 
 
 LANES = 128
+BLOCKS = 8
 
 
 def plan(branches, sensor_count, dims, q, peers):
@@ -102,13 +103,18 @@
 
 def load_kernel(*refs):
     count = len(refs) // 2
-    wait(fetch(refs[-1], 0, *zip(refs[:count], refs[count:-1])))
+    pairs = list(zip(refs[: count - 1], refs[count:-2]))
+    w_hbm, begun_ref = refs[count - 1], refs[-2]
+    blocks, q, _ = begun_ref.shape
+    each = w_hbm.shape[1] // q
+    pairs += [(w_hbm.at[i // each, pl.ds(i % each * q, q)], begun_ref.at[i]) for i in range(blocks)]
+    wait(fetch(refs[-1], 0, *pairs))
 
 
 def latent_kernel(
     row, ahead,
-    got_ref, turned_ref, bias_ref, w2_ref, b2_ref, w1_ref, b1_ref, w_hbm,
-    early_ref, mixed_ref, offset_ref, *refs,
+    got_ref, turned_ref, bias_ref, b2_ref, w1_ref, b1_ref, begun_ref, w_hbm, w2_hbm,
+    early_ref, mixed_ref, offset_ref, w2_ref, *refs,
 ):
     w_ref, sems = refs[-2:]
     chunks = got_ref.shape[0]
@@ -117,20 +123,28 @@
     branches, sensor_count, width = w_ref.shape
     dims = w1_ref.shape[0]
     parts = [(k, c) for k in range(branches) for c in range(0, sensor_count, q)]
-    copies = fetch(sems, 0, *[(w_hbm.at[k, pl.ds(c, q)], w_ref.at[k, pl.ds(c, q)]) for k, c in parts])
+    begun = begun_ref.shape[0]
+    copies = fetch(
+        sems, 0, *[(w_hbm.at[k, pl.ds(c, q)], w_ref.at[k, pl.ds(c, q)]) for k, c in parts[begun:]], (w2_hbm, w2_ref)
+    )
     pre = [bias_ref[k : k + 1, :] for k in range(branches)]
 
     def multiply(i):
         k, c = parts[i]
-        copies[i].wait()
-        pre[k] = pre[k] + dot(turned_ref[i, :, :q], w_ref[k, c : c + q])
+        if i < begun:
+            block = begun_ref[i]
+        else:
+            copies[i - begun].wait()
+            block = w_ref[k, c : c + q]
+        pre[k] = pre[k] + dot(turned_ref[i, :, :q], block)
 
     done = 0
     if ahead:
         first = first_layer(w1_ref, b1_ref)
         for j in range(chunks):
             refs[0][j] = hidden_units(got_ref[j].astype(F32)[row : row + dims, :q], first)
-            while done < len(parts) * max(j - 1, 0) // chunks:
+            ready = begun + (len(parts) - begun) * max(j - 2, 0) // chunks
+            while done < ready:
                 multiply(done)
                 done += 1
     for i in range(done, len(parts)):
@@ -138,19 +152,18 @@
     lats = [jnp.tanh(p).astype(BF).astype(F32) for p in pre]
     product = (lats[0] * lats[1] * lats[2]).astype(BF)
     start = 2 * q // LANES
-    flat = up(branches * sensor_count // chunks, LANES)
+    flat = early_ref.shape[1] - branches * width
     lines = [turned_ref[start + c].astype(F32)[:, q:] for c in range(flat // LANES)]
-    if flat < width:
-        lines.append(jnp.zeros((funcs, width - flat), F32))
-    early_ref[...] = jnp.concatenate(lats + [jnp.concatenate(lines, axis=1)], axis=0).astype(BF)
+    early_ref[...] = jnp.concatenate(lats + lines, axis=1).astype(BF)
     offset = jnp.sum(product.astype(F32) * b2_ref[...], axis=1, keepdims=True)
     offset_ref[...] = jnp.broadcast_to(offset, offset_ref.shape)
+    copies[-1].wait()
     mixed_ref[...] = dot(product, w2_ref[...], ((1,), (1,)))
 
 
 def trunk_kernel(
     row, dims, total_funcs, ahead,
-    got_ref, mixed_ref, offset_ref, *refs,
+    got_ref, mixed_ref, offset_ref, early_ref, *refs,
 ):
     if ahead:
         h_ref, late_ref, g_ref, m_ref, r_ref, coef_ref = refs
@@ -212,69 +225,67 @@
     r = jnp.where(lane < LANES // 2, high.astype(F32), low.astype(F32))
     half = (dims + 1) * funcs
     moments = m_ref[:half] + m_ref[half:]
-    extra = late_ref.shape[1] - width - LANES
+    extra = late_ref.shape[1] - early_ref.shape[1] - width - LANES
     grads = []
     for d in range(dims + 1):
         grad = jnp.sum(moments[d * funcs : (d + 1) * funcs] * mixed_ref[...], axis=0, keepdims=True)
         grads += [grad[:, c : c + extra] for c in range(0, grad.shape[1], extra)]
-    late_ref[...] = jnp.concatenate([g_ref[:funcs] + g_ref[funcs:], r, stack(grads, funcs)], axis=1).astype(BF)
-
-
-def factor_kernel(groups, funcs, *refs):
-    earlies = refs[:groups]
-    product_ref, factor_ref, turned_ref = refs[groups:]
-    branches, cut, _ = turned_ref.shape
-    early = [e[...].astype(F32) for e in earlies]
-
-    def rows(first):
-        return jnp.concatenate([p[first : first + funcs] for p in early], axis=0)
-
-    lat = [rows(k * funcs) for k in range(branches)]
-    product_ref[...] = (lat[0] * lat[1] * lat[2]).astype(BF)
-    lines = rows(branches * funcs)
+    sums = jnp.concatenate([g_ref[:funcs] + g_ref[funcs:], r, stack(grads, funcs)], axis=1)
+    late_ref[:, : sums.shape[1]] = sums.astype(BF)
+    late_ref[:, sums.shape[1] :] = early_ref[...]
+
+
+def tail_kernel(groups, early_width, *refs):
+    w2_ref, b2_ref = refs[groups : groups + 2]
+    outs, bufs, sems = refs[groups + 2 : groups + 8], refs[groups + 8 : groups + 14], refs[-1]
+    gbw_ref, gbb_ref, gw1_ref, gb1_ref, gw2_ref, gb2_ref = bufs
+    width = w2_ref.shape[1]
+    branches, cut, _ = gbw_ref.shape
+    dims = gw1_ref.shape[0]
+    all_rows = [x[...].astype(F32) for x in refs[:groups]]
+    ends = all_rows[0].shape[1] - early_width
+    copies = []
+
+    def send(index, *at):
+        source, target = bufs[index], outs[index]
+        if at:
+            source, target = source.at[at], target.at[at]
+        copies.extend(fetch(sems, len(copies), (source, target)))
+
+    def columns(first, count):
+        return jnp.concatenate([x[:, first : first + count] for x in all_rows], axis=0)
+
+    lat = [columns(ends + k * width, width) for k in range(branches)]
+    product = (lat[0] * lat[1] * lat[2]).astype(BF)
+    g = columns(0, width).astype(BF)
+    height = gw2_ref.shape[0] // BLOCKS
+    for c in range(0, gw2_ref.shape[0], height):
+        gw2_ref[c : c + height] = dot(g[:, c : c + height], product, ((0,), (0,)))
+        send(4, pl.ds(c, height))
+    r = columns(width, LANES)
+    r = r[:, :1] + r[:, LANES // 2 : LANES // 2 + 1]
+    dprod = dot(g, w2_ref[...]) + r * b2_ref[...]
+    lines = columns(ends + branches * width, branches * cut)
+    gbb = []
     for k in range(branches):
         others = [lat[j] for j in range(branches) if j != k]
-        factor_ref[k] = others[0] * others[1] * (1.0 - lat[k] * lat[k])
-        turned_ref[k] = lines[:, k * cut : (k + 1) * cut].T.astype(BF)
-
-
-def tail_kernel(groups, funcs, dims, *refs):
-    lates = refs[:groups]
-    (
-        product_ref, factor_ref, turned_ref, w2_ref, b2_ref,
-        gbw_ref, gbb_ref, gw1_ref, gb1_ref, gw2_ref, gb2_ref, gbw_buf, gw2_buf, sems,
-    ) = refs[groups:]
-    width = w2_ref.shape[1]
-    branches = gbw_ref.shape[0]
-    late = [x[...].astype(F32) for x in lates]
-    product = product_ref[...]
-    g = jnp.concatenate([x[:, :width] for x in late], axis=0)
-    r = jnp.concatenate([x[:, width : width + LANES] for x in late], axis=0)
-    r = r[:, :1] + r[:, LANES // 2 : LANES // 2 + 1]
-    copies = []
-    blocks, height, _ = gw2_buf.shape
-    for c in range(blocks):
-        gw2_buf[c] = dot(g[:, c * height : (c + 1) * height].T.astype(BF), product)
-        copies += fetch(sems, c, (gw2_buf.at[c], gw2_ref.at[pl.ds(c * height, height)]))
-    dprod = dot(g.astype(BF), w2_ref[...]) + r * b2_ref[...]
-    gbb = []
-    for k in range(branches):
-        delta = (dprod * factor_ref[k]).astype(BF)
-        gbw_buf[k] = dot(turned_ref[k], delta)
-        copies += fetch(sems, blocks + k, (gbw_buf.at[k], gbw_ref.at[k]))
+        delta = (dprod * (others[0] * others[1] * (1.0 - lat[k] * lat[k]))).astype(BF)
+        gbw_ref[k] = dot(lines[:, k * cut : (k + 1) * cut].astype(BF), delta, ((0,), (0,)))
+        send(0, k)
         gbb.append(jnp.sum(delta.astype(F32), axis=0, keepdims=True))
     gbb_ref[...] = jnp.concatenate(gbb, axis=0)
-    parts = late[0][:, width + LANES :]
-    for x in late[1:]:
-        parts = parts + x[:, width + LANES :]
+    parts = all_rows[0][:, width + LANES : ends]
+    for x in all_rows[1:]:
+        parts = parts + x[:, width + LANES : ends]
     each = gw1_ref.shape[1] // parts.shape[1]
     grads = [
         jnp.concatenate([parts[d * each + c : d * each + c + 1] for c in range(each)], axis=1) for d in range(dims + 1)
     ]
-    grads = jnp.concatenate(grads, axis=0)
-    gb1_ref[...] = grads[:1]
-    gw1_ref[...] = grads[1:]
+    gb1_ref[...] = grads[0]
+    gw1_ref[...] = jnp.concatenate(grads[1:], axis=0)
     gb2_ref[...] = jnp.sum(r * product.astype(F32), axis=0, keepdims=True)
+    for index in (1, 2, 3, 5):
+        send(index)
     wait(copies)
 
 
@@ -309,43 +320,48 @@
     )(*in_hbm(sensors.reshape(branches, sensor_count), coords, func_index[None], targets[None]))
     got = lax.all_to_all(packed, "query", 0, 0, tiled=True)
 
-    small = (branch_b, trunk_w2, trunk_b2[None], trunk_w1, trunk_b1[None])
+    early_width = branches * width + up(branches * cut, LANES)
+    sums_width = width + LANES + up(-(-(dims + 1) * hidden // funcs), LANES)
+    begun = min(row, 3 * MIB // (2 * queries * width))
+
+    small = (branch_b, trunk_b2[None], trunk_w1, trunk_b1[None])
+    shapes = [jax.ShapeDtypeStruct(x.shape, x.dtype) for x in small]
     small = pl.pallas_call(
         load_kernel,
-        out_shape=tuple(jax.ShapeDtypeStruct(x.shape, x.dtype) for x in small),
-        in_specs=[HBM] * len(small),
-        out_specs=(VMEM,) * len(small),
-        scratch_shapes=[pltpu.SemaphoreType.DMA((len(small),))],
+        out_shape=(*shapes, jax.ShapeDtypeStruct((begun, queries, width), BF)),
+        in_specs=[HBM] * (len(small) + 1),
+        out_specs=(VMEM,) * (len(small) + 1),
+        scratch_shapes=[pltpu.SemaphoreType.DMA((len(small) + begun,))],
         compiler_params=pltpu.CompilerParams(vmem_limit_bytes=8 * MIB),
         cost_estimate=pl.CostEstimate(flops=0, bytes_accessed=4 * trunk_w2.size, transcendentals=0),
         name="load",
-    )(*in_hbm(*small))
-    early, mixed, offset, *units = pl.pallas_call(
+    )(*in_hbm(*small, branch_w))
+    early, mixed, offset, w2_here, *units = pl.pallas_call(
         functools.partial(latent_kernel, row, ahead),
         out_shape=(
-            jax.ShapeDtypeStruct(((branches + 1) * funcs, width), BF),
+            jax.ShapeDtypeStruct((funcs, early_width), BF),
             jax.ShapeDtypeStruct((funcs, hidden), F32),
             jax.ShapeDtypeStruct((funcs, LANES), F32),
+            jax.ShapeDtypeStruct((hidden, width), BF),
         ) + (jax.ShapeDtypeStruct(units_shape, BF),) * ahead,
-        in_specs=[VMEM] * 7 + [HBM],
-        out_specs=(VMEM,) * (3 + ahead),
+        in_specs=[VMEM] * 7 + [HBM] * 2,
+        out_specs=(VMEM,) * (4 + ahead),
         scratch_shapes=[
             pltpu.VMEM(branch_w.shape, BF),
-            pltpu.SemaphoreType.DMA((row,)),
+            pltpu.SemaphoreType.DMA((row - begun + 1,)),
         ],
         compiler_params=pltpu.CompilerParams(vmem_limit_bytes=24 * MIB),
         cost_estimate=pl.CostEstimate(
             flops=2 * 256 * (nq * queries * hidden + branch_w.size), bytes_accessed=2 * branch_w.size, transcendentals=0
         ),
         name="latents",
-    )(got, got.transpose(1, 0, 2), *small, *in_hbm(branch_w))
+    )(got, got.transpose(1, 0, 2), *small, *in_hbm(branch_w, trunk_w2))
 
     needs = units if ahead else [trunk_w1, trunk_b1[None]]
-    late_width = width + LANES + up(-(-(dims + 1) * hidden // funcs), LANES)
-    late = pl.pallas_call(
+    sums = pl.pallas_call(
         functools.partial(trunk_kernel, row, dims, nb * nq, ahead),
-        out_shape=jax.ShapeDtypeStruct((funcs, late_width), BF),
-        in_specs=[VMEM] * (3 + len(needs)),
+        out_shape=jax.ShapeDtypeStruct((funcs, sums_width + early_width), BF),
+        in_specs=[VMEM] * (4 + len(needs)),
         out_specs=VMEM,
         scratch_shapes=[
             pltpu.VMEM((2 * funcs, hidden), F32),
@@ -358,48 +374,37 @@
             flops=2 * 768 * nq * queries * hidden, bytes_accessed=2 * MIB, transcendentals=0
         ),
         name="trunk",
-    )(got, mixed, offset, *needs)
-
-    def gather(x):
-        shifts = [[(i, (i + k) % nb) for i in range(nb)] for k in range(1, nb)]
-        return [x] + [lax.ppermute(x, "branch", pairs) for pairs in shifts]
-
-    earlies, lates = gather(early), gather(late)
-    every = nb * funcs
-    prepared = pl.pallas_call(
-        functools.partial(factor_kernel, nb, funcs),
-        out_shape=(
-            jax.ShapeDtypeStruct((every, width), BF),
-            jax.ShapeDtypeStruct((branches, every, width), F32),
-            jax.ShapeDtypeStruct((branches, cut, every), BF),
-        ),
-        in_specs=[VMEM] * nb,
-        out_specs=(VMEM,) * 3,
-        compiler_params=pltpu.CompilerParams(vmem_limit_bytes=16 * MIB),
-        cost_estimate=pl.CostEstimate(flops=MIB, bytes_accessed=4 * MIB, transcendentals=0),
-        name="factors",
-    )(*earlies)
-    blocks = 4
+    )(got, mixed, offset, early, *needs)
+
+    def shift(x, k):
+        return lax.ppermute(x, "branch", [(i, (i + k) % nb) for i in range(nb)])
+
+    def swap(x):
+        return lax.ppermute(x, "branch", [(i, i ^ 1) for i in range(nb)])
+
+    if nb % 2:
+        every = [sums] + [shift(sums, k) for k in range(1, nb)]
+    else:
+        every = [sums] + [shift(sums, k) for k in range(2, nb, 2)]
+        every += [swap(x) for x in every]
+    outs = (
+        jax.ShapeDtypeStruct((branches, cut, width), F32),
+        jax.ShapeDtypeStruct((branches, width), F32),
+        jax.ShapeDtypeStruct((dims, hidden), F32),
+        jax.ShapeDtypeStruct((1, hidden), F32),
+        jax.ShapeDtypeStruct((hidden, width), F32),
+        jax.ShapeDtypeStruct((1, width), F32),
+    )
     gbw, gbb, gw1, gb1, gw2, gb2 = pl.pallas_call(
-        functools.partial(tail_kernel, nb, funcs, dims),
-        out_shape=(
-            jax.ShapeDtypeStruct((branches, cut, width), F32),
-            jax.ShapeDtypeStruct((branches, width), F32),
-            jax.ShapeDtypeStruct((dims, hidden), F32),
-            jax.ShapeDtypeStruct((1, hidden), F32),
-            jax.ShapeDtypeStruct((hidden, width), F32),
-            jax.ShapeDtypeStruct((1, width), F32),
-        ),
-        in_specs=[VMEM] * (nb + 5),
-        out_specs=(HBM, VMEM, VMEM, VMEM, HBM, VMEM),
-        scratch_shapes=[
-            pltpu.VMEM((branches, cut, width), F32),
-            pltpu.VMEM((blocks, hidden // blocks, width), F32),
-            pltpu.SemaphoreType.DMA((blocks + branches,)),
-        ],
+        functools.partial(tail_kernel, nb, early_width),
+        out_shape=outs,
+        in_specs=[VMEM] * (nb + 2),
+        out_specs=(HBM,) * len(outs),
+        scratch_shapes=[pltpu.VMEM(x.shape, F32) for x in outs]
+        + [pltpu.SemaphoreType.DMA((BLOCKS + branches + 4,))],
         compiler_params=pltpu.CompilerParams(vmem_limit_bytes=24 * MIB),
         name="tail",
-    )(*lates, *prepared, small[1], small[2])
+    )(*every, w2_here, small[1])
     return (gbw, gbb, gw1, gb1[0], gw2, gb2[0])
 
 

time: 39.6 us -> 37.2 us (0.939)
  starting transfers between devices: 11.2 us -> 8.85 us
  waiting for transfers between devices: 9.26 us -> 9.87 us
  Pallas kernels: 18 us -> 17.4 us
    ppermute x6 -> x3, starting transfers between devices: 3.94 us -> 1.56 us  [the longest x1 1.55 us: shift(): return lax.ppermute(x, 'branch', [(i, (i + k) % nb) for i in range(nb)])]
    ppermute x6 -> x3, waiting for transfers between devices: 3.36 us -> 4.3 us  [the longest x1 3.01 us: shift(): return lax.ppermute(x, 'branch', [(i, (i + k) % nb) for i in range(nb)])]
    pallas_call x3 -> x2, Pallas kernels: 5.83 us -> 5.36 us  [the longest x1 3.37 us: shards(): pl.pallas_call(functools.partial(tail_kernel, nb, early_width), out_shape...]
  transfers between devices with their start and end apart: 7 -> 4, of which waited for: 3 -> 3; matrix products, arithmetic and copies ran while one was open for 0% -> 0% of each run, Pallas kernels for 17% -> 5%
where the time goes in v5:
time: 37.2 us; the launch traced here: 36.8 us
  Pallas kernels  17.4 us (47%)
  waiting for transfers between devices  9.87 us (27%)
  starting transfers between devices  8.85 us (24%)
  between operations  0.67 us (2%)
    all_to_all x1, starting transfers between devices, shards(): got = lax.all_to_all(packed, 'query', 0, 0, tiled=True)  7.29 us
    pallas_call x1, Pallas kernels, shards(): pl.pallas_call(functools.partial(latent_kernel, row, ahead), out_shape=(j...  5.72 us
    all_to_all x1, waiting for transfers between devices, shards(): got = lax.all_to_all(packed, 'query', 0, 0, tiled=True)  5.57 us
    pallas_call x1, Pallas kernels, shards(): pl.pallas_call(functools.partial(trunk_kernel, row, dims, nb * nq, ahead)...  4.86 us
    pallas_call x1, Pallas kernels, shards(): pl.pallas_call(functools.partial(tail_kernel, nb, early_width), out_shape...  3.37 us
    ppermute x1, waiting for transfers between devices, shift(): return lax.ppermute(x, 'branch', [(i, (i + k) % nb) for i in range(nb)])  3.01 us
    pallas_call x1, Pallas kernels, shards(): pl.pallas_call(load_kernel, out_shape=(*shapes, jax.ShapeDtypeStruct((beg...  1.98 us
    ppermute x1, starting transfers between devices, shift(): return lax.ppermute(x, 'branch', [(i, (i + k) % nb) for i in range(nb)])  1.55 us
  transfers between devices with their start and end apart: 4, of which 3 were waited for; matrix products, arithmetic and copies ran while one was open for 0% of the time, Pallas kernels for 5%

profile of v5, /device:TPU:0, one launch (start us, length us, event | category | flops | bytes accessed | tf_op | source)
XLA Modules:
  0.0 36.8 jit_solution(13038422264313084606)
XLA Ops:
  0.6 1.5 %pack.1 = bf16[8,16,640]{2,1,0:T(8,128)(2,1)} custom-call(bf16[3,2048]{1,0:T(4,128)(2,1)} %bitcast.9, bf16[3,512]{1,0:T(4,128)(2,1)} %coords_hbm.1, s32[1,512]{1,0:T(1,128)} %bitcast.12, f32[1,512]{1,0:T(1,128)} %bitcast.13), custom_call_target="tpu_custom_call" | custom-call | tf_op jit(solution)/shard_map/pack/pallas_call | solution.py:306
  2.1 7.3 %all-to-all-start = ((bf16[8,16,640]{2,1,0:T(8,128)(2,1)}), bf16[8,16,640]{2,1,0:T(8,128)(2,1)S(1)}, u32[]{:S(2)}, u32[]{:S(2)}) async-start(bf16[8,16,640]{2,1,0:T(8,128)(2,1)} %pack.1), calls=%async_computation | async-start | bytes 327680 | tf_op jit(solution)/shard_map/all_to_all | solution.py:321
  9.4 2.0 %load.1 = (f32[3,1024]{1,0:T(4,128)S(1)}, f32[1,1024]{1,0:T(1,128)S(1)}, bf16[3,1024]{1,0:T(4,128)(2,1)S(1)}, f32[1,1024]{1,0:T(1,128)S(1)}, bf16[3,512,1024]{2,1,0:T(8,128)(2,1)S(1)}) custom-call(f32[3,1024]{1,0:T(4,128)} %refs_0_.1, f32[1,1024]{1,0:T(1,128)} %bitcast.10, bf16[3,1024]{1,0:T(4,128)(2,1)} %refs_2_.1, f32[1,1024]{1,0:T(1,128)} %bitcast.11, ...), custom_call_target="tpu_custom_call" | custom-call | bytes 4194304 | tf_op jit(solution)/shard_map/load/pallas_call | solution.py:329
  11.4 5.6 %all-to-all-done.got_ref = bf16[8,16,640]{2,1,0:T(8,128)(2,1)S(1)} async-done(((bf16[8,16,640]{2,1,0:T(8,128)(2,1)}), bf16[8,16,640]{2,1,0:T(8,128)(2,1)S(1)}, u32[]{:S(2)}, u32[]{:S(2)}) %all-to-all-start) | async-done | bytes 163872 | tf_op jit(solution)/shard_map/all_to_all | solution.py:321
  17.0 5.7 %latents.1 = (bf16[8,3840]{1,0:T(8,128)(2,1)S(1)}, f32[8,1024]{1,0:T(8,128)S(1)}, f32[8,128]{1,0:T(8,128)S(1)}, bf16[1024,1024]{1,0:T(8,128)(2,1)S(1)}, bf16[8,512,1024]{2,1,0:T(8,128)(2,1)S(1)}) custom-call(bf16[8,16,640]{2,1,0:T(8,128)(2,1)S(1)} %all-to-all-done.got_ref, bf16[16,8,640]{2,1,0:T(8,128)(2,1)S(1)} %copy.16.turned_ref, ...), custom_call_target="tpu_custom_call" | custom-call | flops 5368709120 | bytes 12582912 | tf_op jit(solution)/shard_map/latents/pallas_call | solution.py:339
  22.7 4.9 %trunk.1.refs_0_ = bf16[8,5504]{1,0:T(8,128)(2,1)S(1)} custom-call(bf16[8,16,640]{2,1,0:T(8,128)(2,1)S(1)} %all-to-all-done.got_ref, f32[8,1024]{1,0:T(8,128)S(1)} %get-tuple-element.27.mixed_ref, f32[8,128]{1,0:T(8,128)S(1)} %get-tuple-element.28.offset_ref, bf16[8,3840]{1,0:T(8,128)(2,1)S(1)} %get-tuple-element.29.early_ref, ...), custom_call_target="tpu_custom_call" | custom-call | flops 6442450944 | bytes 2097152 | tf_op jit(solution)/shard_map/trunk/pallas_call | solution.py:361
  27.6 1.6 %collective-permute-start = (bf16[8,5504]{1,0:T(8,128)(2,1)S(1)}, bf16[8,5504]{1,0:T(8,128)(2,1)S(1)}, u32[]{:S(2)}, u32[]{:S(2)}) collective-permute-start(bf16[8,5504]{1,0:T(8,128)(2,1)S(1)} %trunk.1.refs_0_), channel_id=1, source_target_pairs={{0,16},{8,24},{16,0},{24,8},{1,17},{9,25},{17,1},{25,9},{2,18},{10... | collective-permute-start | bytes 264200 | tf_op jit(solution)/shard_map/ppermute | solution.py:380
  29.2 0.0 collective-permute-start.1
  29.2 3.0 %collective-permute-done.refs_1_ = bf16[8,5504]{1,0:T(8,128)(2,1)S(1)} collective-permute-done((bf16[8,5504]{1,0:T(8,128)(2,1)S(1)}, bf16[8,5504]{1,0:T(8,128)(2,1)S(1)}, u32[]{:S(2)}, u32[]{:S(2)}) %collective-permute-start) | collective-permute-done | bytes 88096 | tf_op jit(solution)/shard_map/ppermute | solution.py:380
  32.2 0.0 collective-permute-start.2
  32.2 0.0 collective-permute-done.1.refs_2_
  32.2 1.3 %collective-permute-done.2.refs_3_ = bf16[8,5504]{1,0:T(8,128)(2,1)S(1)} collective-permute-done((bf16[8,5504]{1,0:T(8,128)(2,1)S(1)}, bf16[8,5504]{1,0:T(8,128)(2,1)S(1)}, u32[]{:S(2)}, u32[]{:S(2)}) %collective-permute-start.2) | collective-permute-done | bytes 88096 | tf_op jit(solution)/shard_map/ppermute | solution.py:383
  33.5 3.4 %tail.1 = (f32[3,256,1024]{2,1,0:T(8,128)}, f32[3,1024]{1,0:T(4,128)}, f32[3,1024]{1,0:T(4,128)}, f32[1,1024]{1,0:T(1,128)}, f32[1024,1024]{1,0:T(8,128)}, /*index=5*/f32[1,1024]{1,0:T(1,128)}) custom-call(bf16[8,5504]{1,0:T(8,128)(2,1)S(1)} %trunk.1.refs_0_, bf16[8,5504]{1,0:T(8,128)(2,1)S(1)} %collective-permute-done.refs_1_, ...), custom_call_target="tpu_custom_call" | custom-call | tf_op jit(solution)/shard_map/tail/pallas_call | solution.py:398
  (1 shorter events, 0.0 us)
Async XLA Ops:
  2.1 14.9 %all-to-all-start = ((bf16[8,16,640]{2,1,0:T(8,128)(2,1)}), bf16[8,16,640]{2,1,0:T(8,128)(2,1)S(1)}, u32[]{:S(2)}, u32[]{:S(2)}) async-start(bf16[8,16,640]{2,1,0:T(8,128)(2,1)} %pack.1), calls=%async_computation | async-start | bytes 327680 | tf_op jit(solution)/shard_map/all_to_all | solution.py:321
  27.6 4.6 %collective-permute-start = (bf16[8,5504]{1,0:T(8,128)(2,1)S(1)}, bf16[8,5504]{1,0:T(8,128)(2,1)S(1)}, u32[]{:S(2)}, u32[]{:S(2)}) collective-permute-start(bf16[8,5504]{1,0:T(8,128)(2,1)S(1)} %trunk.1.refs_0_), channel_id=1, source_target_pairs={{0,16},{8,24},{16,0},{24,8},{1,17},{9,25},{17,1},{25,9},{2,18},{10... | collective-permute-start | bytes 264200 | tf_op jit(solution)/shard_map/ppermute | solution.py:380
  29.2 3.0 %collective-permute-start.1 = (bf16[8,5504]{1,0:T(8,128)(2,1)S(1)}, bf16[8,5504]{1,0:T(8,128)(2,1)S(1)}, u32[]{:S(2)}, u32[]{:S(2)}) collective-permute-start(bf16[8,5504]{1,0:T(8,128)(2,1)S(1)} %trunk.1.refs_0_), channel_id=1, source_target_pairs={{0,8},{8,0},{16,24},{24,16},{1,9},{9,1},{17,25},{25,17},{2,10},{10... | collective-permute-start | bytes 264200 | tf_op jit(solution)/shard_map/ppermute | solution.py:383
  32.2 1.3 %collective-permute-start.2 = (bf16[8,5504]{1,0:T(8,128)(2,1)S(1)}, bf16[8,5504]{1,0:T(8,128)(2,1)S(1)}, u32[]{:S(2)}, u32[]{:S(2)}) collective-permute-start(bf16[8,5504]{1,0:T(8,128)(2,1)S(1)} %collective-permute-done.refs_1_), channel_id=1, source_target_pairs={{0,8},{8,0},{16,24},{24,16},{1,9},{9,1},{17,25},{25,17},{2,10},{10... | collective-permute-start | bytes 264200 | tf_op jit(solution)/shard_map/ppermute | solution.py:383

commit v6 on v5

--- a/solution.py
+++ b/solution.py
@@ -111,22 +111,26 @@
     wait(fetch(refs[-1], 0, *pairs))
 
 
-def latent_kernel(
-    row, ahead,
+def group_kernel(
+    row, total_funcs,
     got_ref, turned_ref, bias_ref, b2_ref, w1_ref, b1_ref, begun_ref, w_hbm, w2_hbm,
-    early_ref, mixed_ref, offset_ref, w2_ref, *refs,
+    out_ref, w2_ref,
+    h_ref, w_ref, g_ref, m_ref, r_ref, coef_ref, sems,
 ):
-    w_ref, sems = refs[-2:]
     chunks = got_ref.shape[0]
     q = got_ref.shape[2] - LANES
     funcs = turned_ref.shape[1]
     branches, sensor_count, width = w_ref.shape
-    dims = w1_ref.shape[0]
+    dims, hidden = w1_ref.shape
+    scale = width ** (-0.5)
+    at_once = h_ref.shape[0]
+    ahead = at_once == chunks
     parts = [(k, c) for k in range(branches) for c in range(0, sensor_count, q)]
     begun = begun_ref.shape[0]
     copies = fetch(
         sems, 0, *[(w_hbm.at[k, pl.ds(c, q)], w_ref.at[k, pl.ds(c, q)]) for k, c in parts[begun:]], (w2_hbm, w2_ref)
     )
+
     pre = [bias_ref[k : k + 1, :] for k in range(branches)]
 
     def multiply(i):
@@ -139,10 +143,10 @@
         pre[k] = pre[k] + dot(turned_ref[i, :, :q], block)
 
     done = 0
+    first = first_layer(w1_ref, b1_ref)
     if ahead:
-        first = first_layer(w1_ref, b1_ref)
         for j in range(chunks):
-            refs[0][j] = hidden_units(got_ref[j].astype(F32)[row : row + dims, :q], first)
+            h_ref[j] = hidden_units(got_ref[j].astype(F32)[row : row + dims, :q], first)
             ready = begun + (len(parts) - begun) * max(j - 2, 0) // chunks
             while done < ready:
                 multiply(done)
@@ -151,32 +155,11 @@
         multiply(i)
     lats = [jnp.tanh(p).astype(BF).astype(F32) for p in pre]
     product = (lats[0] * lats[1] * lats[2]).astype(BF)
-    start = 2 * q // LANES
-    flat = early_ref.shape[1] - branches * width
-    lines = [turned_ref[start + c].astype(F32)[:, q:] for c in range(flat // LANES)]
-    early_ref[...] = jnp.concatenate(lats + lines, axis=1).astype(BF)
     offset = jnp.sum(product.astype(F32) * b2_ref[...], axis=1, keepdims=True)
-    offset_ref[...] = jnp.broadcast_to(offset, offset_ref.shape)
     copies[-1].wait()
-    mixed_ref[...] = dot(product, w2_ref[...], ((1,), (1,)))
-
-
-def trunk_kernel(
-    row, dims, total_funcs, ahead,
-    got_ref, mixed_ref, offset_ref, early_ref, *refs,
-):
-    if ahead:
-        h_ref, late_ref, g_ref, m_ref, r_ref, coef_ref = refs
-    else:
-        w1_ref, b1_ref, late_ref, g_ref, m_ref, r_ref, coef_ref, h_ref = refs
-        first = first_layer(w1_ref, b1_ref)
-    chunks = got_ref.shape[0]
-    q = got_ref.shape[2] - LANES
-    at_once = h_ref.shape[0]
-    funcs, width = mixed_ref.shape
-    scale = width ** (-0.5)
-    mixed = jnp.concatenate(pieces(mixed_ref[...], 2), axis=0)
-    offset = offset_ref[:, 0:1]
+    mixed_full = dot(product, w2_ref[...], ((1,), (1,)))
+    mixed = jnp.concatenate(pieces(mixed_full, 2), axis=0)
+
     place = lax.broadcasted_iota(jnp.int32, (funcs, q), 0).astype(F32)
     one = jnp.ones((), BF)
     g_ref[...] = jnp.zeros_like(g_ref)
@@ -214,7 +197,7 @@
         g_ref[...] = g
         m_ref[...] = m
 
-    if chunks == at_once:
+    if ahead:
         batch(0)
     else:
         lax.fori_loop(0, chunks // at_once, lambda i, carry: (batch(i * at_once), carry)[1], 0)
@@ -225,14 +208,16 @@
     r = jnp.where(lane < LANES // 2, high.astype(F32), low.astype(F32))
     half = (dims + 1) * funcs
     moments = m_ref[:half] + m_ref[half:]
-    extra = late_ref.shape[1] - early_ref.shape[1] - width - LANES
+    extra = up(-(-(dims + 1) * hidden // funcs), LANES)
     grads = []
     for d in range(dims + 1):
-        grad = jnp.sum(moments[d * funcs : (d + 1) * funcs] * mixed_ref[...], axis=0, keepdims=True)
-        grads += [grad[:, c : c + extra] for c in range(0, grad.shape[1], extra)]
-    sums = jnp.concatenate([g_ref[:funcs] + g_ref[funcs:], r, stack(grads, funcs)], axis=1)
-    late_ref[:, : sums.shape[1]] = sums.astype(BF)
-    late_ref[:, sums.shape[1] :] = early_ref[...]
+        grad = jnp.sum(moments[d * funcs : (d + 1) * funcs] * mixed_full, axis=0, keepdims=True)
+        grads += [grad[:, c : c + extra] for c in range(0, hidden, extra)]
+    start = 2 * q // LANES
+    flat = out_ref.shape[1] - width - LANES - extra - branches * width
+    lines = [turned_ref[start + c].astype(F32)[:, q:] for c in range(flat // LANES)]
+    sums = [g_ref[:funcs] + g_ref[funcs:], r, stack(grads, funcs)]
+    out_ref[...] = jnp.concatenate(sums + lats + lines, axis=1).astype(BF)
 
 
 def tail_kernel(groups, early_width, *refs):
@@ -300,8 +285,8 @@
     funcs = nq
     cut = sensor_count // nq
     row, rows = plan(branches, sensor_count, dims, queries, nq)
-    ahead = nq * queries * hidden * 2 <= 16 * MIB
-    units_shape = (nq if ahead else min(nq, 8), queries, hidden)
+    at_once = nq if nq * queries * hidden * 2 <= 16 * MIB else 8
+    assert nq % at_once == 0
 
     packed = pl.pallas_call(
         functools.partial(pack_kernel, row),
@@ -336,45 +321,29 @@
         cost_estimate=pl.CostEstimate(flops=0, bytes_accessed=4 * trunk_w2.size, transcendentals=0),
         name="load",
     )(*in_hbm(*small, branch_w))
-    early, mixed, offset, w2_here, *units = pl.pallas_call(
-        functools.partial(latent_kernel, row, ahead),
+    sums, w2_here = pl.pallas_call(
+        functools.partial(group_kernel, row, nb * nq),
         out_shape=(
-            jax.ShapeDtypeStruct((funcs, early_width), BF),
-            jax.ShapeDtypeStruct((funcs, hidden), F32),
-            jax.ShapeDtypeStruct((funcs, LANES), F32),
+            jax.ShapeDtypeStruct((funcs, sums_width + early_width), BF),
             jax.ShapeDtypeStruct((hidden, width), BF),
-        ) + (jax.ShapeDtypeStruct(units_shape, BF),) * ahead,
+        ),
         in_specs=[VMEM] * 7 + [HBM] * 2,
-        out_specs=(VMEM,) * (4 + ahead),
+        out_specs=(VMEM,) * 2,
         scratch_shapes=[
+            pltpu.VMEM((at_once, queries, hidden), BF),
             pltpu.VMEM(branch_w.shape, BF),
-            pltpu.SemaphoreType.DMA((row - begun + 1,)),
-        ],
-        compiler_params=pltpu.CompilerParams(vmem_limit_bytes=24 * MIB),
-        cost_estimate=pl.CostEstimate(
-            flops=2 * 256 * (nq * queries * hidden + branch_w.size), bytes_accessed=2 * branch_w.size, transcendentals=0
-        ),
-        name="latents",
-    )(got, got.transpose(1, 0, 2), *small, *in_hbm(branch_w, trunk_w2))
-
-    needs = units if ahead else [trunk_w1, trunk_b1[None]]
-    sums = pl.pallas_call(
-        functools.partial(trunk_kernel, row, dims, nb * nq, ahead),
-        out_shape=jax.ShapeDtypeStruct((funcs, sums_width + early_width), BF),
-        in_specs=[VMEM] * (4 + len(needs)),
-        out_specs=VMEM,
-        scratch_shapes=[
             pltpu.VMEM((2 * funcs, hidden), F32),
             pltpu.VMEM((2 * (dims + 1) * funcs, hidden), F32),
             pltpu.VMEM((funcs, queries), F32),
-            pltpu.VMEM((units_shape[0], 2 * (dims + 2) * funcs, queries), BF),
-        ] + [pltpu.VMEM(units_shape, BF)] * (not ahead),
-        compiler_params=pltpu.CompilerParams(vmem_limit_bytes=24 * MIB),
+            pltpu.VMEM((at_once, 2 * (dims + 2) * funcs, queries), BF),
+            pltpu.SemaphoreType.DMA((row - begun + 1,)),
+        ],
+        compiler_params=pltpu.CompilerParams(vmem_limit_bytes=40 * MIB),
         cost_estimate=pl.CostEstimate(
-            flops=2 * 768 * nq * queries * hidden, bytes_accessed=2 * MIB, transcendentals=0
+            flops=2 * 1024 * nq * queries * hidden, bytes_accessed=2 * branch_w.size, transcendentals=0
         ),
-        name="trunk",
-    )(got, mixed, offset, early, *needs)
+        name="group",
+    )(got, got.transpose(1, 0, 2), *small, *in_hbm(branch_w, trunk_w2))
 
     def shift(x, k):
         return lax.ppermute(x, "branch", [(i, (i + k) % nb) for i in range(nb)])

time: 37.2 us -> 37 us (level)
    pallas_call x2 -> x1, Pallas kernels: 10.6 us -> 10.4 us  [shards(): pl.pallas_call(functools.partial(group_kernel, row, nb * nq), out_shape=(...]
where the time goes in v6:
time: 37 us; the launch traced here: 36.7 us
  Pallas kernels  17.3 us (47%)
  waiting for transfers between devices  9.87 us (27%)
  starting transfers between devices  8.85 us (24%)
  between operations  0.66 us (2%)
    pallas_call x1, Pallas kernels, shards(): pl.pallas_call(functools.partial(group_kernel, row, nb * nq), out_shape=(...  10.4 us
    all_to_all x1, starting transfers between devices, shards(): got = lax.all_to_all(packed, 'query', 0, 0, tiled=True)  7.29 us
    all_to_all x1, waiting for transfers between devices, shards(): got = lax.all_to_all(packed, 'query', 0, 0, tiled=True)  5.57 us
    pallas_call x1, Pallas kernels, shards(): pl.pallas_call(functools.partial(tail_kernel, nb, early_width), out_shape...  3.37 us
    ppermute x1, waiting for transfers between devices, shift(): return lax.ppermute(x, 'branch', [(i, (i + k) % nb) for i in range(nb)])  3.01 us
    pallas_call x1, Pallas kernels, shards(): pl.pallas_call(load_kernel, out_shape=(*shapes, jax.ShapeDtypeStruct((beg...  1.98 us
    ppermute x1, starting transfers between devices, shift(): return lax.ppermute(x, 'branch', [(i, (i + k) % nb) for i in range(nb)])  1.55 us
    pallas_call x1, Pallas kernels, shards(): pl.pallas_call(functools.partial(pack_kernel, row), out_shape=jax.ShapeDt...  1.47 us
  transfers between devices with their start and end apart: 4, of which 3 were waited for; matrix products, arithmetic and copies ran while one was open for 0% of the time, Pallas kernels for 5%

profile of v6, /device:TPU:0, one launch (start us, length us, event | category | flops | bytes accessed | tf_op | source)
XLA Modules:
  0.0 36.7 jit_solution(15584621466542781342)
XLA Ops:
  0.6 1.5 %pack.1 = bf16[8,16,640]{2,1,0:T(8,128)(2,1)} custom-call(bf16[3,2048]{1,0:T(4,128)(2,1)} %bitcast.11, bf16[3,512]{1,0:T(4,128)(2,1)} %coords_hbm.1, s32[1,512]{1,0:T(1,128)} %bitcast.14, f32[1,512]{1,0:T(1,128)} %bitcast.15), custom_call_target="tpu_custom_call" | custom-call | tf_op jit(solution)/shard_map/pack/pallas_call | solution.py:291
  2.1 7.3 %all-to-all-start = ((bf16[8,16,640]{2,1,0:T(8,128)(2,1)}), bf16[8,16,640]{2,1,0:T(8,128)(2,1)S(1)}, u32[]{:S(2)}, u32[]{:S(2)}) async-start(bf16[8,16,640]{2,1,0:T(8,128)(2,1)} %pack.1), calls=%async_computation | async-start | bytes 327680 | tf_op jit(solution)/shard_map/all_to_all | solution.py:306
  9.4 2.0 %load.1 = (f32[3,1024]{1,0:T(4,128)S(1)}, f32[1,1024]{1,0:T(1,128)S(1)}, bf16[3,1024]{1,0:T(4,128)(2,1)S(1)}, f32[1,1024]{1,0:T(1,128)S(1)}, bf16[3,512,1024]{2,1,0:T(8,128)(2,1)S(1)}) custom-call(f32[3,1024]{1,0:T(4,128)} %refs_0_.1, f32[1,1024]{1,0:T(1,128)} %bitcast.12, bf16[3,1024]{1,0:T(4,128)(2,1)} %refs_2_.1, f32[1,1024]{1,0:T(1,128)} %bitcast.13, ...), custom_call_target="tpu_custom_call" | custom-call | bytes 4194304 | tf_op jit(solution)/shard_map/load/pallas_call | solution.py:314
  11.4 5.6 %all-to-all-done.got_ref = bf16[8,16,640]{2,1,0:T(8,128)(2,1)S(1)} async-done(((bf16[8,16,640]{2,1,0:T(8,128)(2,1)}), bf16[8,16,640]{2,1,0:T(8,128)(2,1)S(1)}, u32[]{:S(2)}, u32[]{:S(2)}) %all-to-all-start) | async-done | bytes 163872 | tf_op jit(solution)/shard_map/all_to_all | solution.py:306
  17.0 10.4 %group.1 = (bf16[8,5504]{1,0:T(8,128)(2,1)S(1)}, bf16[1024,1024]{1,0:T(8,128)(2,1)S(1)}) custom-call(bf16[8,16,640]{2,1,0:T(8,128)(2,1)S(1)} %all-to-all-done.got_ref, bf16[16,8,640]{2,1,0:T(8,128)(2,1)S(1)} %bitcast.10, f32[3,1024]{1,0:T(4,128)S(1)} %get-tuple-element.19.bias_ref, f32[1,1024]{1,0:T(1,128)S(1)} %get-tuple-element.20.b2_ref.refs_5_, ...), custom_call_target="tpu_custom_call" | custom-call | flops 8589934592 | bytes 12582912 | tf_op jit(solution)/shard_map/group/pallas_call | solution.py:324
  27.4 1.6 %collective-permute-start = (bf16[8,5504]{1,0:T(8,128)(2,1)S(1)}, bf16[8,5504]{1,0:T(8,128)(2,1)S(1)}, u32[]{:S(2)}, u32[]{:S(2)}) collective-permute-start(bf16[8,5504]{1,0:T(8,128)(2,1)S(1)} %get-tuple-element.24.refs_0_), channel_id=1, source_target_pairs={{0,16},{8,24},{16,0},{24,8},{1,17},{9,25},{17,1},{25,9},{2,18},{10... | collective-permute-start | bytes 264200 | tf_op jit(solution)/shard_map/ppermute | solution.py:349
  29.0 0.0 collective-permute-start.1
  29.0 3.0 %collective-permute-done.refs_1_ = bf16[8,5504]{1,0:T(8,128)(2,1)S(1)} collective-permute-done((bf16[8,5504]{1,0:T(8,128)(2,1)S(1)}, bf16[8,5504]{1,0:T(8,128)(2,1)S(1)}, u32[]{:S(2)}, u32[]{:S(2)}) %collective-permute-start) | collective-permute-done | bytes 88096 | tf_op jit(solution)/shard_map/ppermute | solution.py:349
  32.0 0.0 collective-permute-start.2
  32.0 0.0 collective-permute-done.1.refs_2_
  32.0 1.3 %collective-permute-done.2.refs_3_ = bf16[8,5504]{1,0:T(8,128)(2,1)S(1)} collective-permute-done((bf16[8,5504]{1,0:T(8,128)(2,1)S(1)}, bf16[8,5504]{1,0:T(8,128)(2,1)S(1)}, u32[]{:S(2)}, u32[]{:S(2)}) %collective-permute-start.2) | collective-permute-done | bytes 88096 | tf_op jit(solution)/shard_map/ppermute | solution.py:352
  33.3 3.4 %tail.1 = (f32[3,256,1024]{2,1,0:T(8,128)}, f32[3,1024]{1,0:T(4,128)}, f32[3,1024]{1,0:T(4,128)}, f32[1,1024]{1,0:T(1,128)}, f32[1024,1024]{1,0:T(8,128)}, /*index=5*/f32[1,1024]{1,0:T(1,128)}) custom-call(bf16[8,5504]{1,0:T(8,128)(2,1)S(1)} %get-tuple-element.24.refs_0_, bf16[8,5504]{1,0:T(8,128)(2,1)S(1)} %collective-permute-done.refs_1_, ...), custom_call_target="tpu_custom_call" | custom-call | tf_op jit(solution)/shard_map/tail/pallas_call | solution.py:367
  (1 shorter events, 0.0 us)
Async XLA Ops:
  2.1 14.9 %all-to-all-start = ((bf16[8,16,640]{2,1,0:T(8,128)(2,1)}), bf16[8,16,640]{2,1,0:T(8,128)(2,1)S(1)}, u32[]{:S(2)}, u32[]{:S(2)}) async-start(bf16[8,16,640]{2,1,0:T(8,128)(2,1)} %pack.1), calls=%async_computation | async-start | bytes 327680 | tf_op jit(solution)/shard_map/all_to_all | solution.py:306
  27.4 4.6 %collective-permute-start = (bf16[8,5504]{1,0:T(8,128)(2,1)S(1)}, bf16[8,5504]{1,0:T(8,128)(2,1)S(1)}, u32[]{:S(2)}, u32[]{:S(2)}) collective-permute-start(bf16[8,5504]{1,0:T(8,128)(2,1)S(1)} %get-tuple-element.24.refs_0_), channel_id=1, source_target_pairs={{0,16},{8,24},{16,0},{24,8},{1,17},{9,25},{17,1},{25,9},{2,18},{10... | collective-permute-start | bytes 264200 | tf_op jit(solution)/shard_map/ppermute | solution.py:349
  29.0 3.0 %collective-permute-start.1 = (bf16[8,5504]{1,0:T(8,128)(2,1)S(1)}, bf16[8,5504]{1,0:T(8,128)(2,1)S(1)}, u32[]{:S(2)}, u32[]{:S(2)}) collective-permute-start(bf16[8,5504]{1,0:T(8,128)(2,1)S(1)} %get-tuple-element.24.refs_0_), channel_id=1, source_target_pairs={{0,8},{8,0},{16,24},{24,16},{1,9},{9,1},{17,25},{25,17},{2,10},{10... | collective-permute-start | bytes 264200 | tf_op jit(solution)/shard_map/ppermute | solution.py:352
  32.0 1.3 %collective-permute-start.2 = (bf16[8,5504]{1,0:T(8,128)(2,1)S(1)}, bf16[8,5504]{1,0:T(8,128)(2,1)S(1)}, u32[]{:S(2)}, u32[]{:S(2)}) collective-permute-start(bf16[8,5504]{1,0:T(8,128)(2,1)S(1)} %collective-permute-done.refs_1_), channel_id=1, source_target_pairs={{0,8},{8,0},{16,24},{24,16},{1,9},{9,1},{17,25},{25,17},{2,10},{10... | collective-permute-start | bytes 264200 | tf_op jit(solution)/shard_map/ppermute | solution.py:352

commit v7 on v6

--- a/solution.py
+++ b/solution.py
@@ -68,37 +68,33 @@
 BLOCKS = 8
 
 
-def plan(branches, sensor_count, dims, q, peers):
-    row = branches * sensor_count // q
-    cut = branches * (sensor_count // peers)
-    side = 2 * q // LANES + up(cut, LANES) // LANES
-    return row, up(max(row + dims + 1, side), 8)
-
-
-def pack_kernel(
-    row, sensors_hbm, coords_hbm, index_hbm, targets_hbm, out_ref, sensors_ref, coords_ref, index_ref, targets_ref, sems
-):
+def plan(branches, sensor_count, dims, q):
+    lines = branches * sensor_count // q
+    rows = up(-(-(lines + dims + 1) // 2), 8)
+    return lines, rows, 2 * q + LANES * -(-(2 * q // LANES) // rows)
+
+
+def line_of(block, i, q):
+    return block[i // 2 : i // 2 + 1, i % 2 * q : (i % 2 + 1) * q]
+
+
+def pack_kernel(sensors_hbm, coords_hbm, index_hbm, targets_hbm, out_ref, sensors_ref, coords_ref, index_ref, targets_ref, sems):
     wait(fetch(
         sems, 0, (sensors_hbm, sensors_ref), (coords_hbm, coords_ref), (index_hbm, index_ref), (targets_hbm, targets_ref)
     ))
-    peers, rows, _ = out_ref.shape
+    peers, rows, width = out_ref.shape
     q = coords_ref.shape[1]
-    branches, sensor_count = sensors_ref.shape
-    cut = sensor_count // peers
-    s = sensors_ref[...].astype(F32)
-    base = [s[k : k + 1, c : c + q] for k in range(branches) for c in range(0, sensor_count, q)]
-    base += [coords_ref[...].astype(F32), index_ref[...].astype(F32)]
-    base = stack(base, rows)
+    s, xyz = sensors_ref[...].astype(F32), coords_ref[...].astype(F32)
+    lines = [s[k : k + 1, c : c + q] for k in range(s.shape[0]) for c in range(0, s.shape[1], q)]
+    lines += [xyz[d : d + 1] for d in range(xyz.shape[0])] + [index_ref[...].astype(F32)]
+    lines += [jnp.zeros((1, q), F32)] * (2 * rows - len(lines))
+    main = jnp.concatenate([jnp.concatenate(lines[half::2], axis=0) for half in range(2)], axis=1)
     targets = jnp.concatenate([t.astype(F32) for t in pieces(targets_ref[...], 2)], axis=1)
     targets = [targets[:, c : c + LANES] for c in range(0, 2 * q, LANES)]
-    flat = up(branches * cut, LANES)
+    beside = [stack(targets[c : c + rows], rows) for c in range(0, len(targets), rows)]
+    block = jnp.concatenate([main] + beside, axis=1).astype(BF)
     for j in range(peers):
-        line = [s[k : k + 1, j * cut : (j + 1) * cut] for k in range(branches)]
-        if flat > branches * cut:
-            line.append(jnp.zeros((1, flat - branches * cut), F32))
-        line = jnp.concatenate(line, axis=1)
-        side = stack(targets + [line[:, c : c + LANES] for c in range(0, flat, LANES)], rows)
-        out_ref[j] = jnp.concatenate([base, side], axis=1).astype(BF)
+        out_ref[j] = block
 
 
 def load_kernel(*refs):
@@ -117,11 +113,12 @@
     out_ref, w2_ref,
     h_ref, w_ref, g_ref, m_ref, r_ref, coef_ref, sems,
 ):
-    chunks = got_ref.shape[0]
-    q = got_ref.shape[2] - LANES
+    chunks, rows, _ = got_ref.shape
+    q = begun_ref.shape[1]
     funcs = turned_ref.shape[1]
     branches, sensor_count, width = w_ref.shape
     dims, hidden = w1_ref.shape
+    cut = sensor_count // chunks
     scale = width ** (-0.5)
     at_once = h_ref.shape[0]
     ahead = at_once == chunks
@@ -133,6 +130,9 @@
 
     pre = [bias_ref[k : k + 1, :] for k in range(branches)]
 
+    def sensors(i):
+        return turned_ref[i // 2, :, i % 2 * q : (i % 2 + 1) * q]
+
     def multiply(i):
         k, c = parts[i]
         if i < begun:
@@ -140,19 +140,29 @@
         else:
             copies[i - begun].wait()
             block = w_ref[k, c : c + q]
-        pre[k] = pre[k] + dot(turned_ref[i, :, :q], block)
+        pre[k] = pre[k] + dot(sensors(i), block)
 
     done = 0
     first = first_layer(w1_ref, b1_ref)
+
+    def coords(block):
+        return jnp.concatenate([line_of(block, row + d, q) for d in range(dims)], axis=0)
+
+    def units(j):
+        h_ref[j] = hidden_units(coords(got_ref[j].astype(F32)), first)
+
+    held = 1 if ahead else 0
     if ahead:
-        for j in range(chunks):
-            h_ref[j] = hidden_units(got_ref[j].astype(F32)[row : row + dims, :q], first)
-            ready = begun + (len(parts) - begun) * max(j - 2, 0) // chunks
+        for j in range(chunks - held):
+            units(j)
+            ready = begun + (len(parts) - begun) * max(j - 1, 0) // chunks
             while done < ready:
                 multiply(done)
                 done += 1
     for i in range(done, len(parts)):
         multiply(i)
+    for j in range(chunks - held, chunks if ahead else 0):
+        units(j)
     lats = [jnp.tanh(p).astype(BF).astype(F32) for p in pre]
     product = (lats[0] * lats[1] * lats[2]).astype(BF)
     offset = jnp.sum(product.astype(F32) * b2_ref[...], axis=1, keepdims=True)
@@ -168,9 +178,13 @@
 
     def residuals(j, slot):
         block = got_ref[j].astype(F32)
-        xyz = block[row : row + dims, :q]
-        owner = block[row + dims : row + dims + 1, :q]
-        target = jnp.concatenate([block[c : c + 1, q:] for c in range(2 * q // LANES)], axis=1)
+        xyz = coords(block)
+        owner = line_of(block, row + dims, q)
+        target = [
+            block[c % rows : c % rows + 1, 2 * q + c // rows * LANES : 2 * q + (c // rows + 1) * LANES]
+            for c in range(2 * q // LANES)
+        ]
+        target = jnp.concatenate(target, axis=1)
         target = target[:, :q] + target[:, q:]
         if not ahead:
             h_ref[slot] = hidden_units(xyz, first)
@@ -213,11 +227,19 @@
     for d in range(dims + 1):
         grad = jnp.sum(moments[d * funcs : (d + 1) * funcs] * mixed_full, axis=0, keepdims=True)
         grads += [grad[:, c : c + extra] for c in range(0, hidden, extra)]
-    start = 2 * q // LANES
+    me = lax.axis_index("query")
+    columns = []
+    for k in range(branches):
+        mine = jnp.zeros((funcs, cut), F32)
+        for j in range(chunks):
+            line, at = divmod(k * sensor_count + j * cut, q)
+            mine = jnp.where(me == j, sensors(line)[:, at : at + cut].astype(F32), mine)
+        columns.append(mine)
     flat = out_ref.shape[1] - width - LANES - extra - branches * width
-    lines = [turned_ref[start + c].astype(F32)[:, q:] for c in range(flat // LANES)]
+    if flat > branches * cut:
+        columns.append(jnp.zeros((funcs, flat - branches * cut), F32))
     sums = [g_ref[:funcs] + g_ref[funcs:], r, stack(grads, funcs)]
-    out_ref[...] = jnp.concatenate(sums + lats + lines, axis=1).astype(BF)
+    out_ref[...] = jnp.concatenate(sums + lats + columns, axis=1).astype(BF)
 
 
 def tail_kernel(groups, early_width, *refs):
@@ -281,16 +303,16 @@
     dims, queries = coords.shape
     hidden, width = trunk_w2.shape
     nb, nq = lax.axis_size("branch"), lax.axis_size("query")
-    assert func_dev == 1 and sensor_count % queries == 0 and hidden == width
+    assert func_dev == 1 and hidden == width and sensor_count % queries == 0 and queries % (sensor_count // nq) == 0
     funcs = nq
     cut = sensor_count // nq
-    row, rows = plan(branches, sensor_count, dims, queries, nq)
+    row, rows, packed_width = plan(branches, sensor_count, dims, queries)
     at_once = nq if nq * queries * hidden * 2 <= 16 * MIB else 8
     assert nq % at_once == 0
 
     packed = pl.pallas_call(
-        functools.partial(pack_kernel, row),
-        out_shape=jax.ShapeDtypeStruct((nq, rows, queries + LANES), BF),
+        pack_kernel,
+        out_shape=jax.ShapeDtypeStruct((nq, rows, packed_width), BF),
         in_specs=[HBM] * 4,
         out_specs=VMEM,
         scratch_shapes=[

time: 37 us -> 36.9 us (level)
  no operation moved by 1% of the time
where the time goes in v7:
time: 36.9 us; the launch traced here: 36.5 us
  Pallas kernels  17.2 us (47%)
  waiting for transfers between devices  9.75 us (26%)
  starting transfers between devices  8.86 us (24%)
  between operations  0.66 us (2%)
    pallas_call x1, Pallas kernels, shards(): pl.pallas_call(functools.partial(group_kernel, row, nb * nq), out_shape=(...  10.4 us
    all_to_all x1, starting transfers between devices, shards(): got = lax.all_to_all(packed, 'query', 0, 0, tiled=True)  7.29 us
    all_to_all x1, waiting for transfers between devices, shards(): got = lax.all_to_all(packed, 'query', 0, 0, tiled=True)  5.46 us
    pallas_call x1, Pallas kernels, shards(): pl.pallas_call(functools.partial(tail_kernel, nb, early_width), out_shape...  3.37 us
    ppermute x1, waiting for transfers between devices, shift(): return lax.ppermute(x, 'branch', [(i, (i + k) % nb) for i in range(nb)])  3.01 us
    pallas_call x1, Pallas kernels, shards(): pl.pallas_call(load_kernel, out_shape=(*shapes, jax.ShapeDtypeStruct((beg...  1.98 us
    ppermute x1, starting transfers between devices, shift(): return lax.ppermute(x, 'branch', [(i, (i + k) % nb) for i in range(nb)])  1.56 us
    pallas_call x1, Pallas kernels, shards(): pl.pallas_call(pack_kernel, out_shape=jax.ShapeDtypeStruct((nq, rows, pac...  1.46 us
  transfers between devices with their start and end apart: 4, of which 3 were waited for; matrix products, arithmetic and copies ran while one was open for 0% of the time, Pallas kernels for 5%

profile of v7, /device:TPU:0, one launch (start us, length us, event | category | flops | bytes accessed | tf_op | source)
XLA Modules:
  0.0 36.5 jit_solution(3528956261225963841)
XLA Ops:
  0.6 1.5 %pack.1 = bf16[8,8,1152]{2,1,0:T(8,128)(2,1)} custom-call(bf16[3,2048]{1,0:T(4,128)(2,1)} %bitcast.11, bf16[3,512]{1,0:T(4,128)(2,1)} %coords_hbm.1, s32[1,512]{1,0:T(1,128)} %bitcast.14, f32[1,512]{1,0:T(1,128)} %bitcast.15), custom_call_target="tpu_custom_call" | custom-call | tf_op jit(solution)/shard_map/pack/pallas_call | solution.py:313
  2.1 7.3 %all-to-all-start = ((bf16[8,8,1152]{2,1,0:T(8,128)(2,1)}), bf16[8,8,1152]{2,1,0:T(8,128)(2,1)S(1)}, u32[]{:S(2)}, u32[]{:S(2)}) async-start(bf16[8,8,1152]{2,1,0:T(8,128)(2,1)} %pack.1), calls=%async_computation | async-start | bytes 294912 | tf_op jit(solution)/shard_map/all_to_all | solution.py:328
  9.4 2.0 %load.1 = (f32[3,1024]{1,0:T(4,128)S(1)}, f32[1,1024]{1,0:T(1,128)S(1)}, bf16[3,1024]{1,0:T(4,128)(2,1)S(1)}, f32[1,1024]{1,0:T(1,128)S(1)}, bf16[3,512,1024]{2,1,0:T(8,128)(2,1)S(1)}) custom-call(f32[3,1024]{1,0:T(4,128)} %refs_0_.1, f32[1,1024]{1,0:T(1,128)} %bitcast.12, bf16[3,1024]{1,0:T(4,128)(2,1)} %refs_2_.1, f32[1,1024]{1,0:T(1,128)} %bitcast.13, ...), custom_call_target="tpu_custom_call" | custom-call | bytes 4194304 | tf_op jit(solution)/shard_map/load/pallas_call | solution.py:336
  11.4 5.5 %all-to-all-done.got_ref = bf16[8,8,1152]{2,1,0:T(8,128)(2,1)S(1)} async-done(((bf16[8,8,1152]{2,1,0:T(8,128)(2,1)}), bf16[8,8,1152]{2,1,0:T(8,128)(2,1)S(1)}, u32[]{:S(2)}, u32[]{:S(2)}) %all-to-all-start) | async-done | bytes 147488 | tf_op jit(solution)/shard_map/all_to_all | solution.py:328
  16.9 10.4 %group.1 = (bf16[8,5504]{1,0:T(8,128)(2,1)S(1)}, bf16[1024,1024]{1,0:T(8,128)(2,1)S(1)}) custom-call(bf16[8,8,1152]{2,1,0:T(8,128)(2,1)S(1)} %all-to-all-done.got_ref, bf16[8,8,1152]{2,1,0:T(8,128)(2,1)S(1)} %bitcast.10, f32[3,1024]{1,0:T(4,128)S(1)} %get-tuple-element.19.bias_ref, f32[1,1024]{1,0:T(1,128)S(1)} %get-tuple-element.20.b2_ref.refs_5_, ...), custom_call_target="tpu_custom_call" | custom-call | flops 8589934592 | bytes 12582912 | tf_op jit(solution)/shard_map/group/pallas_call | solution.py:346
  27.3 1.6 %collective-permute-start = (bf16[8,5504]{1,0:T(8,128)(2,1)S(1)}, bf16[8,5504]{1,0:T(8,128)(2,1)S(1)}, u32[]{:S(2)}, u32[]{:S(2)}) collective-permute-start(bf16[8,5504]{1,0:T(8,128)(2,1)S(1)} %get-tuple-element.24.refs_0_), channel_id=1, source_target_pairs={{0,16},{8,24},{16,0},{24,8},{1,17},{9,25},{17,1},{25,9},{2,18},{10... | collective-permute-start | bytes 264200 | tf_op jit(solution)/shard_map/ppermute | solution.py:371
  28.8 0.0 collective-permute-start.1
  28.8 3.0 %collective-permute-done.refs_1_ = bf16[8,5504]{1,0:T(8,128)(2,1)S(1)} collective-permute-done((bf16[8,5504]{1,0:T(8,128)(2,1)S(1)}, bf16[8,5504]{1,0:T(8,128)(2,1)S(1)}, u32[]{:S(2)}, u32[]{:S(2)}) %collective-permute-start) | collective-permute-done | bytes 88096 | tf_op jit(solution)/shard_map/ppermute | solution.py:371
  31.9 0.0 collective-permute-start.2
  31.9 0.0 collective-permute-done.1.refs_2_
  31.9 1.3 %collective-permute-done.2.refs_3_ = bf16[8,5504]{1,0:T(8,128)(2,1)S(1)} collective-permute-done((bf16[8,5504]{1,0:T(8,128)(2,1)S(1)}, bf16[8,5504]{1,0:T(8,128)(2,1)S(1)}, u32[]{:S(2)}, u32[]{:S(2)}) %collective-permute-start.2) | collective-permute-done | bytes 88096 | tf_op jit(solution)/shard_map/ppermute | solution.py:374
  33.1 3.4 %tail.1 = (f32[3,256,1024]{2,1,0:T(8,128)}, f32[3,1024]{1,0:T(4,128)}, f32[3,1024]{1,0:T(4,128)}, f32[1,1024]{1,0:T(1,128)}, f32[1024,1024]{1,0:T(8,128)}, /*index=5*/f32[1,1024]{1,0:T(1,128)}) custom-call(bf16[8,5504]{1,0:T(8,128)(2,1)S(1)} %get-tuple-element.24.refs_0_, bf16[8,5504]{1,0:T(8,128)(2,1)S(1)} %collective-permute-done.refs_1_, ...), custom_call_target="tpu_custom_call" | custom-call | tf_op jit(solution)/shard_map/tail/pallas_call | solution.py:389
  (1 shorter events, 0.0 us)
Async XLA Ops:
  2.1 14.7 %all-to-all-start = ((bf16[8,8,1152]{2,1,0:T(8,128)(2,1)}), bf16[8,8,1152]{2,1,0:T(8,128)(2,1)S(1)}, u32[]{:S(2)}, u32[]{:S(2)}) async-start(bf16[8,8,1152]{2,1,0:T(8,128)(2,1)} %pack.1), calls=%async_computation | async-start | bytes 294912 | tf_op jit(solution)/shard_map/all_to_all | solution.py:328
  27.3 4.6 %collective-permute-start = (bf16[8,5504]{1,0:T(8,128)(2,1)S(1)}, bf16[8,5504]{1,0:T(8,128)(2,1)S(1)}, u32[]{:S(2)}, u32[]{:S(2)}) collective-permute-start(bf16[8,5504]{1,0:T(8,128)(2,1)S(1)} %get-tuple-element.24.refs_0_), channel_id=1, source_target_pairs={{0,16},{8,24},{16,0},{24,8},{1,17},{9,25},{17,1},{25,9},{2,18},{10... | collective-permute-start | bytes 264200 | tf_op jit(solution)/shard_map/ppermute | solution.py:371
  28.8 3.0 %collective-permute-start.1 = (bf16[8,5504]{1,0:T(8,128)(2,1)S(1)}, bf16[8,5504]{1,0:T(8,128)(2,1)S(1)}, u32[]{:S(2)}, u32[]{:S(2)}) collective-permute-start(bf16[8,5504]{1,0:T(8,128)(2,1)S(1)} %get-tuple-element.24.refs_0_), channel_id=1, source_target_pairs={{0,8},{8,0},{16,24},{24,16},{1,9},{9,1},{17,25},{25,17},{2,10},{10... | collective-permute-start | bytes 264200 | tf_op jit(solution)/shard_map/ppermute | solution.py:374
  31.9 1.3 %collective-permute-start.2 = (bf16[8,5504]{1,0:T(8,128)(2,1)S(1)}, bf16[8,5504]{1,0:T(8,128)(2,1)S(1)}, u32[]{:S(2)}, u32[]{:S(2)}) collective-permute-start(bf16[8,5504]{1,0:T(8,128)(2,1)S(1)} %collective-permute-done.refs_1_), channel_id=1, source_target_pairs={{0,8},{8,0},{16,24},{24,16},{1,9},{9,1},{17,25},{25,17},{2,10},{10... | collective-permute-start | bytes 264200 | tf_op jit(solution)/shard_map/ppermute | solution.py:374

commit v8 on v7

--- a/solution.py
+++ b/solution.py
@@ -78,10 +78,10 @@
     return block[i // 2 : i // 2 + 1, i % 2 * q : (i % 2 + 1) * q]
 
 
-def pack_kernel(sensors_hbm, coords_hbm, index_hbm, targets_hbm, out_ref, sensors_ref, coords_ref, index_ref, targets_ref, sems):
-    wait(fetch(
-        sems, 0, (sensors_hbm, sensors_ref), (coords_hbm, coords_ref), (index_hbm, index_ref), (targets_hbm, targets_ref)
-    ))
+def pack_kernel(*refs):
+    count = len(refs) // 2 - 1
+    out_ref, (sensors_ref, coords_ref, index_ref, targets_ref, sems) = refs[count], refs[-5:]
+    wait(fetch(sems, 0, *zip(refs[:4], refs[-5:-1]), *zip(refs[4:count], refs[count + 1 : -5])))
     peers, rows, width = out_ref.shape
     q = coords_ref.shape[1]
     s, xyz = sensors_ref[...].astype(F32), coords_ref[...].astype(F32)
@@ -97,24 +97,14 @@
         out_ref[j] = block
 
 
-def load_kernel(*refs):
-    count = len(refs) // 2
-    pairs = list(zip(refs[: count - 1], refs[count:-2]))
-    w_hbm, begun_ref = refs[count - 1], refs[-2]
-    blocks, q, _ = begun_ref.shape
-    each = w_hbm.shape[1] // q
-    pairs += [(w_hbm.at[i // each, pl.ds(i % each * q, q)], begun_ref.at[i]) for i in range(blocks)]
-    wait(fetch(refs[-1], 0, *pairs))
-
-
 def group_kernel(
     row, total_funcs,
-    got_ref, turned_ref, bias_ref, b2_ref, w1_ref, b1_ref, begun_ref, w_hbm, w2_hbm,
+    got_ref, turned_ref, bias_ref, b2_ref, w1_ref, b1_ref, w_hbm, w2_hbm,
     out_ref, w2_ref,
     h_ref, w_ref, g_ref, m_ref, r_ref, coef_ref, sems,
 ):
     chunks, rows, _ = got_ref.shape
-    q = begun_ref.shape[1]
+    q = h_ref.shape[1]
     funcs = turned_ref.shape[1]
     branches, sensor_count, width = w_ref.shape
     dims, hidden = w1_ref.shape
@@ -123,9 +113,8 @@
     at_once = h_ref.shape[0]
     ahead = at_once == chunks
     parts = [(k, c) for k in range(branches) for c in range(0, sensor_count, q)]
-    begun = begun_ref.shape[0]
     copies = fetch(
-        sems, 0, *[(w_hbm.at[k, pl.ds(c, q)], w_ref.at[k, pl.ds(c, q)]) for k, c in parts[begun:]], (w2_hbm, w2_ref)
+        sems, 0, *[(w_hbm.at[k, pl.ds(c, q)], w_ref.at[k, pl.ds(c, q)]) for k, c in parts], (w2_hbm, w2_ref)
     )
 
     pre = [bias_ref[k : k + 1, :] for k in range(branches)]
@@ -135,12 +124,8 @@
 
     def multiply(i):
         k, c = parts[i]
-        if i < begun:
-            block = begun_ref[i]
-        else:
-            copies[i - begun].wait()
-            block = w_ref[k, c : c + q]
-        pre[k] = pre[k] + dot(sensors(i), block)
+        copies[i].wait()
+        pre[k] = pre[k] + dot(sensors(i), w_ref[k, c : c + q])
 
     done = 0
     first = first_layer(w1_ref, b1_ref)
@@ -155,7 +140,7 @@
     if ahead:
         for j in range(chunks - held):
             units(j)
-            ready = begun + (len(parts) - begun) * max(j - 1, 0) // chunks
+            ready = len(parts) * max(j - 1, 0) // chunks
             while done < ready:
                 multiply(done)
                 done += 1
@@ -310,46 +295,36 @@
     at_once = nq if nq * queries * hidden * 2 <= 16 * MIB else 8
     assert nq % at_once == 0
 
-    packed = pl.pallas_call(
+    small = (branch_b, trunk_b2[None], trunk_w1, trunk_b1[None])
+    packed, *small_here = pl.pallas_call(
         pack_kernel,
-        out_shape=jax.ShapeDtypeStruct((nq, rows, packed_width), BF),
-        in_specs=[HBM] * 4,
-        out_specs=VMEM,
+        out_shape=(
+            jax.ShapeDtypeStruct((nq, rows, packed_width), BF),
+            *[jax.ShapeDtypeStruct(x.shape, x.dtype) for x in small],
+        ),
+        in_specs=[HBM] * (4 + len(small)),
+        out_specs=(VMEM,) * (1 + len(small)),
         scratch_shapes=[
             pltpu.VMEM((branches, sensor_count), BF),
             pltpu.VMEM((dims, queries), BF),
             pltpu.VMEM((1, queries), jnp.int32),
             pltpu.VMEM((1, queries), F32),
-            pltpu.SemaphoreType.DMA((4,)),
+            pltpu.SemaphoreType.DMA((4 + len(small),)),
         ],
         compiler_params=pltpu.CompilerParams(vmem_limit_bytes=8 * MIB),
         name="pack",
-    )(*in_hbm(sensors.reshape(branches, sensor_count), coords, func_index[None], targets[None]))
+    )(*in_hbm(sensors.reshape(branches, sensor_count), coords, func_index[None], targets[None], *small))
     got = lax.all_to_all(packed, "query", 0, 0, tiled=True)
 
     early_width = branches * width + up(branches * cut, LANES)
     sums_width = width + LANES + up(-(-(dims + 1) * hidden // funcs), LANES)
-    begun = min(row, 3 * MIB // (2 * queries * width))
-
-    small = (branch_b, trunk_b2[None], trunk_w1, trunk_b1[None])
-    shapes = [jax.ShapeDtypeStruct(x.shape, x.dtype) for x in small]
-    small = pl.pallas_call(
-        load_kernel,
-        out_shape=(*shapes, jax.ShapeDtypeStruct((begun, queries, width), BF)),
-        in_specs=[HBM] * (len(small) + 1),
-        out_specs=(VMEM,) * (len(small) + 1),
-        scratch_shapes=[pltpu.SemaphoreType.DMA((len(small) + begun,))],
-        compiler_params=pltpu.CompilerParams(vmem_limit_bytes=8 * MIB),
-        cost_estimate=pl.CostEstimate(flops=0, bytes_accessed=4 * trunk_w2.size, transcendentals=0),
-        name="load",
-    )(*in_hbm(*small, branch_w))
     sums, w2_here = pl.pallas_call(
         functools.partial(group_kernel, row, nb * nq),
         out_shape=(
             jax.ShapeDtypeStruct((funcs, sums_width + early_width), BF),
             jax.ShapeDtypeStruct((hidden, width), BF),
         ),
-        in_specs=[VMEM] * 7 + [HBM] * 2,
+        in_specs=[VMEM] * 6 + [HBM] * 2,
         out_specs=(VMEM,) * 2,
         scratch_shapes=[
             pltpu.VMEM((at_once, queries, hidden), BF),
@@ -358,14 +333,14 @@
             pltpu.VMEM((2 * (dims + 1) * funcs, hidden), F32),
             pltpu.VMEM((funcs, queries), F32),
             pltpu.VMEM((at_once, 2 * (dims + 2) * funcs, queries), BF),
-            pltpu.SemaphoreType.DMA((row - begun + 1,)),
+            pltpu.SemaphoreType.DMA((row + 1,)),
         ],
         compiler_params=pltpu.CompilerParams(vmem_limit_bytes=40 * MIB),
         cost_estimate=pl.CostEstimate(
             flops=2 * 1024 * nq * queries * hidden, bytes_accessed=2 * branch_w.size, transcendentals=0
         ),
         name="group",
-    )(got, got.transpose(1, 0, 2), *small, *in_hbm(branch_w, trunk_w2))
+    )(got, got.transpose(1, 0, 2), *small_here, *in_hbm(branch_w, trunk_w2))
 
     def shift(x, k):
         return lax.ppermute(x, "branch", [(i, (i + k) % nb) for i in range(nb)])
@@ -395,7 +370,7 @@
         + [pltpu.SemaphoreType.DMA((BLOCKS + branches + 4,))],
         compiler_params=pltpu.CompilerParams(vmem_limit_bytes=24 * MIB),
         name="tail",
-    )(*every, w2_here, small[1])
+    )(*every, w2_here, small_here[1])
     return (gbw, gbb, gw1, gb1[0], gw2, gb2[0])
 
 

time: 36.9 us -> 36.7 us (level)
  blocking collectives: 0 us -> 14.5 us
  starting transfers between devices: 8.86 us -> 1.56 us
  waiting for transfers between devices: 9.75 us -> 4.29 us
  Pallas kernels: 17.2 us -> 15.3 us
    all_to_all x0 -> x1, blocking collectives: none -> 14.5 us  [shards(): got = lax.all_to_all(packed, 'query', 0, 0, tiled=True)]
    all_to_all x1 -> x0, starting transfers between devices: 7.29 us -> none  [shards(): got = lax.all_to_all(packed, 'query', 0, 0, tiled=True)]
    all_to_all x1 -> x0, waiting for transfers between devices: 5.46 us -> none  [shards(): got = lax.all_to_all(packed, 'query', 0, 0, tiled=True)]
    pallas_call x2 -> x1, Pallas kernels: 3.44 us -> 0.91 us  [shards(): pl.pallas_call(pack_kernel, out_shape=(jax.ShapeDtypeStruct((nq, rows, pa...]
    pallas_call x1, Pallas kernels: 10.4 us -> 11 us  [shards(): pl.pallas_call(functools.partial(group_kernel, row, nb * nq), out_shape=(...]
  transfers between devices with their start and end apart: 4 -> 3, of which waited for: 3 -> 2; matrix products, arithmetic and copies ran while one was open for 0% -> 0% of each run, Pallas kernels for 5% -> 0%
where the time goes in v8:
time: 36.7 us; the launch traced here: 36.4 us
  Pallas kernels  15.3 us (42%)
  blocking collectives  14.5 us (40%)
  waiting for transfers between devices  4.29 us (12%)
  starting transfers between devices  1.56 us (4%)
  between operations  0.66 us (2%)
    all_to_all x1, blocking collectives, shards(): got = lax.all_to_all(packed, 'query', 0, 0, tiled=True)  14.5 us
    pallas_call x1, Pallas kernels, shards(): pl.pallas_call(functools.partial(group_kernel, row, nb * nq), out_shape=(...  11 us
    pallas_call x1, Pallas kernels, shards(): pl.pallas_call(functools.partial(tail_kernel, nb, early_width), out_shape...  3.37 us
    ppermute x1, waiting for transfers between devices, shift(): return lax.ppermute(x, 'branch', [(i, (i + k) % nb) for i in range(nb)])  3.01 us
    ppermute x1, starting transfers between devices, shift(): return lax.ppermute(x, 'branch', [(i, (i + k) % nb) for i in range(nb)])  1.56 us
    ppermute x2, waiting for transfers between devices, swap(): return lax.ppermute(x, 'branch', [(i, i ^ 1) for i in range(nb)])  1.28 us
    pallas_call x1, Pallas kernels, shards(): pl.pallas_call(pack_kernel, out_shape=(jax.ShapeDtypeStruct((nq, rows, pa...  0.91 us
  transfers between devices with their start and end apart: 3, of which 2 were waited for; matrix products, arithmetic and copies ran while one was open for 0% of the time, Pallas kernels for 0%

profile of v8, /device:TPU:0, one launch (start us, length us, event | category | flops | bytes accessed | tf_op | source)
XLA Modules:
  0.0 36.4 jit_solution(11558529584013252263)
XLA Ops:
  0.6 0.9 %pack.1 = (bf16[8,8,1152]{2,1,0:T(8,128)(2,1)S(1)}, f32[3,1024]{1,0:T(4,128)S(1)}, f32[1,1024]{1,0:T(1,128)S(1)}, bf16[3,1024]{1,0:T(4,128)(2,1)S(1)}, f32[1,1024]{1,0:T(1,128)S(1)}) custom-call(bf16[3,2048]{1,0:T(4,128)(2,1)} %bitcast.11, bf16[3,512]{1,0:T(4,128)(2,1)} %refs_1_.1, s32[1,512]{1,0:T(1,128)} %bitcast.14, f32[1,512]{1,0:T(1,128)} %bitcast.15, ...), custom_call_target="tpu_custom_call" | custom-call | tf_op jit(solution)/shard_map/pack/pallas_call | solution.py:299
  1.6 14.5 %all_to_all.5.got_ref = bf16[8,8,1152]{2,1,0:T(8,128)(2,1)S(1)} all-to-all(bf16[8,8,1152]{2,1,0:T(8,128)(2,1)S(1)} %get-tuple-element.19), channel_id=1, replica_groups=mesh['branch'=4,'query'=8] {'query'}, dimensions={0} | all-to-all | bytes 294912 | tf_op jit(solution)/shard_map/all_to_all | solution.py:317
  16.1 11.0 %group.1 = (bf16[8,5504]{1,0:T(8,128)(2,1)S(1)}, bf16[1024,1024]{1,0:T(8,128)(2,1)S(1)}) custom-call(bf16[8,8,1152]{2,1,0:T(8,128)(2,1)S(1)} %all_to_all.5.got_ref, bf16[8,8,1152]{2,1,0:T(8,128)(2,1)S(1)} %bitcast.10, f32[3,1024]{1,0:T(4,128)S(1)} %get-tuple-element.20.bias_ref, f32[1,1024]{1,0:T(1,128)S(1)} %get-tuple-element.21.b2_ref.refs_5_, ...), custom_call_target="tpu_custom_call" | custom-call | flops 8589934592 | bytes 12582912 | tf_op jit(solution)/shard_map/group/pallas_call | solution.py:321
  27.2 1.6 %collective-permute-start = (bf16[8,5504]{1,0:T(8,128)(2,1)S(1)}, bf16[8,5504]{1,0:T(8,128)(2,1)S(1)}, u32[]{:S(2)}, u32[]{:S(2)}) collective-permute-start(bf16[8,5504]{1,0:T(8,128)(2,1)S(1)} %get-tuple-element.24.refs_0_), channel_id=1, source_target_pairs={{0,16},{8,24},{16,0},{24,8},{1,17},{9,25},{17,1},{25,9},{2,18},{10... | collective-permute-start | bytes 264200 | tf_op jit(solution)/shard_map/ppermute | solution.py:346
  28.7 0.0 collective-permute-start.1
  28.7 3.0 %collective-permute-done.refs_1_ = bf16[8,5504]{1,0:T(8,128)(2,1)S(1)} collective-permute-done((bf16[8,5504]{1,0:T(8,128)(2,1)S(1)}, bf16[8,5504]{1,0:T(8,128)(2,1)S(1)}, u32[]{:S(2)}, u32[]{:S(2)}) %collective-permute-start) | collective-permute-done | bytes 88096 | tf_op jit(solution)/shard_map/ppermute | solution.py:346
  31.7 0.0 collective-permute-start.2
  31.7 0.0 collective-permute-done.1.refs_2_
  31.7 1.3 %collective-permute-done.2.refs_3_ = bf16[8,5504]{1,0:T(8,128)(2,1)S(1)} collective-permute-done((bf16[8,5504]{1,0:T(8,128)(2,1)S(1)}, bf16[8,5504]{1,0:T(8,128)(2,1)S(1)}, u32[]{:S(2)}, u32[]{:S(2)}) %collective-permute-start.2) | collective-permute-done | bytes 88096 | tf_op jit(solution)/shard_map/ppermute | solution.py:349
  33.0 3.4 %tail.1 = (f32[3,256,1024]{2,1,0:T(8,128)}, f32[3,1024]{1,0:T(4,128)}, f32[3,1024]{1,0:T(4,128)}, f32[1,1024]{1,0:T(1,128)}, f32[1024,1024]{1,0:T(8,128)}, /*index=5*/f32[1,1024]{1,0:T(1,128)}) custom-call(bf16[8,5504]{1,0:T(8,128)(2,1)S(1)} %get-tuple-element.24.refs_0_, bf16[8,5504]{1,0:T(8,128)(2,1)S(1)} %collective-permute-done.refs_1_, ...), custom_call_target="tpu_custom_call" | custom-call | tf_op jit(solution)/shard_map/tail/pallas_call | solution.py:364
  (1 shorter events, 0.0 us)
Async XLA Ops:
  27.2 4.6 %collective-permute-start = (bf16[8,5504]{1,0:T(8,128)(2,1)S(1)}, bf16[8,5504]{1,0:T(8,128)(2,1)S(1)}, u32[]{:S(2)}, u32[]{:S(2)}) collective-permute-start(bf16[8,5504]{1,0:T(8,128)(2,1)S(1)} %get-tuple-element.24.refs_0_), channel_id=1, source_target_pairs={{0,16},{8,24},{16,0},{24,8},{1,17},{9,25},{17,1},{25,9},{2,18},{10... | collective-permute-start | bytes 264200 | tf_op jit(solution)/shard_map/ppermute | solution.py:346
  28.7 3.0 %collective-permute-start.1 = (bf16[8,5504]{1,0:T(8,128)(2,1)S(1)}, bf16[8,5504]{1,0:T(8,128)(2,1)S(1)}, u32[]{:S(2)}, u32[]{:S(2)}) collective-permute-start(bf16[8,5504]{1,0:T(8,128)(2,1)S(1)} %get-tuple-element.24.refs_0_), channel_id=1, source_target_pairs={{0,8},{8,0},{16,24},{24,16},{1,9},{9,1},{17,25},{25,17},{2,10},{10... | collective-permute-start | bytes 264200 | tf_op jit(solution)/shard_map/ppermute | solution.py:349
  31.7 1.3 %collective-permute-start.2 = (bf16[8,5504]{1,0:T(8,128)(2,1)S(1)}, bf16[8,5504]{1,0:T(8,128)(2,1)S(1)}, u32[]{:S(2)}, u32[]{:S(2)}) collective-permute-start(bf16[8,5504]{1,0:T(8,128)(2,1)S(1)} %collective-permute-done.refs_1_), channel_id=1, source_target_pairs={{0,8},{8,0},{16,24},{24,16},{1,9},{9,1},{17,25},{25,17},{2,10},{10... | collective-permute-start | bytes 264200 | tf_op jit(solution)/shard_map/ppermute | solution.py:349

commit v9 on v8

--- a/solution.py
+++ b/solution.py
@@ -112,9 +112,9 @@
     scale = width ** (-0.5)
     at_once = h_ref.shape[0]
     ahead = at_once == chunks
-    parts = [(k, c) for k in range(branches) for c in range(0, sensor_count, q)]
+    parts = [(k, c) for k in range(branches) for c in range(0, sensor_count, 2 * q)]
     copies = fetch(
-        sems, 0, *[(w_hbm.at[k, pl.ds(c, q)], w_ref.at[k, pl.ds(c, q)]) for k, c in parts], (w2_hbm, w2_ref)
+        sems, 0, *[(w_hbm.at[k, pl.ds(c, 2 * q)], w_ref.at[k, pl.ds(c, 2 * q)]) for k, c in parts], (w2_hbm, w2_ref)
     )
 
     pre = [bias_ref[k : k + 1, :] for k in range(branches)]
@@ -125,7 +125,7 @@
     def multiply(i):
         k, c = parts[i]
         copies[i].wait()
-        pre[k] = pre[k] + dot(sensors(i), w_ref[k, c : c + q])
+        pre[k] = pre[k] + dot(turned_ref[i, :, : 2 * q], w_ref[k, c : c + 2 * q])
 
     done = 0
     first = first_layer(w1_ref, b1_ref)
@@ -288,7 +288,7 @@
     dims, queries = coords.shape
     hidden, width = trunk_w2.shape
     nb, nq = lax.axis_size("branch"), lax.axis_size("query")
-    assert func_dev == 1 and hidden == width and sensor_count % queries == 0 and queries % (sensor_count // nq) == 0
+    assert func_dev == 1 and hidden == width and sensor_count % (2 * queries) == 0 and queries % (sensor_count // nq) == 0
     funcs = nq
     cut = sensor_count // nq
     row, rows, packed_width = plan(branches, sensor_count, dims, queries)
@@ -333,7 +333,7 @@
             pltpu.VMEM((2 * (dims + 1) * funcs, hidden), F32),
             pltpu.VMEM((funcs, queries), F32),
             pltpu.VMEM((at_once, 2 * (dims + 2) * funcs, queries), BF),
-            pltpu.SemaphoreType.DMA((row + 1,)),
+            pltpu.SemaphoreType.DMA((row // 2 + 1,)),
         ],
         compiler_params=pltpu.CompilerParams(vmem_limit_bytes=40 * MIB),
         cost_estimate=pl.CostEstimate(

time: 36.7 us -> 36.5 us (level)
  no operation moved by 1% of the time
where the time goes in v9:
time: 36.5 us; the launch traced here: 36.2 us
  Pallas kernels  15.1 us (41%)
  blocking collectives  14.5 us (40%)
  waiting for transfers between devices  4.3 us (12%)
  starting transfers between devices  1.56 us (4%)
  between operations  0.66 us (2%)
    all_to_all x1, blocking collectives, shards(): got = lax.all_to_all(packed, 'query', 0, 0, tiled=True)  14.5 us
    pallas_call x1, Pallas kernels, shards(): pl.pallas_call(functools.partial(group_kernel, row, nb * nq), out_shape=(...  10.8 us
    pallas_call x1, Pallas kernels, shards(): pl.pallas_call(functools.partial(tail_kernel, nb, early_width), out_shape...  3.37 us
    ppermute x1, waiting for transfers between devices, shift(): return lax.ppermute(x, 'branch', [(i, (i + k) % nb) for i in range(nb)])  3.01 us
    ppermute x1, starting transfers between devices, shift(): return lax.ppermute(x, 'branch', [(i, (i + k) % nb) for i in range(nb)])  1.55 us
    ppermute x2, waiting for transfers between devices, swap(): return lax.ppermute(x, 'branch', [(i, i ^ 1) for i in range(nb)])  1.28 us
    pallas_call x1, Pallas kernels, shards(): pl.pallas_call(pack_kernel, out_shape=(jax.ShapeDtypeStruct((nq, rows, pa...  0.91 us
  transfers between devices with their start and end apart: 3, of which 2 were waited for; matrix products, arithmetic and copies ran while one was open for 0% of the time, Pallas kernels for 0%

profile of v9, /device:TPU:0, one launch (start us, length us, event | category | flops | bytes accessed | tf_op | source)
XLA Modules:
  0.0 36.2 jit_solution(14328157669973661067)
XLA Ops:
  0.6 0.9 %pack.1 = (bf16[8,8,1152]{2,1,0:T(8,128)(2,1)S(1)}, f32[3,1024]{1,0:T(4,128)S(1)}, f32[1,1024]{1,0:T(1,128)S(1)}, bf16[3,1024]{1,0:T(4,128)(2,1)S(1)}, f32[1,1024]{1,0:T(1,128)S(1)}) custom-call(bf16[3,2048]{1,0:T(4,128)(2,1)} %bitcast.11, bf16[3,512]{1,0:T(4,128)(2,1)} %refs_1_.1, s32[1,512]{1,0:T(1,128)} %bitcast.14, f32[1,512]{1,0:T(1,128)} %bitcast.15, ...), custom_call_target="tpu_custom_call" | custom-call | tf_op jit(solution)/shard_map/pack/pallas_call | solution.py:299
  1.6 14.5 %all_to_all.5.got_ref = bf16[8,8,1152]{2,1,0:T(8,128)(2,1)S(1)} all-to-all(bf16[8,8,1152]{2,1,0:T(8,128)(2,1)S(1)} %get-tuple-element.19), channel_id=1, replica_groups=mesh['branch'=4,'query'=8] {'query'}, dimensions={0} | all-to-all | bytes 294912 | tf_op jit(solution)/shard_map/all_to_all | solution.py:317
  16.1 10.8 %group.1 = (bf16[8,5504]{1,0:T(8,128)(2,1)S(1)}, bf16[1024,1024]{1,0:T(8,128)(2,1)S(1)}) custom-call(bf16[8,8,1152]{2,1,0:T(8,128)(2,1)S(1)} %all_to_all.5.got_ref, bf16[8,8,1152]{2,1,0:T(8,128)(2,1)S(1)} %bitcast.10, f32[3,1024]{1,0:T(4,128)S(1)} %get-tuple-element.20.bias_ref, f32[1,1024]{1,0:T(1,128)S(1)} %get-tuple-element.21.b2_ref.refs_5_, ...), custom_call_target="tpu_custom_call" | custom-call | flops 8589934592 | bytes 12582912 | tf_op jit(solution)/shard_map/group/pallas_call | solution.py:321
  26.9 1.6 %collective-permute-start = (bf16[8,5504]{1,0:T(8,128)(2,1)S(1)}, bf16[8,5504]{1,0:T(8,128)(2,1)S(1)}, u32[]{:S(2)}, u32[]{:S(2)}) collective-permute-start(bf16[8,5504]{1,0:T(8,128)(2,1)S(1)} %get-tuple-element.24.refs_0_), channel_id=1, source_target_pairs={{0,16},{8,24},{16,0},{24,8},{1,17},{9,25},{17,1},{25,9},{2,18},{10... | collective-permute-start | bytes 264200 | tf_op jit(solution)/shard_map/ppermute | solution.py:346
  28.5 0.0 collective-permute-start.1
  28.5 3.0 %collective-permute-done.refs_1_ = bf16[8,5504]{1,0:T(8,128)(2,1)S(1)} collective-permute-done((bf16[8,5504]{1,0:T(8,128)(2,1)S(1)}, bf16[8,5504]{1,0:T(8,128)(2,1)S(1)}, u32[]{:S(2)}, u32[]{:S(2)}) %collective-permute-start) | collective-permute-done | bytes 88096 | tf_op jit(solution)/shard_map/ppermute | solution.py:346
  31.5 0.0 collective-permute-start.2
  31.5 0.0 collective-permute-done.1.refs_2_
  31.5 1.3 %collective-permute-done.2.refs_3_ = bf16[8,5504]{1,0:T(8,128)(2,1)S(1)} collective-permute-done((bf16[8,5504]{1,0:T(8,128)(2,1)S(1)}, bf16[8,5504]{1,0:T(8,128)(2,1)S(1)}, u32[]{:S(2)}, u32[]{:S(2)}) %collective-permute-start.2) | collective-permute-done | bytes 88096 | tf_op jit(solution)/shard_map/ppermute | solution.py:349
  32.8 3.4 %tail.1 = (f32[3,256,1024]{2,1,0:T(8,128)}, f32[3,1024]{1,0:T(4,128)}, f32[3,1024]{1,0:T(4,128)}, f32[1,1024]{1,0:T(1,128)}, f32[1024,1024]{1,0:T(8,128)}, /*index=5*/f32[1,1024]{1,0:T(1,128)}) custom-call(bf16[8,5504]{1,0:T(8,128)(2,1)S(1)} %get-tuple-element.24.refs_0_, bf16[8,5504]{1,0:T(8,128)(2,1)S(1)} %collective-permute-done.refs_1_, ...), custom_call_target="tpu_custom_call" | custom-call | tf_op jit(solution)/shard_map/tail/pallas_call | solution.py:364
  (1 shorter events, 0.0 us)
Async XLA Ops:
  26.9 4.6 %collective-permute-start = (bf16[8,5504]{1,0:T(8,128)(2,1)S(1)}, bf16[8,5504]{1,0:T(8,128)(2,1)S(1)}, u32[]{:S(2)}, u32[]{:S(2)}) collective-permute-start(bf16[8,5504]{1,0:T(8,128)(2,1)S(1)} %get-tuple-element.24.refs_0_), channel_id=1, source_target_pairs={{0,16},{8,24},{16,0},{24,8},{1,17},{9,25},{17,1},{25,9},{2,18},{10... | collective-permute-start | bytes 264200 | tf_op jit(solution)/shard_map/ppermute | solution.py:346
  28.5 3.0 %collective-permute-start.1 = (bf16[8,5504]{1,0:T(8,128)(2,1)S(1)}, bf16[8,5504]{1,0:T(8,128)(2,1)S(1)}, u32[]{:S(2)}, u32[]{:S(2)}) collective-permute-start(bf16[8,5504]{1,0:T(8,128)(2,1)S(1)} %get-tuple-element.24.refs_0_), channel_id=1, source_target_pairs={{0,8},{8,0},{16,24},{24,16},{1,9},{9,1},{17,25},{25,17},{2,10},{10... | collective-permute-start | bytes 264200 | tf_op jit(solution)/shard_map/ppermute | solution.py:349
  31.5 1.3 %collective-permute-start.2 = (bf16[8,5504]{1,0:T(8,128)(2,1)S(1)}, bf16[8,5504]{1,0:T(8,128)(2,1)S(1)}, u32[]{:S(2)}, u32[]{:S(2)}) collective-permute-start(bf16[8,5504]{1,0:T(8,128)(2,1)S(1)} %collective-permute-done.refs_1_), channel_id=1, source_target_pairs={{0,8},{8,0},{16,24},{24,16},{1,9},{9,1},{17,25},{25,17},{2,10},{10... | collective-permute-start | bytes 264200 | tf_op jit(solution)/shard_map/ppermute | solution.py:349

commit v10 on v9

--- a/solution.py
+++ b/solution.py
@@ -65,7 +65,7 @@
 
 
 LANES = 128
-BLOCKS = 8
+BLOCKS = 4
 
 
 def plan(branches, sensor_count, dims, q):

time: 36.5 us -> 36.5 us (level)
  no operation moved by 1% of the time
where the time goes in v10:
time: 36.5 us; the launch traced here: 36.2 us
  Pallas kernels  15.2 us (42%)
  blocking collectives  14.5 us (40%)
  waiting for transfers between devices  4.3 us (12%)
  starting transfers between devices  1.56 us (4%)
  between operations  0.66 us (2%)
    all_to_all x1, blocking collectives, shards(): got = lax.all_to_all(packed, 'query', 0, 0, tiled=True)  14.5 us
    pallas_call x1, Pallas kernels, shards(): pl.pallas_call(functools.partial(group_kernel, row, nb * nq), out_shape=(...  10.8 us
    pallas_call x1, Pallas kernels, shards(): pl.pallas_call(functools.partial(tail_kernel, nb, early_width), out_shape...  3.4 us
    ppermute x1, waiting for transfers between devices, shift(): return lax.ppermute(x, 'branch', [(i, (i + k) % nb) for i in range(nb)])  3.01 us
    ppermute x1, starting transfers between devices, shift(): return lax.ppermute(x, 'branch', [(i, (i + k) % nb) for i in range(nb)])  1.55 us
    ppermute x2, waiting for transfers between devices, swap(): return lax.ppermute(x, 'branch', [(i, i ^ 1) for i in range(nb)])  1.28 us
    pallas_call x1, Pallas kernels, shards(): pl.pallas_call(pack_kernel, out_shape=(jax.ShapeDtypeStruct((nq, rows, pa...  0.91 us
  transfers between devices with their start and end apart: 3, of which 2 were waited for; matrix products, arithmetic and copies ran while one was open for 0% of the time, Pallas kernels for 0%

profile of v10, /device:TPU:0, one launch (start us, length us, event | category | flops | bytes accessed | tf_op | source)
XLA Modules:
  0.0 36.2 jit_solution(7908487726970223780)
XLA Ops:
  0.6 0.9 %pack.1 = (bf16[8,8,1152]{2,1,0:T(8,128)(2,1)S(1)}, f32[3,1024]{1,0:T(4,128)S(1)}, f32[1,1024]{1,0:T(1,128)S(1)}, bf16[3,1024]{1,0:T(4,128)(2,1)S(1)}, f32[1,1024]{1,0:T(1,128)S(1)}) custom-call(bf16[3,2048]{1,0:T(4,128)(2,1)} %bitcast.11, bf16[3,512]{1,0:T(4,128)(2,1)} %refs_1_.1, s32[1,512]{1,0:T(1,128)} %bitcast.14, f32[1,512]{1,0:T(1,128)} %bitcast.15, ...), custom_call_target="tpu_custom_call" | custom-call | tf_op jit(solution)/shard_map/pack/pallas_call | solution.py:299
  1.6 14.5 %all_to_all.5.got_ref = bf16[8,8,1152]{2,1,0:T(8,128)(2,1)S(1)} all-to-all(bf16[8,8,1152]{2,1,0:T(8,128)(2,1)S(1)} %get-tuple-element.19), channel_id=1, replica_groups=mesh['branch'=4,'query'=8] {'query'}, dimensions={0} | all-to-all | bytes 294912 | tf_op jit(solution)/shard_map/all_to_all | solution.py:317
  16.1 10.8 %group.1 = (bf16[8,5504]{1,0:T(8,128)(2,1)S(1)}, bf16[1024,1024]{1,0:T(8,128)(2,1)S(1)}) custom-call(bf16[8,8,1152]{2,1,0:T(8,128)(2,1)S(1)} %all_to_all.5.got_ref, bf16[8,8,1152]{2,1,0:T(8,128)(2,1)S(1)} %bitcast.10, f32[3,1024]{1,0:T(4,128)S(1)} %get-tuple-element.20.bias_ref, f32[1,1024]{1,0:T(1,128)S(1)} %get-tuple-element.21.b2_ref.refs_5_, ...), custom_call_target="tpu_custom_call" | custom-call | flops 8589934592 | bytes 12582912 | tf_op jit(solution)/shard_map/group/pallas_call | solution.py:321
  26.9 1.6 %collective-permute-start = (bf16[8,5504]{1,0:T(8,128)(2,1)S(1)}, bf16[8,5504]{1,0:T(8,128)(2,1)S(1)}, u32[]{:S(2)}, u32[]{:S(2)}) collective-permute-start(bf16[8,5504]{1,0:T(8,128)(2,1)S(1)} %get-tuple-element.24.refs_0_), channel_id=1, source_target_pairs={{0,16},{8,24},{16,0},{24,8},{1,17},{9,25},{17,1},{25,9},{2,18},{10... | collective-permute-start | bytes 264200 | tf_op jit(solution)/shard_map/ppermute | solution.py:346
  28.5 0.0 collective-permute-start.1
  28.5 3.0 %collective-permute-done.refs_1_ = bf16[8,5504]{1,0:T(8,128)(2,1)S(1)} collective-permute-done((bf16[8,5504]{1,0:T(8,128)(2,1)S(1)}, bf16[8,5504]{1,0:T(8,128)(2,1)S(1)}, u32[]{:S(2)}, u32[]{:S(2)}) %collective-permute-start) | collective-permute-done | bytes 88096 | tf_op jit(solution)/shard_map/ppermute | solution.py:346
  31.5 0.0 collective-permute-start.2
  31.5 0.0 collective-permute-done.1.refs_2_
  31.5 1.3 %collective-permute-done.2.refs_3_ = bf16[8,5504]{1,0:T(8,128)(2,1)S(1)} collective-permute-done((bf16[8,5504]{1,0:T(8,128)(2,1)S(1)}, bf16[8,5504]{1,0:T(8,128)(2,1)S(1)}, u32[]{:S(2)}, u32[]{:S(2)}) %collective-permute-start.2) | collective-permute-done | bytes 88096 | tf_op jit(solution)/shard_map/ppermute | solution.py:349
  32.8 3.4 %tail.1 = (f32[3,256,1024]{2,1,0:T(8,128)}, f32[3,1024]{1,0:T(4,128)}, f32[3,1024]{1,0:T(4,128)}, f32[1,1024]{1,0:T(1,128)}, f32[1024,1024]{1,0:T(8,128)}, /*index=5*/f32[1,1024]{1,0:T(1,128)}) custom-call(bf16[8,5504]{1,0:T(8,128)(2,1)S(1)} %get-tuple-element.24.refs_0_, bf16[8,5504]{1,0:T(8,128)(2,1)S(1)} %collective-permute-done.refs_1_, ...), custom_call_target="tpu_custom_call" | custom-call | tf_op jit(solution)/shard_map/tail/pallas_call | solution.py:364
  (1 shorter events, 0.0 us)
Async XLA Ops:
  26.9 4.6 %collective-permute-start = (bf16[8,5504]{1,0:T(8,128)(2,1)S(1)}, bf16[8,5504]{1,0:T(8,128)(2,1)S(1)}, u32[]{:S(2)}, u32[]{:S(2)}) collective-permute-start(bf16[8,5504]{1,0:T(8,128)(2,1)S(1)} %get-tuple-element.24.refs_0_), channel_id=1, source_target_pairs={{0,16},{8,24},{16,0},{24,8},{1,17},{9,25},{17,1},{25,9},{2,18},{10... | collective-permute-start | bytes 264200 | tf_op jit(solution)/shard_map/ppermute | solution.py:346
  28.5 3.0 %collective-permute-start.1 = (bf16[8,5504]{1,0:T(8,128)(2,1)S(1)}, bf16[8,5504]{1,0:T(8,128)(2,1)S(1)}, u32[]{:S(2)}, u32[]{:S(2)}) collective-permute-start(bf16[8,5504]{1,0:T(8,128)(2,1)S(1)} %get-tuple-element.24.refs_0_), channel_id=1, source_target_pairs={{0,8},{8,0},{16,24},{24,16},{1,9},{9,1},{17,25},{25,17},{2,10},{10... | collective-permute-start | bytes 264200 | tf_op jit(solution)/shard_map/ppermute | solution.py:349
  31.5 1.3 %collective-permute-start.2 = (bf16[8,5504]{1,0:T(8,128)(2,1)S(1)}, bf16[8,5504]{1,0:T(8,128)(2,1)S(1)}, u32[]{:S(2)}, u32[]{:S(2)}) collective-permute-start(bf16[8,5504]{1,0:T(8,128)(2,1)S(1)} %collective-permute-done.refs_1_), channel_id=1, source_target_pairs={{0,8},{8,0},{16,24},{24,16},{1,9},{9,1},{17,25},{25,17},{2,10},{10... | collective-permute-start | bytes 264200 | tf_op jit(solution)/shard_map/ppermute | solution.py:349
